TPU v7x, 128 devices: a whole 4x4x4 slice. The times are simulated.
128 devices in a mesh: dp: 64 (over z, x, y_lo, core), mp: 2 (over y_hi).
Axes of the slice: x: 4, y: 4 (y_hi: 2, y_lo: 2; y = y_hi * 2 + y_lo), z: 4, core: 2. Of those that a mesh axis runs over, the one named last changes fastest.
Arguments:
- tokens: bfloat16 [16384, 2048], P(('dp', 'mp')), may hold values from -6 to 6
- cotangent: bfloat16 [16384, 2048], P(('dp', 'mp')), may hold values from -6 to 6
- norm_params: float32 [4, 2048], P(None, ('dp', 'mp')), may hold values from -1.5 to 2.1
- qkv_weight: bfloat16 [3, 2048, 2048], P(None, 'dp', 'mp'), may hold values from -0.125 to 0.125
- qkv_bias: bfloat16 [3, 32, 64], P(None, 'mp', 'dp'), may hold values from -3 to 3
- out_weight: bfloat16 [2048, 2048], P('mp', 'dp'), may hold values from -0.375 to 0.375
- gate_up_weight: bfloat16 [2, 2048, 5632], P(None, 'dp', 'mp'), may hold values from -0.125 to 0.125
- down_weight: bfloat16 [5632, 2048], P('mp', 'dp'), may hold values from -0.078125 to 0.078125
Outputs:
- mixed: bfloat16 [16384, 2048], P(('dp', 'mp'))
- grad_tokens: float32 [16384, 2048], P(('dp', 'mp'))
- grad_norm: float32 [4, 2048], P(None, ('dp', 'mp'))
- grad_qkv: float32 [3, 2048, 2048], P(None, 'dp', 'mp')
- grad_qkv_bias: float32 [3, 32, 64], P(None, 'mp', 'dp')
- grad_out: float32 [2048, 2048], P('mp', 'dp')
- grad_gate_up: float32 [2, 2048, 5632], P(None, 'dp', 'mp')
- grad_down: float32 [5632, 2048], P('mp', 'dp')
All inputs are finite; a program needn't handle non-finite values.
Results may differ from a plain program's by a relative error of at most 0.013.
Values may be sent and summed in bfloat16 or wider, within the bound.
A program may use at most 384 MiB of HBM per device.

v0:
```python
import jax
import jax.numpy as jnp
from jax import lax
from jax.sharding import PartitionSpec as P

HEAD_DIM = 64
ROTARY = 16


epsilon = 1e-05
score_scale = 0.125


def from_everyone(array, axis):
    devices = lax.axis_size(axis)
    return lax.all_to_all(
        jnp.broadcast_to(array[None], (devices, *array.shape)), axis, 0, 0, tiled=True
    )


def joined_along(blocks, dim):
    shape = list(blocks.shape[1:])
    shape[dim] *= blocks.shape[0]
    return jnp.moveaxis(blocks, 0, dim).reshape(shape)


def collect_2(array, axis, dim):
    blocks = from_everyone(array, axis)
    return joined_along(blocks, dim)


def in_blocks(array, dim, devices):
    shape = array.shape
    blocks = array.reshape(*shape[:dim], devices, shape[dim] // devices, *shape[dim + 1 :])
    return jnp.moveaxis(blocks, dim, 0)


def sum_at_owner(array, axis, dim):
    blocks = in_blocks(array, dim, lax.axis_size(axis))
    arrived = lax.all_to_all(blocks, axis, split_axis=0, concat_axis=0, tiled=True)
    return arrived.sum(axis=0)


def rows_first(arrays, axis, dims):
    turned = [jnp.moveaxis(a, dim, 0) for a, dim in zip(arrays, dims)]
    widths = [t[0].size for t in turned]
    both = jnp.concatenate([t.reshape(-1, w) for t, w in zip(turned, widths)], axis=1)
    result = lax.all_gather(both, axis, axis=0, tiled=True)
    blocks = jnp.split(result, [sum(widths[:k]) for k in range(1, len(widths))], axis=1)
    return tuple(
        (
            jnp.moveaxis(b.reshape(-1, *t.shape[1:]), 0, dim)
            for b, t, dim in zip(blocks, turned, dims)
        )
    )


def collect(rows):
    return collect_2(rows, "mp", 0)


def spread(total):
    return sum_at_owner(total, "mp", 0)


def sum_down(grad_down):
    return lax.psum_scatter(grad_down, "dp", scatter_dimension=1, tiled=True)


def sum_gate_up(grad_gate_up):
    gate_part = lax.psum_scatter(grad_gate_up[0], "dp", scatter_dimension=0, tiled=True)
    up_part = lax.psum_scatter(grad_gate_up[1], "dp", scatter_dimension=0, tiled=True)
    return jnp.stack([gate_part, up_part])


def normalize(values, gain, shift):
    row_mean = jnp.mean(values, -1, keepdims=True)
    centered = values - row_mean
    variance = jnp.mean(centered * centered, -1, keepdims=True)
    inverse = lax.rsqrt(variance + epsilon)
    unit_rows = centered * inverse
    return (unit_rows * gain + shift, unit_rows, inverse)


def normalize_back(incoming, unit_rows, inverse, gain):
    grad_unit = incoming * gain
    return inverse * (
        grad_unit
        - jnp.mean(grad_unit, -1, keepdims=True)
        - unit_rows * jnp.mean(grad_unit * unit_rows, -1, keepdims=True)
    )


def rotary_tables(length):
    position = jnp.arange(length).astype(jnp.float32)
    frequency = jnp.power(10000.0, -jnp.arange(ROTARY // 2).astype(jnp.float32) * (2.0 / ROTARY))
    angles = position[:, None] * frequency[None, :]
    return (jnp.cos(angles)[:, None, :], jnp.sin(angles)[:, None, :])


def rotate(values, cosine, sine_table):
    half_rot = ROTARY // 2
    lower_part = values[..., :half_rot]
    upper_part = values[..., half_rot:ROTARY]
    return jnp.concatenate(
        [
            lower_part * cosine - upper_part * sine_table,
            upper_part * cosine + lower_part * sine_table,
            values[..., ROTARY:],
        ],
        -1,
    )


def rotate_back(grads, cosine, sine_table):
    half_rot = ROTARY // 2
    lower_part = grads[..., :half_rot]
    upper_part = grads[..., half_rot:ROTARY]
    return jnp.concatenate(
        [
            lower_part * cosine + upper_part * sine_table,
            upper_part * cosine - lower_part * sine_table,
            grads[..., ROTARY:],
        ],
        -1,
    )


def shards(
    tokens, cotangent, norm_params, qkv_weight, qkv_bias, out_weight, gate_up_weight, down_weight
):
    norm_table = lax.all_gather(norm_params, ("dp", "mp"), axis=1, tiled=True)
    qkv_full, qkv_shift, out_full = (
        lax.all_gather(qkv_weight, "dp", axis=1, tiled=True),
        lax.all_gather(qkv_bias, "dp", axis=2, tiled=True),
        lax.all_gather(out_weight, "dp", axis=1, tiled=True),
    )
    inputs = tokens.astype(jnp.float32)
    norm_full, unit_one, scale_one = normalize(inputs, norm_table[0], norm_table[1])
    normed_one = collect(norm_full.astype(jnp.bfloat16))
    length = normed_one.shape[0]
    half_dim = qkv_full.shape[2]
    head_count = half_dim // HEAD_DIM
    projected = jnp.einsum("sd,tde->tse", normed_one, qkv_full, preferred_element_type=jnp.float32)
    projected = projected + qkv_shift.reshape(3, 1, half_dim).astype(jnp.float32)
    cosine, sine_table = rotary_tables(length)
    queries = rotate(projected[0].reshape(length, head_count, HEAD_DIM), cosine, sine_table).astype(
        jnp.bfloat16
    )
    key_heads = rotate(
        projected[1].reshape(length, head_count, HEAD_DIM), cosine, sine_table
    ).astype(jnp.bfloat16)
    value_heads = projected[2].reshape(length, head_count, HEAD_DIM).astype(jnp.bfloat16)
    causal = jnp.arange(length)[:, None] >= jnp.arange(length)[None, :]
    scores = (
        jnp.einsum("shd,thd->hst", queries, key_heads, preferred_element_type=jnp.float32)
        * score_scale
    )
    scores = jnp.where(causal[None], scores, -1000000000.0)
    row_top = jnp.max(scores, -1, keepdims=True)
    log_total = row_top + jnp.log(jnp.sum(jnp.exp(scores - row_top), -1, keepdims=True))
    soft_weights = jnp.exp(scores - log_total)
    soft_low = soft_weights.astype(jnp.bfloat16)
    head_mix = jnp.einsum("hst,thd->shd", soft_low, value_heads, preferred_element_type=jnp.float32)
    head_mix = head_mix.reshape(length, half_dim).astype(jnp.bfloat16)
    first_sum = inputs + spread(jnp.dot(head_mix, out_full, preferred_element_type=jnp.float32))
    norm_second, unit_two, scale_two = normalize(first_sum, norm_table[2], norm_table[3])
    normed_two = collect(norm_second.astype(jnp.bfloat16))
    gate_up_full, down_full = (
        lax.all_gather(gate_up_weight, "dp", axis=1, tiled=True),
        lax.all_gather(down_weight, "dp", axis=1, tiled=True),
    )
    gate_up = jnp.einsum(
        "sd,tdf->tsf", normed_two, gate_up_full, preferred_element_type=jnp.float32
    )
    gate_pre = gate_up[0]
    up_pre = gate_up[1]
    sigmoid_gate = jax.nn.sigmoid(gate_pre)
    activated = gate_pre * sigmoid_gate
    hidden = (activated * up_pre).astype(jnp.bfloat16)
    mixed = (
        first_sum + spread(jnp.dot(hidden, down_full, preferred_element_type=jnp.float32))
    ).astype(jnp.bfloat16)
    gate_up_full, down_full = rows_first((gate_up_weight, down_weight), "dp", (1, 1))
    qkv_full, out_full = (
        lax.all_gather(qkv_weight, "dp", axis=1, tiled=True),
        lax.all_gather(out_weight, "dp", axis=1, tiled=True),
    )
    grad_rows = collect(cotangent)
    grad_hidden = lax.dot_general(
        grad_rows, down_full, (((1,), (1,)), ((), ())), preferred_element_type=jnp.float32
    )
    grad_down = lax.dot_general(
        hidden, grad_rows, (((0,), (0,)), ((), ())), preferred_element_type=jnp.float32
    )
    grad_gate = grad_hidden * up_pre * sigmoid_gate * (1.0 + gate_pre * (1.0 - sigmoid_gate))
    grad_up = grad_hidden * activated
    grad_pair = jnp.stack([grad_gate, grad_up]).astype(jnp.bfloat16)
    grad_gate_up = jnp.einsum(
        "sd,tsf->tdf", normed_two, grad_pair, preferred_element_type=jnp.float32
    )
    grad_second = spread(
        jnp.einsum("tsf,tdf->sd", grad_pair, gate_up_full, preferred_element_type=jnp.float32)
    )
    grad_resid = cotangent.astype(jnp.float32) + normalize_back(
        grad_second, unit_two, scale_two, norm_table[2]
    )
    gain_two = jnp.sum(grad_second * unit_two, 0)
    shift_two = jnp.sum(grad_second, 0)
    resid_rows = collect(grad_resid.astype(jnp.bfloat16))
    grad_mix = lax.dot_general(
        resid_rows, out_full, (((1,), (1,)), ((), ())), preferred_element_type=jnp.float32
    )
    grad_mix = grad_mix.astype(jnp.bfloat16).reshape(length, head_count, HEAD_DIM)
    grad_outproj = lax.dot_general(
        head_mix, resid_rows, (((0,), (0,)), ((), ())), preferred_element_type=jnp.float32
    )
    grad_soft = jnp.einsum(
        "shd,thd->hst", grad_mix, value_heads, preferred_element_type=jnp.float32
    )
    row_dot = jnp.sum(grad_soft * soft_weights, -1, keepdims=True)
    grad_score = (soft_weights * (grad_soft - row_dot)).astype(jnp.bfloat16)
    grad_query = (
        jnp.einsum("hst,thd->shd", grad_score, key_heads, preferred_element_type=jnp.float32)
        * score_scale
    )
    grad_key = (
        jnp.einsum("hst,shd->thd", grad_score, queries, preferred_element_type=jnp.float32)
        * score_scale
    )
    grad_value = jnp.einsum("hst,shd->thd", soft_low, grad_mix, preferred_element_type=jnp.float32)
    grad_proj = jnp.stack(
        [
            rotate_back(grad_query, cosine, sine_table).reshape(length, half_dim),
            rotate_back(grad_key, cosine, sine_table).reshape(length, half_dim),
            grad_value.reshape(length, half_dim),
        ]
    ).astype(jnp.bfloat16)
    grad_shift = jnp.sum(grad_proj.astype(jnp.float32), axis=1).reshape(3, head_count, HEAD_DIM)
    grad_qkvproj = jnp.einsum(
        "sd,tse->tde", normed_one, grad_proj, preferred_element_type=jnp.float32
    )
    grad_first = spread(
        jnp.einsum("tse,tde->sd", grad_proj, qkv_full, preferred_element_type=jnp.float32)
    )
    grad_input = grad_resid + normalize_back(grad_first, unit_one, scale_one, norm_table[0])
    gain_one = jnp.sum(grad_first * unit_one, 0)
    shift_one = jnp.sum(grad_first, 0)
    norm_terms = jnp.stack([gain_one, shift_one, gain_two, shift_two])
    grad_norm = lax.psum_scatter(norm_terms, ("dp", "mp"), scatter_dimension=1, tiled=True)
    grad_qkv, grad_qkv_bias, grad_out = (
        lax.psum_scatter(grad_qkvproj, "dp", scatter_dimension=1, tiled=True),
        lax.psum_scatter(grad_shift, "dp", scatter_dimension=2, tiled=True),
        lax.psum_scatter(grad_outproj, "dp", scatter_dimension=1, tiled=True),
    )
    grad_dn = sum_down(grad_down)
    grad_gu = sum_gate_up(grad_gate_up)
    return (mixed, grad_input, grad_norm, grad_qkv, grad_qkv_bias, grad_out, grad_gu, grad_dn)


def solution(mesh):
    placed = (
        P(("dp", "mp"), None),
        P(("dp", "mp"), None),
        P(None, ("dp", "mp")),
        P(None, "dp", "mp"),
        P(None, "mp", "dp"),
        P("mp", "dp"),
        P(None, "dp", "mp"),
        P("mp", "dp"),
    )
    return jax.shard_map(
        shards,
        mesh=mesh,
        in_specs=placed,
        out_specs=(
            P(("dp", "mp"), None),
            P(("dp", "mp"), None),
            P(None, ("dp", "mp")),
            P(None, "dp", "mp"),
            P(None, "mp", "dp"),
            P("mp", "dp"),
            P(None, "dp", "mp"),
            P("mp", "dp"),
        ),
        check_vma=False,
    )
```

profile of v0, /device:TPU:0, one launch (start us, length us, event | category | flops | bytes accessed | tf_op | source)
XLA Modules:
  0.0 3577.8 jit_solution(14270908643177495790)
XLA Ops:
  11.0 1.8 pad_maximum_fusion.5
  12.8 319.5 %all-gather = f32[128,16,4]{1,2,0:T(4,128)S(1)} all-gather(f32[1,16,4]{1,2,0:T(4,128)S(1)} %bitcast.191), channel_id=1, replica_groups=mesh['dp'=64,'mp'=2] {'dp','mp'}, dimensions={0}, use_global_device_ids=true | all-gather | bytes 33024 | tf_op jit(solution)/shard_map/all_gather | solution.py:132
  334.6 1.1 broadcast_in_dim.16
  335.7 3.6 all-to-all-start
  339.3 82.2 %all_gather.25 = bf16[3,16,64]{1,0,2:T(4,128)(2,1)S(1)} all-gather(bf16[3,16,1]{1,0,2:T(4,128)(2,1)S(1)} %copy-done.49), channel_id=1, replica_groups=mesh['dp'=64,'mp'=2] {'dp'}, dimensions={2}, use_global_device_ids=true | all-gather | bytes 6240 | tf_op jit(solution)/shard_map/all_gather | solution.py:135
  422.5 6.9 add_bitcast_fusion
  430.5 1.3 copy.91
  431.9 1.2 copy.90
  433.1 1.2 slice.160
  434.7 1.2 subtract_convert_fusion.3
  436.0 1.8 fusion.11
  440.0 3.5 fusion.6
  443.5 32.0 all_to_all.40
  475.5 1.8 reduce_sum.174
  478.5 17.2 all_to_all.41
  495.7 1.2 broadcast_in_dim.24
  496.9 4.6 all-to-all-start.4
  501.6 10.9 convolution_bitcast_fusion.2
  512.5 2.5 copy-done
  515.1 2.8 fusion.65
  517.9 10.5 fusion.4
  528.3 179.9 %all-gather.15.cloned.1.call-done = bf16[2048,8448]{1,0:T(8,128)(2,1)} async-done(((bf16[32,8448]{1,0:T(8,128)(2,1)}), bf16[2048,8448]{1,0:T(8,128)(2,1)}) %all-gather.15.cloned.1.call-update) | async-done | bytes 34603024 | tf_op jit(solution)/shard_map/all_gather | solution.py:48
  708.2 20.0 split.9
  728.2 27.8 copy.97
  756.0 28.7 copy.98
  784.6 4.9 all-to-all-start.3
  789.5 9.4 fusion.26
  799.0 12.5 fusion
  811.5 5.2 all-to-all-done.3
  816.7 4.8 all-to-all-start.5
  821.9 1.8 reduce_sum.177
  823.8 24.0 all-to-all-done.5
  847.8 2.7 fusion.62
  851.4 1.7 fusion.63
  853.2 16.5 all_to_all.42
  870.8 1.3 convolution_convert_fusion.2
  872.3 4.2 convolution_convert_fusion
  876.4 1.4 multiply_reduce_fusion
  877.8 1.2 multiply_convert_fusion
  881.9 6.7 fusion.58
  888.6 26.9 all_to_all.43
  916.3 1.3 copy.121
  917.9 11.4 convolution_bitcast_fusion.1
  929.3 36.0 %copy.107 = f32[3,2048,1024]{2,0,1:T(4,128)} copy(f32[3,2048,1024]{1,2,0:T(8,128)} %convolution_bitcast_fusion.1) | data formatting | bytes 50331648 | tf_op jit(solution)/shard_map/sd,tse->tde/transpose | solution.py:240
  965.4 1.1 copy-done.5
  966.5 19.6 convolution_bitcast_fusion
  986.2 29.3 slice_bitcast_fusion.1
  1015.5 23.4 copy.123
  1038.9 23.3 copy.125
  1062.3 1.1 copy-done.11
  1063.5 5.7 fusion.70
  1069.2 13.9 fusion.22
  1085.6 280.1 %all-reduce.1 = f32[3,16,64]{1,0,2:T(4,128)S(1)} all-reduce(f32[3,16,64]{1,0,2:T(4,128)S(1)} %copy.108), channel_id=4, replica_groups=mesh['dp'=64,'mp'=2] {'dp'}, use_global_device_ids=true, to_apply=%region_22.23.clone | all-reduce | flops 3072 | bytes 24576
  1366.9 2.6 fusion.40
  1369.5 192.3 %reduce-scatter.16.cloned.1.call-done = f32[16,4]{1,0:T(8,128)} async-done(((f32[2048,4]{1,0:T(8,128)}), f32[16,4]{1,0:T(8,128)}) %reduce-scatter.16.cloned.1.call-update) | async-done | bytes 272
  1561.8 1.3 copy.122
  1563.2 730.8 %all-reduce.4.cloned.1.call-done = f32[3,2048,1024]{2,0,1:T(4,128)} async-done(((f32[3,2048,1024]{2,0,1:T(4,128)}), f32[3,2048,1024]{2,0,1:T(4,128)}) %all-reduce.4.cloned.1.call-update) | async-done | bytes 25165840
  2294.0 1.1 constant_dynamic-slice_fusion.1
  2296.1 327.5 %reduce-scatter.18.cloned.1.call-done = f32[32,2816]{1,0:T(8,128)} async-done(((f32[2048,2816]{1,0:T(8,128)}), f32[32,2816]{1,0:T(8,128)}) %reduce-scatter.18.cloned.1.call-update) | async-done | bytes 360464
  2623.6 1.4 copy.124
  2625.4 322.5 %reduce-scatter.20.cloned.1.call-done = f32[32,2816]{1,0:T(8,128)} async-done(((f32[2048,2816]{1,0:T(8,128)}), f32[32,2816]{1,0:T(8,128)}) %reduce-scatter.20.cloned.1.call-update) | async-done | bytes 360464
  2947.9 1.4 copy.126
  2950.7 295.5 %reduce-scatter.12.cloned.1.call-done = f32[1024,32]{0,1:T(8,128)} async-done(((f32[1024,2048]{0,1:T(8,128)}), f32[1024,32]{0,1:T(8,128)}) %reduce-scatter.12.cloned.1.call-update) | async-done | bytes 131088 | tf_op jit(solution)/shard_map/reduce_scatter | solution.py:254
  3246.2 324.9 %reduce-scatter.14.cloned.1.call-done = f32[2816,32]{0,1:T(8,128)} async-done(((f32[2816,2048]{0,1:T(8,128)}), f32[2816,32]{0,1:T(8,128)}) %reduce-scatter.14.cloned.1.call-update) | async-done | bytes 360464 | tf_op jit(solution)/shard_map/reduce_scatter | solution.py:67
  (187 shorter events, 24.1 us)
Async XLA Ops:
  7.2 5.7 copy-start.48
  7.2 325.3 %copy-start.3 = (bf16[128,2048]{1,0:T(8,128)(2,1)S(1)}, bf16[128,2048]{1,0:T(8,128)(2,1)}, u32[]{:S(2)}) copy-start(bf16[128,2048]{1,0:T(8,128)(2,1)} %param.8) | copy-start | bytes 1572868
  7.2 415.3 %all-gather.7.cloned.1.call-start = ((), (), s32[]{:S(2)}) async-start(), calls=%async_computation.13 | async-start | bytes 12779520 | tf_op jit(solution)/shard_map/all_gather | solution.py:134
  7.9 432.0 %all-gather.9.cloned.1.call-start = ((), (), s32[]{:S(2)}) async-start(), calls=%async_computation.14 | async-start | bytes 4259840 | tf_op jit(solution)/shard_map/all_gather | solution.py:136
  8.7 492.9 %all-gather.11.cloned.1.call-start = ((), (), s32[]{:S(2)}) async-start(), calls=%async_computation.15 | async-start | bytes 23429120 | tf_op jit(solution)/shard_map/all_gather | solution.py:170
  9.4 508.4 %all-gather.13.cloned.1.call-start = ((), (), s32[]{:S(2)}) async-start(), calls=%async_computation.16 | async-start | bytes 11714560 | tf_op jit(solution)/shard_map/all_gather | solution.py:171
  10.0 698.2 %all-gather.15.cloned.1.call-start = ((), (), s32[]{:S(2)}) async-start(), calls=%async_computation.17 | async-start | bytes 35143680 | tf_op jit(solution)/shard_map/all_gather | solution.py:48
  332.3 7.0 copy-start.49
  332.7 3.0 copy-start.40
  333.0 2.7 copy-start.44
  335.7 86.8 %all-to-all-start = ((bf16[2,128,2048]{2,1,0:T(8,128)(2,1)}), bf16[2,128,2048]{2,1,0:T(8,128)(2,1)S(1)}, u32[]{:S(2)}, u32[]{:S(2)}) async-start(bf16[2,128,2048]{2,1,0:T(8,128)(2,1)} %broadcast_in_dim.16), calls=%async_computation | async-start | bytes 2097152 | tf_op jit(solution)/shard_map/all_to_all | solution.py:16
  422.5 12.2 copy-start.33
  422.5 12.2 copy-start.35
  422.5 6.9 copy-start.12
  434.7 3.0 copy-start.16
  435.9 1.8 copy-start.21
  435.9 1.8 copy-start.23
  435.9 1.8 copy-start.25
  435.9 1.8 copy-start.27
  435.9 1.9 copy-start.18
  437.8 2.0 copy-start.1
  439.8 3.7 copy-start.13
  477.4 0.7 copy-start.31
  477.4 0.7 copy-start.39
  477.6 0.7 copy-start.42
  477.6 18.1 copy-start.14
  495.7 16.8 copy-start.4
  496.9 287.7 %all-to-all-start.4 = ((bf16[2,128,2048]{2,1,0:T(8,128)(2,1)}), bf16[2,128,2048]{2,1,0:T(8,128)(2,1)}, u32[]{:S(2)}, u32[]{:S(2)}) async-start(bf16[2,128,2048]{2,1,0:T(8,128)(2,1)} %broadcast_in_dim.24), calls=%async_computation.4 | async-start | bytes 2097152 | tf_op jit(solution)/shard_map/all_to_all | solution.py:16
  512.5 2.5 copy-start
  784.6 32.0 all-to-all-start.3
  816.7 31.1 all-to-all-start.5
  821.5 740.3 %reduce-scatter.16.cloned.1.call-start = ((), (), s32[]{:S(2)}) async-start(), calls=%async_computation.20 | async-start | bytes 1056768
  847.8 2.7 copy-start.32
  847.8 2.7 copy-start.43
  847.8 2.7 copy-start.47
  847.8 3.6 copy-start.15
  851.4 19.4 copy-start.50
  869.7 1.0 copy-start.10
  870.8 1.5 copy-start.19
  872.2 4.2 copy-start.2
  877.8 1.2 copy-start.26
  877.8 1.2 copy-start.28
  879.1 1.0 copy-start.17
  879.1 1.0 copy-start.22
  879.1 1.0 copy-start.24
  879.1 1.5 copy-start.34
  879.1 1.5 copy-start.36
  880.1 1.0 copy-start.20
  881.6 36.3 %copy-start.6 = (bf16[1,256,1024]{2,1,0:T(8,128)(2,1)}, bf16[1,256,1024]{2,1,0:T(8,128)(2,1)S(1)}, u32[]{:S(2)}) copy-start(bf16[1,256,1024]{2,1,0:T(8,128)(2,1)S(1)} %copy.103) | copy-start | bytes 1572868
  881.9 36.0 %copy-start.8 = (bf16[1,256,1024]{2,1,0:T(8,128)(2,1)}, bf16[1,256,1024]{2,1,0:T(8,128)(2,1)S(1)}, u32[]{:S(2)}) copy-start(bf16[1,256,1024]{2,1,0:T(8,128)(2,1)S(1)} %copy.104) | copy-start | bytes 1572868
  888.5 27.2 copy-start.30
  888.6 27.2 copy-start.41
  888.6 27.2 copy-start.45
  915.5 0.7 copy-start.37
  915.5 0.7 copy-start.38
  917.6 1376.3 %all-reduce.4.cloned.1.call-start = ((), (), s32[]{:S(2)}) async-start(), calls=%async_computation.23 | async-start | bytes 67108864
  965.3 1.2 copy-start.5
  965.3 1658.2 %reduce-scatter.18.cloned.1.call-start = ((), (), s32[]{:S(2)}) async-start(), calls=%async_computation.21 | async-start | bytes 23429120
  1038.8 1909.1 %reduce-scatter.20.cloned.1.call-start = ((), (), s32[]{:S(2)}) async-start(), calls=%async_computation.22 | async-start | bytes 23429120
  1062.2 1.2 copy-start.11
  1062.3 2183.9 %reduce-scatter.12.cloned.1.call-start = ((), (), s32[]{:S(2)}) async-start(), calls=%async_computation.18 | async-start | bytes 8519680 | tf_op jit(solution)/shard_map/reduce_scatter | solution.py:254
  1069.2 2501.9 %reduce-scatter.14.cloned.1.call-start = ((), (), s32[]{:S(2)}) async-start(), calls=%async_computation.19 | async-start | bytes 23429120 | tf_op jit(solution)/shard_map/reduce_scatter | solution.py:67
  1083.2 1.9 copy-start.7
  1083.2 1.9 copy-start.9
  (3 other events, 1.8 us)
Sparse Core Ops, SparseCore 0:
  9.8 120.9 all-gather.6
  132.4 104.5 all-gather.8
  238.7 148.8 all-gather.10
  389.2 125.8 all-gather.12
  517.2 190.9 all-gather.14
  917.8 643.9 reduce-scatter.15
  1564.5 729.4 all-reduce.3
  2296.5 326.9 reduce-scatter.17
  2626.1 321.7 reduce-scatter.19
  2950.8 295.2 reduce-scatter.11
  3249.3 321.7 reduce-scatter.13
where the time goes:
time: 3590 us; the launch traced here: 3580 us
  waiting for transfers between devices  2410 us (67%)
  blocking collectives  774 us (22%)
  local copies, waits for them, and re-layouts  221 us (6%)
  matrix products  122 us (3%)
    unnamed x15, waiting for transfers between devices  1580 us
    reduce_scatter x1, waiting for transfers between devices, sum_down(): return lax.psum_scatter(grad_down, 'dp', scatter_dimension=1, tiled=True)  325 us
    all_gather x1, blocking collectives, shards(): norm_table = lax.all_gather(norm_params, ('dp', 'mp'), axis=1, tiled=True)  319 us
    reduce_scatter x1, waiting for transfers between devices, shards(): lax.psum_scatter(grad_outproj, 'dp', scatter_dimension=1, tiled=True)  295 us
    unnamed x1, blocking collectives  280 us
    all_gather x1, waiting for transfers between devices, rows_first(): result = lax.all_gather(both, axis, axis=0, tiled=True)  180 us
    all_gather x1, blocking collectives, shards(): lax.all_gather(qkv_bias, 'dp', axis=2, tiled=True)  82.2 us
  transfers between devices with their start and end apart: 15, of which 9 were waited for; matrix products, arithmetic and copies ran while one was open for 9% of the time, Pallas kernels for 0%

commit v1 on v0

v1 whole, which is shorter than its diff:
```python
import jax
import jax.numpy as jnp
from jax import lax
from jax.sharding import Mesh
from jax.sharding import PartitionSpec as P

HEAD_DIM = 64
ROTARY = 16
EPSILON = 1e-05
SCALE = 0.125

GRID = ("z", "x", "yl", "c", "yh")
ROWS = ("z", "x", "yl", "c")
SPREAD = ("z", "x", "c")
RING = ("yl", "yh")
PAIR = ("yl", "c")
EXTRA = 128

SAME = [(0, 0), (1, 2), (2, 1), (3, 3)]
CROSS = [(0, 2), (1, 0), (2, 3), (3, 1)]

bf16 = jnp.bfloat16
f32 = jnp.float32


def turn(k):
    place = [0, 2, 1, 3]
    return [(place[y], place[(y + k) % 4]) for y in range(4)]


def mm(a, b, ca, cb):
    return lax.dot_general(a, b, (((ca,), (cb,)), ((), ())), preferred_element_type=f32)


def to_quarters(quarters):
    yl, c = lax.axis_index("yl"), lax.axis_index("c")
    one = lax.ppermute(lax.dynamic_index_in_dim(quarters, c, 0, False), PAIR, SAME)
    two = lax.ppermute(lax.dynamic_index_in_dim(quarters, 1 - c, 0, False), PAIR, CROSS)
    low = jnp.where(yl == 0, one, two)
    high = jnp.where(yl == 0, two, one)
    return jnp.concatenate([low, high], axis=0)


def from_quarters(rows):
    yl, c = lax.axis_index("yl"), lax.axis_index("c")
    halves = rows.reshape(2, 32, rows.shape[1])
    one = lax.ppermute(
        lax.dynamic_index_in_dim(halves, yl, 0, False), PAIR, [(b, a) for a, b in SAME]
    )
    two = lax.ppermute(
        lax.dynamic_index_in_dim(halves, 1 - yl, 0, False), PAIR, [(b, a) for a, b in CROSS]
    )
    return jnp.stack([jnp.where(c == 0, one, two), jnp.where(c == 0, two, one)])


def gather_ring(block):
    got = [block]
    for k in (2, 1, 3):
        got.append(lax.ppermute(block, RING, turn(-k)))
    return jnp.concatenate(got, axis=0)


def sum_ring(parts):
    blocks = parts.reshape(4, -1, parts.shape[1])
    total = blocks[0]
    low = blocks.astype(bf16)
    for place, k in ((1, 2), (2, 1), (3, 3)):
        total = total + lax.ppermute(
            low[place], RING, turn(k)
        ).astype(f32)
    return total


def unit_of(values):
    centered = values - jnp.mean(values, -1, keepdims=True)
    variance = jnp.mean(centered * centered, -1, keepdims=True)
    inverse = lax.rsqrt(variance + EPSILON)
    return centered * inverse, inverse


def normalize_back(incoming, unit_rows, inverse, gain):
    grad_unit = incoming * gain
    return inverse * (
        grad_unit
        - jnp.mean(grad_unit, -1, keepdims=True)
        - unit_rows * jnp.mean(grad_unit * unit_rows, -1, keepdims=True)
    )


def rotate(values, cosine, sine):
    half = ROTARY // 2
    low, high = values[..., :half], values[..., half:ROTARY]
    return jnp.concatenate(
        [low * cosine - high * sine, high * cosine + low * sine, values[..., ROTARY:]], -1
    )


def shards(
    tokens, cotangent, norm_params, qkv_weight, qkv_bias, out_weight, gate_up_weight, down_weight
):
    yl, yh = lax.axis_index("yl"), lax.axis_index("yh")
    y = yh * 2 + yl
    rows = qkv_weight.shape[1]
    hq = qkv_weight.shape[2] // 2
    fq = gate_up_weight.shape[2] // 2
    heads = hq // HEAD_DIM
    here = tokens.shape[0]
    length = 2 * here

    qkv_q = qkv_weight.reshape(3, rows, 2, hq).transpose(2, 1, 0, 3).reshape(2, rows, 3 * hq)
    out_q = out_weight.T.reshape(rows, 2, hq).transpose(1, 0, 2)
    gu_q = gate_up_weight.reshape(2, rows, 2, fq).transpose(2, 1, 0, 3).reshape(2, rows, 2 * fq)
    down_q = down_weight.T.reshape(rows, 2, fq).transpose(1, 0, 2)
    other = lax.ppermute(norm_params, "yh", [(0, 1), (1, 0)])
    norm_rows = jnp.where(
        yh == 0,
        jnp.concatenate([norm_params, other], 1),
        jnp.concatenate([other, norm_params], 1),
    ).T
    norm_high = norm_rows.astype(bf16)
    norm_low = (norm_rows - norm_high.astype(f32)).astype(bf16)
    bias_q = qkv_bias.reshape(3, 2, heads).transpose(1, 0, 2).reshape(2, 1, 3 * heads)
    bias_q = jnp.pad(bias_q, ((0, 0), (0, rows - 1), (8, EXTRA - 8 - 3 * heads)))
    extra = jnp.pad(jnp.concatenate([norm_high, norm_low], 1), ((0, 0), (0, EXTRA - 8)))
    extra_q = bias_q + extra[None]

    first = to_quarters(jnp.concatenate([qkv_q, out_q, extra_q], axis=2))
    second = to_quarters(jnp.concatenate([gu_q, down_q], axis=2))
    first = lax.all_gather(first, SPREAD, axis=0, tiled=True)
    second = lax.all_gather(second, SPREAD, axis=0, tiled=True)
    w_qkv, w_out = first[:, : 3 * hq], first[:, 3 * hq : 4 * hq]
    extras = first[:, 4 * hq :]
    w_gu, w_down = second[:, : 2 * fq], second[:, 2 * fq :]
    width = extras.shape[0]
    norm_table = (extras[:, :4].astype(f32) + extras[:, 4:8].astype(f32)).T
    bias = extras.reshape(HEAD_DIM, rows, EXTRA)[:, 0, 8 : 8 + 3 * heads].T.reshape(3 * hq)

    token_rows = gather_ring(tokens).astype(f32)
    cot_rows = gather_ring(cotangent)
    unit_rows, inverse_rows = unit_of(token_rows)
    unit_one, scale_one = unit_rows[:here], inverse_rows[:here]
    normed_one = (unit_rows * norm_table[0] + norm_table[1]).astype(bf16)
    projected = mm(normed_one, w_qkv, 1, 0) + bias.astype(f32)
    place = jnp.stack([((y + k) % 4) // 2 for k in (0, 2, 1, 3)])
    position = (place[:, None] * here + jnp.arange(here)[None, :]).reshape(2, length)
    frequency = jnp.power(10000.0, -jnp.arange(ROTARY // 2).astype(f32) * (2.0 / ROTARY))
    angles = position.astype(f32)[:, :, None] * frequency
    cosine, sine = jnp.cos(angles)[:, :, None, :], jnp.sin(angles)[:, :, None, :]
    split = projected.reshape(2, length, 3, heads, HEAD_DIM)
    queries = rotate(split[:, :, 0], cosine, sine).astype(bf16)
    key_heads = rotate(split[:, :, 1], cosine, sine).astype(bf16)
    value_heads = split[:, :, 2].astype(bf16)
    causal = position[:, :, None] >= position[:, None, :]
    scores = (
        jnp.einsum("bshd,bthd->bhst", queries, key_heads, preferred_element_type=f32) * SCALE
    )
    scores = jnp.where(causal[:, None], scores, -1000000000.0)
    powers = jnp.exp(scores - jnp.max(scores, -1, keepdims=True))
    soft = powers / jnp.sum(powers, -1, keepdims=True)
    soft_low = soft.astype(bf16)
    head_mix = jnp.einsum("bhst,bthd->bshd", soft_low, value_heads, preferred_element_type=f32)
    head_mix = head_mix.reshape(2 * length, hq).astype(bf16)
    first_sum = tokens.astype(f32) + sum_ring(mm(head_mix, w_out, 1, 1))

    unit_two, scale_two = unit_of(first_sum)
    normed_two = gather_ring((unit_two * norm_table[2] + norm_table[3]).astype(bf16))
    gate_up = mm(normed_two, w_gu, 1, 0)
    gate_pre, up_pre = gate_up[:, :fq], gate_up[:, fq:]
    sigmoid = jax.nn.sigmoid(gate_pre)
    activated = gate_pre * sigmoid
    hidden = (activated * up_pre).astype(bf16)
    grad_down = mm(cot_rows, hidden, 0, 0).astype(bf16)
    down_sums = lax.psum_scatter(grad_down, SPREAD, scatter_dimension=0, tiled=True)
    mixed = (first_sum + sum_ring(mm(hidden, w_down, 1, 1))).astype(bf16)
    grad_hidden = mm(cot_rows, w_down, 1, 0)
    grad_gate = grad_hidden * up_pre * sigmoid * (1.0 + gate_pre * (1.0 - sigmoid))
    grad_pair = jnp.concatenate([grad_gate, grad_hidden * activated], 1).astype(bf16)
    grad_gu = mm(normed_two, grad_pair, 0, 0).astype(bf16)
    gu_sums = lax.psum_scatter(grad_gu, SPREAD, scatter_dimension=0, tiled=True)
    grad_second = sum_ring(mm(grad_pair, w_gu, 1, 1))
    grad_resid = cotangent.astype(f32) + normalize_back(
        grad_second, unit_two, scale_two, norm_table[2]
    )
    gain_two = jnp.sum(grad_second * unit_two, 0)
    shift_two = jnp.sum(grad_second, 0)

    resid_rows = gather_ring(grad_resid.astype(bf16))
    grad_mix = mm(resid_rows, w_out, 1, 0).astype(bf16).reshape(2, length, heads, HEAD_DIM)
    grad_out = mm(resid_rows, head_mix, 0, 0).astype(bf16)
    grad_soft = jnp.einsum("bshd,bthd->bhst", grad_mix, value_heads, preferred_element_type=f32)
    row_dot = jnp.sum(grad_soft * soft, -1, keepdims=True)
    grad_score = (soft * (grad_soft - row_dot)).astype(bf16)
    grad_query = (
        jnp.einsum("bhst,bthd->bshd", grad_score, key_heads, preferred_element_type=f32) * SCALE
    )
    grad_key = (
        jnp.einsum("bhst,bshd->bthd", grad_score, queries, preferred_element_type=f32) * SCALE
    )
    grad_value = jnp.einsum("bhst,bshd->bthd", soft_low, grad_mix, preferred_element_type=f32)
    grad_proj = jnp.concatenate(
        [
            rotate(grad_query, cosine, -sine).reshape(2 * length, hq),
            rotate(grad_key, cosine, -sine).reshape(2 * length, hq),
            grad_value.reshape(2 * length, hq),
        ],
        1,
    ).astype(bf16)
    grad_qkv = mm(normed_one, grad_proj, 0, 0).astype(bf16)
    first_parts = mm(grad_proj, w_qkv, 1, 1)
    gain_one = jnp.sum(first_parts * unit_rows, 0)
    shift_one = jnp.sum(first_parts, 0)
    grad_bias = jnp.sum(grad_proj.astype(f32), 0).reshape(3 * heads, HEAD_DIM).T
    norm_terms = jnp.stack([gain_one, shift_one, gain_two, shift_two], 1)
    grad_extra = jnp.pad(norm_terms, ((0, 0), (0, EXTRA - 4))) + jnp.pad(
        grad_bias[:, None, :], ((0, 0), (0, rows - 1), (8, EXTRA - 8 - 3 * heads))
    ).reshape(width, EXTRA)
    grad_first = jnp.concatenate([grad_qkv, grad_out, grad_extra.astype(bf16)], 1)
    first_sums = lax.psum_scatter(grad_first, SPREAD, scatter_dimension=0, tiled=True)
    grad_input = grad_resid + normalize_back(
        sum_ring(first_parts), unit_one, scale_one, norm_table[0]
    )

    down_back = from_quarters(down_sums)
    gu_back = from_quarters(gu_sums)
    first_back = from_quarters(first_sums)
    out_down = down_back.transpose(0, 2, 1).reshape(2 * fq, rows).astype(f32)
    out_gu = (
        gu_back.reshape(2, rows, 2, fq).transpose(2, 1, 0, 3).reshape(2, rows, 2 * fq).astype(f32)
    )
    out_qkv = (
        first_back[:, :, : 3 * hq]
        .reshape(2, rows, 3, hq)
        .transpose(2, 1, 0, 3)
        .reshape(3, rows, 2 * hq)
        .astype(f32)
    )
    out_out = (
        first_back[:, :, 3 * hq : 4 * hq].transpose(0, 2, 1).reshape(2 * hq, rows).astype(f32)
    )
    extra_back = first_back[:, :, 4 * hq :].astype(f32)
    out_bias = (
        extra_back[:, 0, 8 : 8 + 3 * heads]
        .reshape(2, 3, heads)
        .transpose(1, 0, 2)
        .reshape(3, 2 * heads, 1)
    )
    norm_back = (extra_back[0, :, :4] + extra_back[1, :, :4]).T.reshape(4, 2, rows // 2)
    mine = lax.dynamic_index_in_dim(norm_back, yh, 1, False)
    theirs = lax.dynamic_index_in_dim(norm_back, 1 - yh, 1, False)
    out_norm = mine + lax.ppermute(theirs, "yh", [(0, 1), (1, 0)])
    return (mixed, grad_input, out_norm, out_qkv, out_bias, out_out, out_gu, out_down)


def solution(mesh):
    grid = Mesh(mesh.devices.reshape(4, 4, 2, 2, 2), GRID)
    placed = (
        P(GRID, None),
        P(GRID, None),
        P(None, GRID),
        P(None, ROWS, "yh"),
        P(None, "yh", ROWS),
        P("yh", ROWS),
        P(None, ROWS, "yh"),
        P("yh", ROWS),
    )
    return jax.shard_map(
        shards,
        mesh=grid,
        in_specs=placed,
        out_specs=(
            P(GRID, None),
            P(GRID, None),
            P(None, GRID),
            P(None, ROWS, "yh"),
            P(None, "yh", ROWS),
            P("yh", ROWS),
            P(None, ROWS, "yh"),
            P("yh", ROWS),
        ),
        check_vma=False,
    )
```

time: 3590 us -> 618 us (0.17)
  waiting for transfers between devices: 2410 us -> 341 us
  blocking collectives: 774 us -> 0 us
  local copies, waits for them, and re-layouts: 221 us -> 65 us
  starting transfers between devices: 18.9 us -> 54.8 us
    unnamed x15 -> x5, waiting for transfers between devices: 1580 us -> 0.08 us
    reduce_scatter x2 -> x3, waiting for transfers between devices: 620 us -> 163 us  [the longest x1 94.8 us: shards(): gu_sums = lax.psum_scatter(grad_gu, SPREAD, scatter_dimension=0, tiled=True)]
    all_gather x2 -> x0, blocking collectives: 402 us -> none  [the longest x1 319 us: shards(): norm_table = lax.all_gather(norm_params, ('dp', 'mp'), axis=1, tiled=True)]
    unnamed x1 -> x0, blocking collectives: 280 us -> none
    all_gather x5 -> x2, waiting for transfers between devices: 180 us -> 14.8 us  [the longest x1 14.8 us: shards(): first = lax.all_gather(first, SPREAD, axis=0, tiled=True)]
    ppermute x0 -> x36, waiting for transfers between devices: none -> 163 us  [the longest x12 85.7 us: sum_ring(): total = total + lax.ppermute(low[place], RING, turn(k)).astype(f32)]
    all_to_all x4 -> x0, blocking collectives: 92.6 us -> none  [the longest x2 58.9 us: sum_at_owner(): lax.all_to_all(blocks, axis, split_axis=0, concat_axis=0, tiled=True)]
    ppermute x0 -> x36, starting transfers between devices: none -> 54.4 us  [the longest x12 17.6 us: gather_ring(): got.append(lax.ppermute(block, RING, turn(-k)))]
  transfers between devices with their start and end apart: 15 -> 41, of which waited for: 9 -> 22; matrix products, arithmetic and copies ran while one was open for 9% -> 24% of each run, Pallas kernels for 0% -> 0%
where the time goes in v1:
time: 618 us; the launch traced here: 607 us
  waiting for transfers between devices  341 us (55%)
  matrix products  104 us (17%)
  local copies, waits for them, and re-layouts  65 us (11%)
  starting transfers between devices  54.8 us (9%)
  other arithmetic  26.4 us (4%)
  between operations  15.2 us (2%)
    reduce_scatter x1, waiting for transfers between devices, shards(): gu_sums = lax.psum_scatter(grad_gu, SPREAD, scatter_dimension=0, tiled=True)  94.8 us
    dot_general x12, matrix products, mm(): lax.dot_general(a, b, (((ca,), (cb,)), ((), ())), preferred_element_type=...  91.1 us
    ppermute x12, waiting for transfers between devices, sum_ring(): total = total + lax.ppermute(low[place], RING, turn(k)).astype(f32)  85.7 us
    reduce_scatter x1, waiting for transfers between devices, shards(): lax.psum_scatter(grad_first, SPREAD, scatter_dimension=0, tiled=True)  68.4 us
    ppermute x12, waiting for transfers between devices, gather_ring(): got.append(lax.ppermute(block, RING, turn(-k)))  63.5 us
    unnamed x128, local copies, waits for them, and re-layouts  24.2 us
    ppermute x12, starting transfers between devices, gather_ring(): got.append(lax.ppermute(block, RING, turn(-k)))  17.6 us
    all_gather x1, waiting for transfers between devices, shards(): first = lax.all_gather(first, SPREAD, axis=0, tiled=True)  14.8 us
  transfers between devices with their start and end apart: 41, of which 22 were waited for; matrix products, arithmetic and copies ran while one was open for 24% of the time, Pallas kernels for 0%

profile of v1, /device:TPU:0, one launch (start us, length us, event | category | flops | bytes accessed | tf_op | source)
XLA Modules:
  0.0 606.6 jit_solution(7515879627692219187)
XLA Ops:
  7.2 3.4 collective-permute-start.3
  16.6 2.5 collective-permute-start.5
  19.1 2.9 collective-permute-done.5
  24.3 4.3 collective-permute-start.13
  28.6 5.7 collective-permute-done.13
  35.3 2.6 collective-permute-start.2
  42.3 20.7 %collective-permute-done.2 = bf16[128,2048]{1,0:T(8,128)(2,1)S(1)} collective-permute-done((bf16[128,2048]{1,0:T(8,128)(2,1)S(1)}, bf16[128,2048]{1,0:T(8,128)(2,1)S(1)}, u32[]{:S(2)}, u32[]{:S(2)}) %collective-permute-start.2) | collective-permute-done | bytes 524320 | tf_op jit(solution)/shard_map/ppermute | solution.py:59
  63.4 1.9 fusion.15
  65.3 14.8 %all-gather.3.cloned.1.call-done = bf16[2048,2176]{1,0:T(8,128)(2,1)} async-done(((bf16[64,2176]{1,0:T(8,128)(2,1)}), bf16[2048,2176]{1,0:T(8,128)(2,1)}) %all-gather.3.cloned.1.call-update) | async-done | bytes 8912912 | tf_op jit(solution)/shard_map/all_gather | solution.py:129
  83.0 2.3 slice_reduce_fusion.1
  85.3 7.9 %fusion.16 = f32[512,1536]{1,0:T(8,128)} fusion(bf16[2048,2176]{1,0:T(8,128)(2,1)} %all-gather.3.cloned.1.call-done, f32[1536]{0:T(1024)S(1)} %reshape.338, f32[2048]{0:T(1024)S(1)} %get-tuple-element.50, f32[2048]{0:T(1024)S(1)} %get-tuple-element.51, f32[512]{0:T(512)S(1)} %add_rsqrt_fusion, f32[512]{0:T(512)S(1)} %broadcast_multiply_fusion, ...), kind=kOutput, calls=%fused_computation.28 | convolution fusion | flops 3235643392 | bytes 11560960 | tf_op jit(solution)/shard_map/dot_general | solution.py:32
  93.3 5.9 reshape.349
  99.2 1.8 slice.245
  102.4 3.9 fusion.84
  106.3 3.1 copy.145
  110.6 1.7 copy.144
  114.7 4.5 fusion.89
  119.3 2.7 fusion.33
  122.6 3.2 fusion.90
  126.0 2.8 collective-permute-start.8
  128.9 2.3 collective-permute-start.6
  132.4 3.2 collective-permute-start.18
  135.7 27.8 %collective-permute-done.8 = bf16[128,2048]{1,0:T(8,128)(2,1)S(1)} collective-permute-done((bf16[128,2048]{1,0:T(8,128)(2,1)S(1)}, bf16[128,2048]{1,0:T(8,128)(2,1)S(1)}, u32[]{:S(2)}, u32[]{:S(2)}) %collective-permute-start.8) | collective-permute-done | bytes 524320 | tf_op jit(solution)/shard_map/ppermute | solution.py:68
  163.5 2.7 collective-permute-done.7
  167.4 3.2 collective-permute-start.10
  172.0 2.8 collective-permute-done.18
  174.9 5.3 collective-permute-done.19
  180.2 10.5 %collective-permute-done.11 = bf16[128,2048]{1,0:T(8,128)(2,1)S(1)} collective-permute-done((bf16[128,2048]{1,0:T(8,128)(2,1)S(1)}, bf16[128,2048]{1,0:T(8,128)(2,1)S(1)}, u32[]{:S(2)}, u32[]{:S(2)}) %collective-permute-start.11) | collective-permute-done | bytes 524320 | tf_op jit(solution)/shard_map/ppermute | solution.py:59
  190.7 5.8 collective-permute-done.10
  197.3 3.7 collective-permute-done.9
  201.1 20.0 %fusion.3 = f32[512,2816]{1,0:T(8,128)S(1)} fusion(bf16[2048,4224]{1,0:T(8,128)(2,1)} %all-gather.5.cloned.1.call-done, bf16[128,2048]{1,0:T(8,128)(2,1)} %copy-done.50, bf16[128,2048]{1,0:T(8,128)(2,1)} %copy-done.52, bf16[128,2048]{1,0:T(8,128)(2,1)} %collective-permute-done.9, bf16[128,2048]{1,0:T(8,128)(2,1)S(1)} %add_convert_fusion.1), kind=kOutput, calls=%fused_computation.4 | convolution fusion | flops 5913968640 | bytes 19398656 | tf_op jit(solution)/shard_map/dot_general | solution.py:32
  221.1 8.5 %multiply_convert_fusion.2 = (bf16[512,1408]{1,0:T(8,128)(2,1)}, bf16[512,1408]{1,0:T(8,128)(2,1)}, bf16[512,1408]{1,0:T(8,128)(2,1)S(1)}) fusion(f32[512,2816]{1,0:T(8,128)S(1)} %fusion.3, bf16[512,2048]{1,0:T(8,128)(2,1)S(1)} %copy-done.31, bf16[2048,4224]{1,0:T(8,128)(2,1)} %all-gather.5.cloned.1.call-done), kind=kOutput, calls=%fused_computation.34 | convolution fusion | flops 2963603456 | bytes 17956864 | tf_op jit(solution)/shard_map/dot_general | solution.py:32
  229.7 9.8 %fusion.91 = (bf16[512,2048]{1,0:T(8,128)(2,1)S(1)}, f32[512,2048]{1,0:T(8,128)S(1)}) fusion(bf16[2048,4224]{1,0:T(8,128)(2,1)} %all-gather.5.cloned.1.call-done, bf16[512,1408]{1,0:T(8,128)(2,1)} %get-tuple-element.61, bf16[512,1408]{1,0:T(8,128)(2,1)} %get-tuple-element.60), kind=kOutput, calls=%fused_computation.216 | convolution fusion | flops 5912395776 | bytes 20709376 | tf_op jit(solution)/shard_map/dot_general | solution.py:32
  240.0 1.7 collective-permute-start.21
  241.8 5.5 fusion.92
  247.4 2.7 collective-permute-start.16
  250.2 11.7 %collective-permute-done.22 = bf16[128,2048]{1,0:T(8,128)(2,1)S(1)} collective-permute-done((bf16[128,2048]{1,0:T(8,128)(2,1)S(1)}, bf16[128,2048]{1,0:T(8,128)(2,1)S(1)}, u32[]{:S(2)}, u32[]{:S(2)}) %collective-permute-start.22) | collective-permute-done | bytes 524320 | tf_op jit(solution)/shard_map/ppermute | solution.py:68
  261.9 5.4 collective-permute-done.21
  268.6 15.8 %collective-permute-done.16 = bf16[128,2048]{1,0:T(8,128)(2,1)S(1)} collective-permute-done((bf16[128,2048]{1,0:T(8,128)(2,1)S(1)}, bf16[128,2048]{1,0:T(8,128)(2,1)S(1)}, u32[]{:S(2)}, u32[]{:S(2)}) %collective-permute-start.16) | collective-permute-done | bytes 524320 | tf_op jit(solution)/shard_map/ppermute | solution.py:68
  284.4 3.4 collective-permute-done.15
  287.7 1.8 fusion.79
  289.6 3.2 collective-permute-start.24
  292.8 5.3 convolution_convert_fusion.2
  298.4 14.7 %collective-permute-done.25 = bf16[128,2048]{1,0:T(8,128)(2,1)S(1)} collective-permute-done((bf16[128,2048]{1,0:T(8,128)(2,1)}, bf16[128,2048]{1,0:T(8,128)(2,1)S(1)}, u32[]{:S(2)}, u32[]{:S(2)}) %collective-permute-start.25) | collective-permute-done | bytes 524320 | tf_op jit(solution)/shard_map/ppermute | solution.py:59
  314.0 4.1 fusion.30
  321.2 3.7 multiply_reduce_fusion.1
  335.6 2.9 convolution_convert_fusion.3
  338.6 8.6 %multiply_reduce_fusion = (f32[2048]{0:T(1024)S(1)}, f32[2048]{0:T(1024)S(1)}, bf16[512,2048]{1,0:T(8,128)(2,1)}, f32[512,2048]{1,0:T(8,128)}, f32[512,2048]{1,0:T(8,128)}) fusion(f32[512]{0:T(512)S(1)} %copy-done.49, f32[512]{0:T(512)S(1)} %copy-done.45, bf16[128,2048]{1,0:T(8,128)(2,1)S(1)} %copy-done.7, bf16[128,2048]{1,0:T(8,128)(2,1)S(1)} %copy-done.9, ...), kind=kOutput, calls=%fused_computation.22 | convolution fusion | flops 3235901440 | bytes 20467712 | tf_op jit(solution)/shard_map/dot_general | solution.py:32
  347.4 4.4 convolution_convert_fusion.1
  351.7 4.3 pad_maximum_fusion
  356.1 11.8 %copy.135 = bf16[2048,2176]{1,0:T(8,128)(2,1)} copy(bf16[2048,2176]{0,1:T(8,128)(2,1)} %pad_maximum_fusion) | data formatting | bytes 17825792
  369.3 10.8 %convolution_convert_fusion = bf16[2048,2816]{1,0:T(8,128)(2,1)} fusion(bf16[512,1408]{1,0:T(8,128)(2,1)} %get-tuple-element.61, bf16[512,1408]{1,0:T(8,128)(2,1)} %get-tuple-element.60, bf16[128,2048]{1,0:T(8,128)(2,1)S(1)} %copy-done.51, bf16[128,2048]{1,0:T(8,128)(2,1)S(1)} %copy-done.53, bf16[128,2048]{1,0:T(8,128)(2,1)} %collective-permute-done.9, ...), kind=kOutput, calls=%fused_computation.1 | convolution fusion | flops 5925502976 | bytes 16515072 | tf_op jit(solution)/shard_map/dot_general | solution.py:32
  381.6 2.8 collective-permute-start.28
  385.9 15.3 %collective-permute-done.28 = bf16[128,2048]{1,0:T(8,128)(2,1)S(1)} collective-permute-done((bf16[128,2048]{1,0:T(8,128)(2,1)S(1)}, bf16[128,2048]{1,0:T(8,128)(2,1)S(1)}, u32[]{:S(2)}, u32[]{:S(2)}) %collective-permute-start.28) | collective-permute-done | bytes 524320 | tf_op jit(solution)/shard_map/ppermute | solution.py:68
  401.3 3.5 collective-permute-done.27
  404.8 2.5 fusion.77
  409.0 2.5 multiply_add_fusion
  411.6 2.0 collective-permute-done.35
  413.6 68.4 %reduce-scatter.10.cloned.1.call-done = bf16[64,2176]{1,0:T(8,128)(2,1)} async-done(((bf16[2048,2176]{1,0:T(8,128)(2,1)}), bf16[64,2176]{1,0:T(8,128)(2,1)}) %reduce-scatter.10.cloned.1.call-update) | async-done | bytes 278544 | tf_op jit(solution)/shard_map/reduce_scatter | solution.py:218
  483.7 2.9 collective-permute-start.30
  487.4 3.5 collective-permute-done.30
  491.2 94.8 %reduce-scatter.6.cloned.1.call-done = bf16[64,2816]{1,0:T(8,128)(2,1)} async-done(((bf16[2048,2816]{1,0:T(8,128)(2,1)}), bf16[64,2816]{1,0:T(8,128)(2,1)}) %reduce-scatter.6.cloned.1.call-update) | async-done | bytes 360464 | tf_op jit(solution)/shard_map/reduce_scatter | solution.py:179
  587.7 2.9 collective-permute-start.33
  590.5 3.0 collective-permute-start.31
  (283 shorter events, 61.2 us)
Async XLA Ops:
  7.2 15.7 %copy-start.18 = (bf16[2,32,2816]{2,1,0:T(8,128)(2,1)S(1)}, bf16[2,32,2816]{2,1,0:T(8,128)(2,1)}, u32[]{:S(2)}) copy-start(bf16[2,32,2816]{2,1,0:T(8,128)(2,1)} %param.14) | copy-start | bytes 1081348
  7.2 16.4 %copy-start.27 = (bf16[2816,32]{0,1:T(8,128)(2,1)S(1)}, bf16[2816,32]{0,1:T(8,128)(2,1)}, u32[]{:S(2)}) copy-start(bf16[2816,32]{0,1:T(8,128)(2,1)} %param.15) | copy-start | bytes 540676
  7.2 72.9 %all-gather.3.cloned.1.call-start = ((), (), s32[]{:S(2)}) async-start(), calls=%async_computation.3 | async-start | bytes 9191424 | tf_op jit(solution)/shard_map/all_gather | solution.py:129
  7.2 6.6 %collective-permute-start.3 = (f32[4,16]{1,0:T(4,128)}, f32[4,16]{1,0:T(4,128)S(1)}, u32[]{:S(2)}, u32[]{:S(2)}) collective-permute-start(f32[4,16]{1,0:T(4,128)} %param.10), channel_id=1, source_target_pairs={{0,1},{1,0},{2,3},{3,2},{4,5},{5,4},{6,7},{7,6},{8,9},{9,8},{10,11... | collective-permute-start | bytes 776 | tf_op jit(solution)/shard_map/ppermute | solution.py:114
  15.7 19.5 %copy-start = (bf16[128,2048]{1,0:T(8,128)(2,1)S(1)}, bf16[128,2048]{1,0:T(8,128)(2,1)}, u32[]{:S(2)}) copy-start(bf16[128,2048]{1,0:T(8,128)(2,1)} %param.8) | copy-start | bytes 1572868
  15.8 3.3 collective-permute-start.4
  16.6 5.4 collective-permute-start.5
  22.8 178.3 %all-gather.5.cloned.1.call-start = ((), (), s32[]{:S(2)}) async-start(), calls=%async_computation.4 | async-start | bytes 17842176 | tf_op jit(solution)/shard_map/all_gather | solution.py:130
  23.6 5.0 collective-permute-start.12
  24.3 10.0 %collective-permute-start.13 = (bf16[32,4224]{1,0:T(8,128)(2,1)S(1)}, bf16[32,4224]{1,0:T(8,128)(2,1)S(1)}, u32[]{:S(2)}, u32[]{:S(2)}) collective-permute-start(bf16[32,4224]{1,0:T(8,128)(2,1)S(1)} %get-tuple-element.91), channel_id=1, source_target_pairs={{0,4},{2,0},{4,6},{6,2},{1,5},{3,1},{5,7},{7,3},{8,12},{10,8},{12,... | collective-permute-start | bytes 811016 | tf_op jit(solution)/shard_map/ppermute | solution.py:38
  35.2 372.0 %reduce-scatter.8.cloned.1.call-start = ((), (), s32[]{:S(2)}) async-start(), calls=%async_computation.6 | async-start | bytes 5947392 | tf_op jit(solution)/shard_map/reduce_scatter | solution.py:173
  35.3 27.7 %collective-permute-start.2 = (bf16[128,2048]{1,0:T(8,128)(2,1)S(1)}, bf16[128,2048]{1,0:T(8,128)(2,1)S(1)}, u32[]{:S(2)}, u32[]{:S(2)}) collective-permute-start(bf16[128,2048]{1,0:T(8,128)(2,1)S(1)} %copy-done), channel_id=1, source_target_pairs={{0,4},{4,1},{1,5},{5,0},{2,6},{6,3},{3,7},{7,2},{8,12},{12,9},{9,1... | collective-permute-start | bytes 1572872 | tf_op jit(solution)/shard_map/ppermute | solution.py:59
  37.8 25.2 %collective-permute-start.1 = (bf16[128,2048]{1,0:T(8,128)(2,1)S(1)}, bf16[128,2048]{1,0:T(8,128)(2,1)S(1)}, u32[]{:S(2)}, u32[]{:S(2)}) collective-permute-start(bf16[128,2048]{1,0:T(8,128)(2,1)S(1)} %copy-done), channel_id=1, source_target_pairs={{0,5},{4,0},{1,4},{5,1},{2,7},{6,2},{3,6},{7,3},{8,13},{12,8},{9,1... | collective-permute-start | bytes 1572872 | tf_op jit(solution)/shard_map/ppermute | solution.py:59
  39.1 23.9 %collective-permute-start = (bf16[128,2048]{1,0:T(8,128)(2,1)S(1)}, bf16[128,2048]{1,0:T(8,128)(2,1)S(1)}, u32[]{:S(2)}, u32[]{:S(2)}) collective-permute-start(bf16[128,2048]{1,0:T(8,128)(2,1)S(1)} %copy-done), channel_id=1, source_target_pairs={{0,1},{4,5},{1,0},{5,4},{2,3},{6,7},{3,2},{7,6},{8,9},{12,13},{9,8... | collective-permute-start | bytes 1572872 | tf_op jit(solution)/shard_map/ppermute | solution.py:59
  63.0 22.3 %copy-start.6 = (bf16[128,2048]{1,0:T(8,128)(2,1)}, bf16[128,2048]{1,0:T(8,128)(2,1)S(1)}, u32[]{:S(2)}) copy-start(bf16[128,2048]{1,0:T(8,128)(2,1)S(1)} %collective-permute-done.2) | copy-start | bytes 1572868
  63.0 22.3 %copy-start.8 = (bf16[128,2048]{1,0:T(8,128)(2,1)}, bf16[128,2048]{1,0:T(8,128)(2,1)S(1)}, u32[]{:S(2)}) copy-start(bf16[128,2048]{1,0:T(8,128)(2,1)S(1)} %collective-permute-done.1) | copy-start | bytes 1572868
  63.0 22.3 %copy-start.10 = (bf16[128,2048]{1,0:T(8,128)(2,1)}, bf16[128,2048]{1,0:T(8,128)(2,1)S(1)}, u32[]{:S(2)}) copy-start(bf16[128,2048]{1,0:T(8,128)(2,1)S(1)} %collective-permute-done) | copy-start | bytes 1572868
  63.4 22.0 %copy-start.44 = (f32[512]{0:T(512)}, f32[512]{0:T(512)S(1)}, u32[]{:S(2)}) copy-start(f32[512]{0:T(512)S(1)} %broadcast_multiply_fusion) | copy-start | bytes 6148
  65.3 27.9 %copy-start.48 = (f32[512]{0:T(512)}, f32[512]{0:T(512)S(1)}, u32[]{:S(2)}) copy-start(f32[512]{0:T(512)S(1)} %add_rsqrt_fusion) | copy-start | bytes 6148
  125.8 41.2 %copy-start.28 = (f32[2048]{0:T(1024)S(1)}, f32[2048]{0:T(1024)}, u32[]{:S(2)}) copy-start(f32[2048]{0:T(1024)} %get-tuple-element.48) | copy-start | bytes 24580
  125.8 41.2 %copy-start.35 = (f32[2048]{0:T(1024)S(1)}, f32[2048]{0:T(1024)}, u32[]{:S(2)}) copy-start(f32[2048]{0:T(1024)} %get-tuple-element.49) | copy-start | bytes 24580
  126.0 37.5 %collective-permute-start.8 = (bf16[128,2048]{1,0:T(8,128)(2,1)S(1)}, bf16[128,2048]{1,0:T(8,128)(2,1)S(1)}, u32[]{:S(2)}, u32[]{:S(2)}) collective-permute-start(bf16[128,2048]{1,0:T(8,128)(2,1)S(1)} %get-tuple-element.77), channel_id=1, source_target_pairs={{0,5},{4,0},{1,4},{5,1},{2,7},{6,2},{3,6},{7,3},{8,13},{12,8},{9,1... | collective-permute-start | bytes 1572872 | tf_op jit(solution)/shard_map/ppermute | solution.py:68
  128.9 37.3 %collective-permute-start.7 = (bf16[128,2048]{1,0:T(8,128)(2,1)S(1)}, bf16[128,2048]{1,0:T(8,128)(2,1)S(1)}, u32[]{:S(2)}, u32[]{:S(2)}) collective-permute-start(bf16[128,2048]{1,0:T(8,128)(2,1)S(1)} %get-tuple-element.78), channel_id=1, source_target_pairs={{0,4},{4,1},{1,5},{5,0},{2,6},{6,3},{3,7},{7,2},{8,12},{12,9},{9,1... | collective-permute-start | bytes 1572872 | tf_op jit(solution)/shard_map/ppermute | solution.py:68
  128.9 37.3 %collective-permute-start.6 = (bf16[128,2048]{1,0:T(8,128)(2,1)S(1)}, bf16[128,2048]{1,0:T(8,128)(2,1)S(1)}, u32[]{:S(2)}, u32[]{:S(2)}) collective-permute-start(bf16[128,2048]{1,0:T(8,128)(2,1)S(1)} %get-tuple-element.76), channel_id=1, source_target_pairs={{0,1},{4,5},{1,0},{5,4},{2,3},{6,7},{3,2},{7,6},{8,9},{12,13},{9,8... | collective-permute-start | bytes 1572872 | tf_op jit(solution)/shard_map/ppermute | solution.py:68
  131.2 39.4 %collective-permute-start.17 = (bf16[128,2048]{1,0:T(8,128)(2,1)S(1)}, bf16[128,2048]{1,0:T(8,128)(2,1)S(1)}, u32[]{:S(2)}, u32[]{:S(2)}) collective-permute-start(bf16[128,2048]{1,0:T(8,128)(2,1)S(1)} %copy-done.4), channel_id=1, source_target_pairs={{0,1},{4,5},{1,0},{5,4},{2,3},{6,7},{3,2},{7,6},{8,9},{12,13},{9,8... | collective-permute-start | bytes 1572872 | tf_op jit(solution)/shard_map/ppermute | solution.py:59
  132.4 42.5 %collective-permute-start.18 = (bf16[128,2048]{1,0:T(8,128)(2,1)S(1)}, bf16[128,2048]{1,0:T(8,128)(2,1)S(1)}, u32[]{:S(2)}, u32[]{:S(2)}) collective-permute-start(bf16[128,2048]{1,0:T(8,128)(2,1)S(1)} %copy-done.4), channel_id=1, source_target_pairs={{0,5},{4,0},{1,4},{5,1},{2,7},{6,2},{3,6},{7,3},{8,13},{12,8},{9,1... | collective-permute-start | bytes 1572872 | tf_op jit(solution)/shard_map/ppermute | solution.py:59
  163.5 16.7 %collective-permute-start.19 = (bf16[128,2048]{1,0:T(8,128)(2,1)S(1)}, bf16[128,2048]{1,0:T(8,128)(2,1)S(1)}, u32[]{:S(2)}, u32[]{:S(2)}) collective-permute-start(bf16[128,2048]{1,0:T(8,128)(2,1)S(1)} %copy-done.4), channel_id=1, source_target_pairs={{0,4},{4,1},{1,5},{5,0},{2,6},{6,3},{3,7},{7,2},{8,12},{12,9},{9,1... | collective-permute-start | bytes 1572872 | tf_op jit(solution)/shard_map/ppermute | solution.py:59
  166.7 29.8 %copy-start.40 = (f32[128]{0:T(128)}, f32[128]{0:T(128)S(1)}, u32[]{:S(2)}) copy-start(f32[128]{0:T(128)S(1)} %broadcast_multiply_fusion.5) | copy-start | bytes 1540
  167.0 29.5 %copy-start.46 = (f32[128]{0:T(128)}, f32[128]{0:T(128)S(1)}, u32[]{:S(2)}) copy-start(f32[128]{0:T(128)S(1)} %add_rsqrt_fusion.1) | copy-start | bytes 1540
  167.3 53.8 %copy-start.16 = (bf16[128,2048]{1,0:T(8,128)(2,1)}, bf16[128,2048]{1,0:T(8,128)(2,1)S(1)}, u32[]{:S(2)}) copy-start(bf16[128,2048]{1,0:T(8,128)(2,1)S(1)} %add_convert_fusion.1) | copy-start | bytes 1572868
  167.3 23.4 %collective-permute-start.11 = (bf16[128,2048]{1,0:T(8,128)(2,1)S(1)}, bf16[128,2048]{1,0:T(8,128)(2,1)S(1)}, u32[]{:S(2)}, u32[]{:S(2)}) collective-permute-start(bf16[128,2048]{1,0:T(8,128)(2,1)S(1)} %add_convert_fusion.1), channel_id=1, source_target_pairs={{0,4},{4,1},{1,5},{5,0},{2,6},{6,3},{3,7},{7,2},{8,12},{12,9},{9,1... | collective-permute-start | bytes 1572872 | tf_op jit(solution)/shard_map/ppermute | solution.py:59
  167.4 29.1 %collective-permute-start.10 = (bf16[128,2048]{1,0:T(8,128)(2,1)S(1)}, bf16[128,2048]{1,0:T(8,128)(2,1)S(1)}, u32[]{:S(2)}, u32[]{:S(2)}) collective-permute-start(bf16[128,2048]{1,0:T(8,128)(2,1)S(1)} %add_convert_fusion.1), channel_id=1, source_target_pairs={{0,5},{4,0},{1,4},{5,1},{2,7},{6,2},{3,6},{7,3},{8,13},{12,8},{9,1... | collective-permute-start | bytes 1572872 | tf_op jit(solution)/shard_map/ppermute | solution.py:59
  170.6 30.5 %collective-permute-start.9 = (bf16[128,2048]{1,0:T(8,128)(2,1)S(1)}, bf16[128,2048]{1,0:T(8,128)(2,1)}, u32[]{:S(2)}, u32[]{:S(2)}) collective-permute-start(bf16[128,2048]{1,0:T(8,128)(2,1)S(1)} %add_convert_fusion.1), channel_id=1, source_target_pairs={{0,1},{4,5},{1,0},{5,4},{2,3},{6,7},{3,2},{7,6},{8,9},{12,13},{9,8... | collective-permute-start | bytes 1572872 | tf_op jit(solution)/shard_map/ppermute | solution.py:59
  180.2 16.3 %copy-start.30 = (bf16[512,2048]{1,0:T(8,128)(2,1)}, bf16[512,2048]{1,0:T(8,128)(2,1)S(1)}, u32[]{:S(2)}) copy-start(bf16[512,2048]{1,0:T(8,128)(2,1)S(1)} %constant_dynamic-update-slice_fusion) | copy-start | bytes 6291460
  201.1 20.1 %copy-start.31 = (bf16[512,2048]{1,0:T(8,128)(2,1)S(1)}, bf16[512,2048]{1,0:T(8,128)(2,1)}, u32[]{:S(2)}) copy-start(bf16[512,2048]{1,0:T(8,128)(2,1)} %copy-done.30) | copy-start | bytes 6291460
  239.7 22.2 %collective-permute-start.22 = (bf16[128,2048]{1,0:T(8,128)(2,1)S(1)}, bf16[128,2048]{1,0:T(8,128)(2,1)S(1)}, u32[]{:S(2)}, u32[]{:S(2)}) collective-permute-start(bf16[128,2048]{1,0:T(8,128)(2,1)S(1)} %get-tuple-element.71), channel_id=1, source_target_pairs={{0,5},{4,0},{1,4},{5,1},{2,7},{6,2},{3,6},{7,3},{8,13},{12,8},{9,1... | collective-permute-start | bytes 1572872 | tf_op jit(solution)/shard_map/ppermute | solution.py:68
  240.0 27.3 %collective-permute-start.21 = (bf16[128,2048]{1,0:T(8,128)(2,1)S(1)}, bf16[128,2048]{1,0:T(8,128)(2,1)S(1)}, u32[]{:S(2)}, u32[]{:S(2)}) collective-permute-start(bf16[128,2048]{1,0:T(8,128)(2,1)S(1)} %get-tuple-element.72), channel_id=1, source_target_pairs={{0,4},{4,1},{1,5},{5,0},{2,6},{6,3},{3,7},{7,2},{8,12},{12,9},{9,1... | collective-permute-start | bytes 1572872 | tf_op jit(solution)/shard_map/ppermute | solution.py:68
  241.8 25.6 %collective-permute-start.20 = (bf16[128,2048]{1,0:T(8,128)(2,1)S(1)}, bf16[128,2048]{1,0:T(8,128)(2,1)S(1)}, u32[]{:S(2)}, u32[]{:S(2)}) collective-permute-start(bf16[128,2048]{1,0:T(8,128)(2,1)S(1)} %get-tuple-element.70), channel_id=1, source_target_pairs={{0,1},{4,5},{1,0},{5,4},{2,3},{6,7},{3,2},{7,6},{8,9},{12,13},{9,8... | collective-permute-start | bytes 1572872 | tf_op jit(solution)/shard_map/ppermute | solution.py:68
  241.8 25.6 %copy-start.29 = (f32[2048]{0:T(1024)S(1)}, f32[2048]{0:T(1024)}, u32[]{:S(2)}) copy-start(f32[2048]{0:T(1024)} %get-tuple-element.48) | copy-start | bytes 24580
  241.8 25.6 %copy-start.41 = (f32[128]{0:T(128)S(1)}, f32[128]{0:T(128)}, u32[]{:S(2)}) copy-start(f32[128]{0:T(128)} %copy-done.40) | copy-start | bytes 1540
  241.8 25.6 %copy-start.47 = (f32[128]{0:T(128)S(1)}, f32[128]{0:T(128)}, u32[]{:S(2)}) copy-start(f32[128]{0:T(128)} %copy-done.46) | copy-start | bytes 1540
  247.3 40.4 %copy-start.5 = (bf16[128,2048]{1,0:T(8,128)(2,1)S(1)}, bf16[128,2048]{1,0:T(8,128)(2,1)}, u32[]{:S(2)}) copy-start(bf16[128,2048]{1,0:T(8,128)(2,1)} %param.9) | copy-start | bytes 1572868
  247.4 36.9 %collective-permute-start.16 = (bf16[128,2048]{1,0:T(8,128)(2,1)S(1)}, bf16[128,2048]{1,0:T(8,128)(2,1)S(1)}, u32[]{:S(2)}, u32[]{:S(2)}) collective-permute-start(bf16[128,2048]{1,0:T(8,128)(2,1)S(1)} %get-tuple-element.74), channel_id=1, source_target_pairs={{0,5},{4,0},{1,4},{5,1},{2,7},{6,2},{3,6},{7,3},{8,13},{12,8},{9,1... | collective-permute-start | bytes 1572872 | tf_op jit(solution)/shard_map/ppermute | solution.py:68
  250.2 37.6 %collective-permute-start.15 = (bf16[128,2048]{1,0:T(8,128)(2,1)S(1)}, bf16[128,2048]{1,0:T(8,128)(2,1)S(1)}, u32[]{:S(2)}, u32[]{:S(2)}) collective-permute-start(bf16[128,2048]{1,0:T(8,128)(2,1)S(1)} %get-tuple-element.75), channel_id=1, source_target_pairs={{0,4},{4,1},{1,5},{5,0},{2,6},{6,3},{3,7},{7,2},{8,12},{12,9},{9,1... | collective-permute-start | bytes 1572872 | tf_op jit(solution)/shard_map/ppermute | solution.py:68
  261.9 25.8 %collective-permute-start.14 = (bf16[128,2048]{1,0:T(8,128)(2,1)S(1)}, bf16[128,2048]{1,0:T(8,128)(2,1)S(1)}, u32[]{:S(2)}, u32[]{:S(2)}) collective-permute-start(bf16[128,2048]{1,0:T(8,128)(2,1)S(1)} %get-tuple-element.73), channel_id=1, source_target_pairs={{0,1},{4,5},{1,0},{5,4},{2,3},{6,7},{3,2},{7,6},{8,9},{12,13},{9,8... | collective-permute-start | bytes 1572872 | tf_op jit(solution)/shard_map/ppermute | solution.py:68
  289.6 23.5 %collective-permute-start.25 = (bf16[128,2048]{1,0:T(8,128)(2,1)}, bf16[128,2048]{1,0:T(8,128)(2,1)S(1)}, u32[]{:S(2)}, u32[]{:S(2)}) collective-permute-start(bf16[128,2048]{1,0:T(8,128)(2,1)} %get-tuple-element.53), channel_id=1, source_target_pairs={{0,4},{4,1},{1,5},{5,0},{2,6},{6,3},{3,7},{7,2},{8,12},{12,9},{9,1... | collective-permute-start | bytes 1572872 | tf_op jit(solution)/shard_map/ppermute | solution.py:59
  289.6 23.5 %collective-permute-start.24 = (bf16[128,2048]{1,0:T(8,128)(2,1)}, bf16[128,2048]{1,0:T(8,128)(2,1)S(1)}, u32[]{:S(2)}, u32[]{:S(2)}) collective-permute-start(bf16[128,2048]{1,0:T(8,128)(2,1)} %get-tuple-element.53), channel_id=1, source_target_pairs={{0,5},{4,0},{1,4},{5,1},{2,7},{6,2},{3,6},{7,3},{8,13},{12,8},{9,1... | collective-permute-start | bytes 1572872 | tf_op jit(solution)/shard_map/ppermute | solution.py:59
  292.8 20.3 %collective-permute-start.23 = (bf16[128,2048]{1,0:T(8,128)(2,1)}, bf16[128,2048]{1,0:T(8,128)(2,1)}, u32[]{:S(2)}, u32[]{:S(2)}) collective-permute-start(bf16[128,2048]{1,0:T(8,128)(2,1)} %get-tuple-element.53), channel_id=1, source_target_pairs={{0,1},{4,5},{1,0},{5,4},{2,3},{6,7},{3,2},{7,6},{8,9},{12,13},{9,8... | collective-permute-start | bytes 1572872 | tf_op jit(solution)/shard_map/ppermute | solution.py:59
  298.1 183.9 %reduce-scatter.10.cloned.1.call-start = ((), (), s32[]{:S(2)}) async-start(), calls=%async_computation.7 | async-start | bytes 9191424 | tf_op jit(solution)/shard_map/reduce_scatter | solution.py:218
  338.6 8.7 %copy-start.33 = (f32[2048]{0:T(1024)S(1)}, f32[2048]{0:T(1024)}, u32[]{:S(2)}) copy-start(f32[2048]{0:T(1024)} %get-tuple-element.42) | copy-start | bytes 24580
  338.6 8.7 %copy-start.37 = (f32[2048]{0:T(1024)S(1)}, f32[2048]{0:T(1024)}, u32[]{:S(2)}) copy-start(f32[2048]{0:T(1024)} %copy-done.36) | copy-start | bytes 24580
  338.6 8.7 %copy-start.43 = (f32[2048]{0:T(1024)S(1)}, f32[2048]{0:T(1024)}, u32[]{:S(2)}) copy-start(f32[2048]{0:T(1024)} %copy-done.42) | copy-start | bytes 24580
  367.9 218.0 %reduce-scatter.6.cloned.1.call-start = ((), (), s32[]{:S(2)}) async-start(), calls=%async_computation.5 | async-start | bytes 11894784 | tf_op jit(solution)/shard_map/reduce_scatter | solution.py:179
  380.1 29.0 %slice-start = ((f32[512]{0:T(512)}), f32[128]{0:T(128)S(1)}, s32[]{:S(2)}) async-start(f32[512]{0:T(512)} %copy-done.48), calls=%async_computation.8 | async-start | bytes 1024 | tf_op jit(solution)/shard_map/slice | solution.py:141
  381.6 19.7 %collective-permute-start.28 = (bf16[128,2048]{1,0:T(8,128)(2,1)S(1)}, bf16[128,2048]{1,0:T(8,128)(2,1)S(1)}, u32[]{:S(2)}, u32[]{:S(2)}) collective-permute-start(bf16[128,2048]{1,0:T(8,128)(2,1)S(1)} %get-tuple-element.68), channel_id=1, source_target_pairs={{0,5},{4,0},{1,4},{5,1},{2,7},{6,2},{3,6},{7,3},{8,13},{12,8},{9,1... | collective-permute-start | bytes 1572872 | tf_op jit(solution)/shard_map/ppermute | solution.py:68
  384.4 20.4 %collective-permute-start.27 = (bf16[128,2048]{1,0:T(8,128)(2,1)S(1)}, bf16[128,2048]{1,0:T(8,128)(2,1)}, u32[]{:S(2)}, u32[]{:S(2)}) collective-permute-start(bf16[128,2048]{1,0:T(8,128)(2,1)S(1)} %get-tuple-element.69), channel_id=1, source_target_pairs={{0,4},{4,1},{1,5},{5,0},{2,6},{6,3},{3,7},{7,2},{8,12},{12,9},{9,1... | collective-permute-start | bytes 1572872 | tf_op jit(solution)/shard_map/ppermute | solution.py:68
  384.4 20.4 %collective-permute-start.26 = (bf16[128,2048]{1,0:T(8,128)(2,1)S(1)}, bf16[128,2048]{1,0:T(8,128)(2,1)}, u32[]{:S(2)}, u32[]{:S(2)}) collective-permute-start(bf16[128,2048]{1,0:T(8,128)(2,1)S(1)} %get-tuple-element.67), channel_id=1, source_target_pairs={{0,1},{4,5},{1,0},{5,4},{2,3},{6,7},{3,2},{7,6},{8,9},{12,13},{9,8... | collective-permute-start | bytes 1572872 | tf_op jit(solution)/shard_map/ppermute | solution.py:68
  408.3 3.3 collective-permute-start.34
  408.9 4.6 collective-permute-start.35
  483.0 4.4 collective-permute-start.29
  483.7 7.2 %collective-permute-start.30 = (bf16[32,2176]{1,0:T(8,128)(2,1)S(1)}, bf16[32,2176]{1,0:T(8,128)(2,1)S(1)}, u32[]{:S(2)}, u32[]{:S(2)}) collective-permute-start(bf16[32,2176]{1,0:T(8,128)(2,1)S(1)} %get-tuple-element.99), channel_id=1, source_target_pairs={{4,0},{0,2},{6,4},{2,6},{5,1},{1,3},{7,5},{3,7},{12,8},{8,10},{14,... | collective-permute-start | bytes 417800 | tf_op jit(solution)/shard_map/ppermute | solution.py:50
  587.0 10.3 %collective-permute-start.32 = (bf16[32,2816]{1,0:T(8,128)(2,1)S(1)}, bf16[32,2816]{1,0:T(8,128)(2,1)S(1)}, u32[]{:S(2)}, u32[]{:S(2)}) collective-permute-start(bf16[32,2816]{1,0:T(8,128)(2,1)S(1)} %get-tuple-element.94), channel_id=1, source_target_pairs={{0,0},{4,2},{2,4},{6,6},{1,1},{5,3},{3,5},{7,7},{8,8},{12,10},{10,... | collective-permute-start | bytes 540680 | tf_op jit(solution)/shard_map/ppermute | solution.py:47
  587.7 9.6 %collective-permute-start.33 = (bf16[32,2816]{1,0:T(8,128)(2,1)S(1)}, bf16[32,2816]{1,0:T(8,128)(2,1)S(1)}, u32[]{:S(2)}, u32[]{:S(2)}) collective-permute-start(bf16[32,2816]{1,0:T(8,128)(2,1)S(1)} %get-tuple-element.95), channel_id=1, source_target_pairs={{4,0},{0,2},{6,4},{2,6},{5,1},{1,3},{7,5},{3,7},{12,8},{8,10},{14,... | collective-permute-start | bytes 540680 | tf_op jit(solution)/shard_map/ppermute | solution.py:50
  590.5 6.2 %collective-permute-start.31 = (f32[4,16]{1,0:T(4,128)S(1)}, f32[4,16]{1,0:T(4,128)S(1)}, u32[]{:S(2)}, u32[]{:S(2)}) collective-permute-start(f32[4,16]{1,0:T(4,128)S(1)} %bitcast.196), channel_id=1, source_target_pairs={{0,1},{1,0},{2,3},{3,2},{4,5},{5,4},{6,7},{7,6},{8,9},{9,8},{10,11... | collective-permute-start | bytes 776 | tf_op jit(solution)/shard_map/ppermute | solution.py:250
  (34 other events, 114.6 us)
Sparse Core Ops, SparseCore 0:
  22.9 57.1 all-gather.2
  82.9 73.3 all-gather.4
  298.2 86.1 reduce-scatter.7
  388.5 93.4 reduce-scatter.9
  485.7 100.2 reduce-scatter.5

commit v2 on v1

--- a/solution.py
+++ b/solution.py
@@ -1,6 +1,10 @@
+import functools
+
 import jax
 import jax.numpy as jnp
 from jax import lax
+from jax.experimental import pallas as pl
+from jax.experimental.pallas import tpu as pltpu
 from jax.sharding import Mesh
 from jax.sharding import PartitionSpec as P
 
@@ -12,7 +16,6 @@
 GRID = ("z", "x", "yl", "c", "yh")
 ROWS = ("z", "x", "yl", "c")
 SPREAD = ("z", "x", "c")
-RING = ("yl", "yh")
 PAIR = ("yl", "c")
 EXTRA = 128
 
@@ -23,22 +26,690 @@
 f32 = jnp.float32
 
 
-def turn(k):
-    place = [0, 2, 1, 3]
-    return [(place[y], place[(y + k) % 4]) for y in range(4)]
+MESH = pl.DeviceIdType.MESH
+VMEM = pltpu.VMEM
+DMA = pltpu.SemaphoreType.DMA
+VMEM_LIMIT = 60 * 1024 * 1024
+
+
+def at_y(k):
+    y = (lax.axis_index("yh") * 2 + lax.axis_index("yl") + k) % 4
+    return {"yl": y % 2, "yh": y // 2}
+
+
+def at_z(k):
+    return {"z": (lax.axis_index("z") + k) % 4}
+
+
+def at_x(k):
+    return {"x": (lax.axis_index("x") + k) % 4}
+
+
+def sibling():
+    return {"c": 1 - lax.axis_index("c")}
+
+
+def greet(devices):
+    barrier = pltpu.get_barrier_semaphore()
+    for device in devices:
+        pl.semaphore_signal(barrier, inc=1, device_id=device, device_id_type=MESH)
+    pl.semaphore_wait(barrier, len(devices))
+
+
+def remote(src, dst, sems, index, device):
+    send, recv = sems
+    return pltpu.make_async_remote_copy(
+        src_ref=src,
+        dst_ref=dst,
+        send_sem=send.at[index],
+        recv_sem=recv.at[index],
+        device_id=device,
+        device_id_type=MESH,
+    )
+
+
+def ring_sum(parts, mid, sent, far, near, sems):
+    started = ring_sum_start(parts, mid, near, sems, 0)
+    middle = ring_sum_middle(parts, started, mid, sent, far, sems, 0)
+    return ring_sum_finish(parts, started, middle, far, near), started + middle
+
+
+def ring_gather_half(out, top, sems, base):
+    here = out.shape[0] // 4
+    half = here // 2
+    copies = []
+    for way, step, block in ((0, 1, 3), (1, -1, 2)):
+        copies.append(
+            remote(
+                out.at[pl.ds(top * half, half)],
+                out.at[pl.ds(block * here + top * half, half)],
+                sems,
+                base + 2 * way + top,
+                at_y(step),
+            )
+        )
+        copies[-1].start()
+    return copies
+
+
+def ring_gather_pass(out, halves, sems, base):
+    here = out.shape[0] // 4
+    half = here // 2
+    passed = []
+    for way, step, block in ((0, 1, 3), (1, -1, 2)):
+        halves[way][way].wait_recv()
+        passed.append(
+            remote(
+                out.at[pl.ds(block * here + way * half, half)],
+                out.at[pl.ds(here + way * half, half)],
+                sems,
+                base + 4 + way,
+                at_y(step),
+            )
+        )
+        passed[-1].start()
+    return passed
+
+
+def second_norm_kernel(parts, tokens, gains, summed, unit, scale, normed, mid, sent, far, near, send, recv):
+    sems = (send, recv)
+    greet([at_y(1), at_y(3)])
+    finish, copies = ring_sum(parts, mid, sent, far, near, sems)
+    half = tokens.shape[0] // 2
+    halves = []
+    for top in range(2):
+        rows = pl.ds(top * half, half)
+        total = tokens[rows].astype(f32) + finish(top)
+        summed[rows] = total
+        centered = total - jnp.mean(total, -1, keepdims=True)
+        inverse = lax.rsqrt(jnp.mean(centered * centered, -1, keepdims=True) + EPSILON)
+        unit_rows = centered * inverse
+        unit[rows] = unit_rows
+        scale[rows] = inverse
+        normed[rows] = (unit_rows * gains[0:1] + gains[1:2]).astype(bf16)
+        halves.append(ring_gather_half(normed, top, sems, 6))
+    passed = ring_gather_pass(normed, halves, sems, 6)
+    for copy in passed + [halves[1][0], halves[0][1]]:
+        copy.wait_recv()
+    for copy in copies + halves[0] + halves[1] + passed:
+        copy.wait_send()
+
+
+def second_norm(parts, tokens, gains):
+    here, width = tokens.shape
+    half = here // 2
+    full = pl.BlockSpec(memory_space=VMEM)
+    return pl.pallas_call(
+        second_norm_kernel,
+        out_shape=(
+            jax.ShapeDtypeStruct((here, width), f32),
+            jax.ShapeDtypeStruct((here, width), f32),
+            jax.ShapeDtypeStruct((here, 1), f32),
+            jax.ShapeDtypeStruct((4 * here, width), bf16),
+        ),
+        in_specs=[full] * 3,
+        out_specs=(full,) * 4,
+        scratch_shapes=[VMEM((2, half, width), bf16)] * 4 + [DMA((12,)), DMA((12,))],
+        compiler_params=pltpu.CompilerParams(
+            collective_id=1, has_side_effects=True, vmem_limit_bytes=VMEM_LIMIT
+        ),
+    )(parts, tokens, gains)
+
+
+def second_norm_back_kernel(
+    parts, cotangent, unit, scale, gains, resid, sums, spread, mid, sent, far, near, send, recv
+):
+    sems = (send, recv)
+    greet([at_y(1), at_y(3)])
+    finish, copies = ring_sum(parts, mid, sent, far, near, sems)
+    half = cotangent.shape[0] // 2
+    halves = []
+    for top in range(2):
+        rows = pl.ds(top * half, half)
+        total = finish(top)
+        unit_rows = unit[rows]
+        incoming = total * gains[0:1]
+        result = cotangent[rows].astype(f32) + scale[rows] * (
+            incoming
+            - jnp.mean(incoming, -1, keepdims=True)
+            - unit_rows * jnp.mean(incoming * unit_rows, -1, keepdims=True)
+        )
+        resid[rows] = result
+        spread[rows] = result.astype(bf16)
+        halves.append(ring_gather_half(spread, top, sems, 6))
+        both = jnp.concatenate(
+            [
+                jnp.sum(total * unit_rows, 0, keepdims=True),
+                jnp.sum(total, 0, keepdims=True),
+            ],
+            0,
+        )
+        sums[...] = both if top == 0 else sums[...] + both
+    passed = ring_gather_pass(spread, halves, sems, 6)
+    for copy in passed + [halves[1][0], halves[0][1]]:
+        copy.wait_recv()
+    for copy in copies + halves[0] + halves[1] + passed:
+        copy.wait_send()
+
+
+def second_norm_back(parts, cotangent, unit, scale, gains):
+    here, width = cotangent.shape
+    half = here // 2
+    full = pl.BlockSpec(memory_space=VMEM)
+    return pl.pallas_call(
+        second_norm_back_kernel,
+        out_shape=(
+            jax.ShapeDtypeStruct((here, width), f32),
+            jax.ShapeDtypeStruct((2, width), f32),
+            jax.ShapeDtypeStruct((4 * here, width), bf16),
+        ),
+        in_specs=[full] * 5,
+        out_specs=(full,) * 3,
+        scratch_shapes=[VMEM((2, half, width), bf16)] * 4 + [DMA((12,)), DMA((12,))],
+        compiler_params=pltpu.CompilerParams(
+            collective_id=2, has_side_effects=True, vmem_limit_bytes=VMEM_LIMIT
+        ),
+    )(parts, cotangent, unit, scale, gains)
+
+
+def pair_moves():
+    yl, c = lax.axis_index("yl"), lax.axis_index("c")
+    return {"yl": c, "c": yl}, {"yl": 1 - c, "c": yl}
+
+
+def diagonal():
+    return {"yl": 1 - lax.axis_index("yl"), "c": 1 - lax.axis_index("c")}
+
+
+def everyone_near():
+    return [at_z(1), at_z(3), at_x(1), at_x(3), at_y(1), at_y(3), sibling(), diagonal()]
+
+
+def stay_or_go(src, dst, sems, index, device, local_sem):
+    yl, c = lax.axis_index("yl"), lax.axis_index("c")
+
+    @pl.when(yl == c)
+    def _():
+        pltpu.make_async_copy(src, dst, local_sem).start()
+
+    @pl.when(yl != c)
+    def _():
+        remote(src, dst, sems, index, device).start()
+
+
+def stay_or_go_wait(src, dst, sems, index, device, local_sem):
+    yl, c = lax.axis_index("yl"), lax.axis_index("c")
+
+    @pl.when(yl == c)
+    def _():
+        pltpu.make_async_copy(src, dst, local_sem).wait()
+
+    @pl.when(yl != c)
+    def _():
+        copy = remote(src, dst, sems, index, device)
+        copy.wait_recv()
+        copy.wait_send()
+
+
+def first_gather_kernel(
+    one_q, two_q, tokens, cotangent, one, two, token_rows, cot_rows,
+    pair_send, pair_recv, local_sem, y_send, y_recv, send, recv, core_send, core_recv,
+):
+    z, x = lax.axis_index("z"), lax.axis_index("x")
+    yl, c = lax.axis_index("yl"), lax.axis_index("c")
+    pair_sems, y_sems, sems, core_sems = (
+        (pair_send, pair_recv),
+        (y_send, y_recv),
+        (send, recv),
+        (core_send, core_recv),
+    )
+    rows = one_q.shape[1]
+    here = tokens.shape[0]
+    piece = rows // 2
+    same, cross = pair_moves()
+    token_rows[pl.ds(0, here)] = tokens[...]
+    cot_rows[pl.ds(0, here)] = cotangent[...]
+    greet(everyone_near())
+
+    def start_of(dz, dx, half):
+        return (((z + dz) % 4) * 4 + (x + dx) % 4) * 4 * rows + c * 2 * rows + half * rows
+
+    target = ((z * 4 + x) * 4 + yl * 2 + c) * rows
+    moves = [
+        (one_q.at[c], one.at[pl.ds(target, rows)], 0, same),
+        (one_q.at[1 - c], one.at[pl.ds(target, rows)], 1, cross),
+        (two_q.at[c], two.at[pl.ds(c * rows, rows)], 2, same),
+        (two_q.at[1 - c], two.at[pl.ds(c * rows, rows)], 3, cross),
+    ]
+
+    def launch(k):
+        src, dst, index, device = moves[k]
+        if device is same:
+            stay_or_go(src, dst, pair_sems, index, device, local_sem.at[index // 2])
+        else:
+            remote(src, dst, pair_sems, index, device).start()
+
+    def land(k):
+        src, dst, index, device = moves[k]
+        if device is same:
+            stay_or_go_wait(src, dst, pair_sems, index, device, local_sem.at[index // 2])
+        else:
+            copy = remote(src, dst, pair_sems, index, device)
+            copy.wait_recv()
+            copy.wait_send()
+
+    launch(0)
+    launch(1)
+    y_halves = {}
+    y_passed = {}
+    for top in range(2):
+        y_halves[0, top] = ring_gather_half(token_rows, top, y_sems, 0)
+    land(0)
+    land(1)
+
+    done = []
+
+    def index_of(half, df, dg, part):
+        return ((half * 4 + df % 4) * 4 + dg % 4) * 2 + part
+
+    def block(half, df, dg):
+        return start_of(df, dg, half) if half == 0 else start_of(dg, df, half)
+
+    def push(half, df, dg, axis, step, part):
+        along_z = (half == 0) == (axis == 0)
+        device = at_z(step) if along_z else at_x(step)
+        to = (df - step, dg) if axis == 0 else (df, dg - step)
+        rng = pl.ds(block(half, df, dg) + part * piece, piece)
+        copy = remote(one.at[rng], one.at[rng], sems, index_of(half, *to, part), device)
+        copy.start()
+        done.append(copy)
+
+    def arrived(half, df, dg, part):
+        rng = pl.ds(block(half, df, dg) + part * piece, piece)
+        remote(one.at[rng], one.at[rng], sems, index_of(half, df, dg, part), at_z(1)).wait_recv()
+
+    def to_sibling(half, df, dg):
+        rng = pl.ds(block(half, df, dg), rows)
+        copy = remote(
+            one.at[rng], one.at[rng], core_sems, (half * 4 + df % 4) * 4 + dg % 4, sibling()
+        )
+        copy.start()
+        done.append(copy)
+        core.append(copy)
+
+    core = []
+    for axis in range(2):
+        for half in range(2):
+            for part in range(2):
+                push(half, 0, 0, axis, 1, part)
+                push(half, 0, 0, axis, -1, 1 - part)
+    launch(2)
+    launch(3)
+    for half in range(2):
+        to_sibling(half, 0, 0)
+    for half in range(2):
+        arrived(half, 3, 0, 0)
+        push(half, 3, 0, 0, 1, 0)
+        arrived(half, 1, 0, 1)
+        push(half, 1, 0, 0, -1, 1)
+    for half in range(2):
+        arrived(half, 3, 0, 1)
+        arrived(half, 1, 0, 0)
+        for df in (3, 1):
+            for part in range(2):
+                push(half, df, 0, 1, 1, part)
+                push(half, df, 0, 1, -1, 1 - part)
+            to_sibling(half, df, 0)
+    y_passed[0] = ring_gather_pass(token_rows, [y_halves[0, 0], y_halves[0, 1]], y_sems, 0)
+    for top in range(2):
+        y_halves[1, top] = ring_gather_half(cot_rows, top, y_sems, 6)
+
+    def second_axis(df):
+        for half in range(2):
+            arrived(half, df, 3, 0)
+            push(half, df, 3, 1, 1, 0)
+            arrived(half, df, 1, 1)
+            push(half, df, 1, 1, -1, 1)
+        for half in range(2):
+            arrived(half, df, 3, 1)
+            to_sibling(half, df, 3)
+            arrived(half, df, 1, 0)
+            to_sibling(half, df, 1)
+
+    second_axis(0)
+    for half in range(2):
+        arrived(half, 2, 0, 0)
+        arrived(half, 2, 0, 1)
+        for part in range(2):
+            push(half, 2, 0, 1, 1, part)
+            push(half, 2, 0, 1, -1, 1 - part)
+        to_sibling(half, 2, 0)
+    second_axis(3)
+    second_axis(1)
+    y_passed[1] = ring_gather_pass(cot_rows, [y_halves[1, 0], y_halves[1, 1]], y_sems, 6)
+    second_axis(2)
+    for df in (0, 3, 1, 2):
+        for half in range(2):
+            for part in range(2):
+                arrived(half, df, 2, part)
+            to_sibling(half, df, 2)
+    land(2)
+    land(3)
+    for which in range(2):
+        for copy in y_passed[which] + [y_halves[which, 1][0], y_halves[which, 0][1]]:
+            copy.wait_recv()
+        for copy in y_passed[which] + y_halves[which, 0] + y_halves[which, 1]:
+            copy.wait_send()
+    for copy in core:
+        copy.wait_recv()
+    for copy in done:
+        copy.wait_send()
+
+
+def first_gather(one_q, two_q, tokens, cotangent):
+    rows = one_q.shape[1]
+    here, width = tokens.shape
+    anywhere = pl.BlockSpec(memory_space=pl.ANY)
+    full = pl.BlockSpec(memory_space=VMEM)
+    return pl.pallas_call(
+        first_gather_kernel,
+        out_shape=(
+            jax.ShapeDtypeStruct((64 * rows, one_q.shape[2]), bf16),
+            jax.ShapeDtypeStruct((2 * rows, two_q.shape[2]), bf16),
+            jax.ShapeDtypeStruct((4 * here, width), bf16),
+            jax.ShapeDtypeStruct((4 * here, width), bf16),
+        ),
+        in_specs=[full] * 4,
+        out_specs=(anywhere, anywhere, full, full),
+        scratch_shapes=[
+            DMA((4,)), DMA((4,)), DMA((2,)), DMA((12,)), DMA((12,)),
+            DMA((64,)), DMA((64,)), DMA((32,)), DMA((32,)),
+        ],
+        compiler_params=pltpu.CompilerParams(
+            collective_id=0, has_side_effects=True, vmem_limit_bytes=VMEM_LIMIT
+        ),
+    )(one_q, two_q, tokens, cotangent)
+
+
+def last_sum_kernel(
+    grads, first_parts, mixed_parts, resid, unit, scale, gains, first_sum,
+    result, grad_tokens, mixed,
+    sib, mid, sent, far, near, stage, mid2, sent2, far2, near2, packed,
+    ymid, ysent, yfar, ynear,
+    core_send, core_recv, send, recv, send2, recv2, pair_send, pair_recv, local_sem, y_send, y_recv,
+):
+    z, x = lax.axis_index("z"), lax.axis_index("x")
+    yl, c = lax.axis_index("yl"), lax.axis_index("c")
+    core_sems, sems, sems2, pair_sems, y_sems = (
+        (core_send, core_recv),
+        (send, recv),
+        (send2, recv2),
+        (pair_send, pair_recv),
+        (y_send, y_recv),
+    )
+    rows = result.shape[1]
+    piece = rows // 2
+    greet(everyone_near())
+    done = []
+
+    def begin(copy):
+        copy.start()
+        done.append(copy)
+        return copy
+
+    def start_of(dz, dx, core):
+        return (((z + dz) % 4) * 4 + (x + dx) % 4) * 4 * rows + core * 2 * rows
+
+    order = []
+    for d in (2, 1, 3, 0):
+        for e in (2, 1, 3, 0):
+            for pair in ((d, e), (e, d)):
+                if pair not in order:
+                    order.append(pair)
+    core = {}
+    for dz, dx in order:
+        core[dz, dx] = begin(
+            remote(
+                grads.at[pl.ds(start_of(dz, dx, 1 - c), 2 * rows)],
+                sib.at[dz, dx],
+                core_sems,
+                dz * 4 + dx,
+                sibling(),
+            )
+        )
+    y_jobs = [
+        ring_sum_start(first_parts, ymid.at[0], ynear.at[0], y_sems, 0),
+        ring_sum_start(mixed_parts, ymid.at[1], ynear.at[1], y_sems, 6),
+    ]
+    summed = set()
+
+    def core_sum(dz, dx):
+        if (dz, dx) in summed:
+            return
+        summed.add((dz, dx))
+        core[dz, dx].wait_recv()
+        sib[dz, dx] = (
+            sib[dz, dx].astype(f32)
+            + grads[pl.ds(start_of(dz, dx, c), 2 * rows)].astype(f32)
+        ).astype(bf16)
+
+    def view(half, df, part):
+        rng = pl.ds(half * rows + part * piece, piece)
+        return sib.at[df, :, rng] if half == 0 else sib.at[:, df, rng]
+
+    def device(half, axis, step):
+        return at_z(step) if (half == 0) == (axis == 0) else at_x(step)
+
+    def ring_first(half, axis, src, mids, nears, some_sems):
+        base = half * 6
+        got = {}
+        for way, step in ((0, 1), (1, -1)):
+            got["first", way] = begin(
+                remote(src(2, way), mids.at[half, way], some_sems, base + way, device(half, axis, step))
+            )
+        return got
+
+    def ring_second(half, axis, src, nears, some_sems, got):
+        base = half * 6
+        for way, step in ((0, 1), (1, -1)):
+            got["second", way] = begin(
+                remote(
+                    src(step % 4, 1 - way), nears.at[half, way], some_sems, base + 2 + way,
+                    device(half, axis, step),
+                )
+            )
+
+    def ring_third(half, axis, src, mids, sents, fars, some_sems, got):
+        base = half * 6
+        for way, step in ((0, 1), (1, -1)):
+            got["first", way].wait_recv()
+            sents[half, way] = (
+                src(step % 4, way)[...].astype(f32) + mids[half, way].astype(f32)
+            ).astype(bf16)
+            got["third", way] = begin(
+                remote(
+                    sents.at[half, way], fars.at[half, way], some_sems, base + 4 + way,
+                    device(half, axis, step),
+                )
+            )
+
+    def ring_last(half, part, src, fars, nears, got):
+        got["third", part].wait_recv()
+        got["second", 1 - part].wait_recv()
+        return (
+            src(0, part)[...].astype(f32)
+            + fars[half, part].astype(f32)
+            + nears[half, 1 - part].astype(f32)
+        )
+
+    got = {}
+    sources = [functools.partial(view, half) for half in range(2)]
+    for half in range(2):
+        for d in (2, 1, 3, 0):
+            core_sum(*((2, d) if half == 0 else (d, 2)))
+        got[half] = ring_first(half, 0, sources[half], mid, near, sems)
+    for half in range(2):
+        for step in (1, 3):
+            for d in (2, 1, 3, 0):
+                core_sum(*((step, d) if half == 0 else (d, step)))
+        ring_second(half, 0, sources[half], near, sems, got[half])
+    y_more = [
+        ring_sum_middle(first_parts, y_jobs[0], ymid.at[0], ysent.at[0], yfar.at[0], y_sems, 0)
+    ]
+    for half in range(2):
+        ring_third(half, 0, sources[half], mid, sent, far, sems, got[half])
+    core_sum(0, 0)
+    y_more.append(
+        ring_sum_middle(mixed_parts, y_jobs[1], ymid.at[1], ysent.at[1], yfar.at[1], y_sems, 6)
+    )
+    finish = ring_sum_finish(first_parts, y_jobs[0], y_more[0], yfar.at[0], ynear.at[0])
+    here = grad_tokens.shape[0] // 2
+    for top in range(2):
+        rng = pl.ds(top * here, here)
+        incoming = finish(top) * gains[0:1]
+        unit_rows = unit[rng]
+        grad_tokens[rng] = resid[rng] + scale[rng] * (
+            incoming
+            - jnp.mean(incoming, -1, keepdims=True)
+            - unit_rows * jnp.mean(incoming * unit_rows, -1, keepdims=True)
+        )
+    for half in range(2):
+        for part in range(2):
+            stage[half, :, part * piece : (part + 1) * piece] = ring_last(
+                half, part, sources[half], far, near, got[half]
+            ).astype(bf16)
+
+    def stage_view(half, dg, part):
+        return stage.at[half, dg, pl.ds(part * piece, piece)]
+
+    sources = [functools.partial(stage_view, half) for half in range(2)]
+    got = {}
+    for half in range(2):
+        got[half] = ring_first(half, 1, sources[half], mid2, near2, sems2)
+    for half in range(2):
+        ring_second(half, 1, sources[half], near2, sems2, got[half])
+    for half in range(2):
+        ring_third(half, 1, sources[half], mid2, sent2, far2, sems2, got[half])
+    finish = ring_sum_finish(mixed_parts, y_jobs[1], y_more[1], yfar.at[1], ynear.at[1])
+    for top in range(2):
+        rng = pl.ds(top * here, here)
+        mixed[rng] = (first_sum[rng] + finish(top)).astype(bf16)
+    for half in range(2):
+        for part in range(2):
+            packed[half, part * piece : (part + 1) * piece] = ring_last(
+                half, part, sources[half], far2, near2, got[half]
+            ).astype(bf16)
+
+    home, away = {"yl": c, "c": yl}, {"yl": c, "c": 1 - yl}
+    stay_or_go(packed.at[yl], result.at[yl], pair_sems, 0, home, local_sem)
+    cross = remote(packed.at[1 - yl], result.at[yl], pair_sems, 1, away)
+    cross.start()
+    cross.wait_recv()
+    cross.wait_send()
+    stay_or_go_wait(packed.at[yl], result.at[yl], pair_sems, 0, home, local_sem)
+    for jobs in y_jobs + y_more:
+        for copy in jobs:
+            copy.wait_send()
+    for copy in done:
+        copy.wait_send()
+
+
+def ring_sum_start(parts, mid, near, sems, base):
+    here = parts.shape[0] // 4
+    half = here // 2
+    copies = []
+    for way, step in ((0, 1), (1, -1)):
+        copies.append(
+            remote(
+                parts.at[pl.ds(here + way * half, half)], mid.at[way], sems, base + way, at_y(step)
+            )
+        )
+    for way, step, block in ((0, 1, 2), (1, -1, 3)):
+        copies.append(
+            remote(
+                parts.at[pl.ds(block * here + (1 - way) * half, half)],
+                near.at[way],
+                sems,
+                base + 2 + way,
+                at_y(step),
+            )
+        )
+    for copy in copies:
+        copy.start()
+    return copies
+
+
+def ring_sum_middle(parts, started, mid, sent, far, sems, base):
+    here = parts.shape[0] // 4
+    half = here // 2
+    copies = []
+    for way, step, block in ((0, 1, 2), (1, -1, 3)):
+        started[way].wait_recv()
+        sent[way] = (
+            parts[pl.ds(block * here + way * half, half)].astype(f32) + mid[way].astype(f32)
+        ).astype(bf16)
+        copies.append(remote(sent.at[way], far.at[way], sems, base + 4 + way, at_y(step)))
+        copies[-1].start()
+    return copies
+
+
+def ring_sum_finish(parts, started, middle, far, near):
+    half = parts.shape[0] // 8
+
+    def finish(top):
+        started[2 + 1 - top].wait_recv()
+        middle[top].wait_recv()
+        return (
+            parts[pl.ds(top * half, half)].astype(f32)
+            + far[top].astype(f32)
+            + near[1 - top].astype(f32)
+        )
+
+    return finish
+
+
+def last_sum(grads, first_parts, mixed_parts, resid, unit, scale, gains, first_sum):
+    rows = grads.shape[0] // 64
+    wide = grads.shape[1]
+    here, width = resid.shape
+    full = pl.BlockSpec(memory_space=VMEM)
+    piece = rows // 2
+    return pl.pallas_call(
+        last_sum_kernel,
+        out_shape=(
+            jax.ShapeDtypeStruct((2, rows, wide), bf16),
+            jax.ShapeDtypeStruct((here, width), f32),
+            jax.ShapeDtypeStruct((here, width), bf16),
+        ),
+        in_specs=[full] * 8,
+        out_specs=(full,) * 3,
+        scratch_shapes=[
+            VMEM((4, 4, 2 * rows, wide), bf16),
+            VMEM((2, 2, 4, piece, wide), bf16),
+            VMEM((2, 2, 4, piece, wide), bf16),
+            VMEM((2, 2, 4, piece, wide), bf16),
+            VMEM((2, 2, 4, piece, wide), bf16),
+            VMEM((2, 4, rows, wide), bf16),
+            VMEM((2, 2, piece, wide), bf16),
+            VMEM((2, 2, piece, wide), bf16),
+            VMEM((2, 2, piece, wide), bf16),
+            VMEM((2, 2, piece, wide), bf16),
+            VMEM((2, rows, wide), bf16),
+            VMEM((2, 2, here // 2, width), bf16),
+            VMEM((2, 2, here // 2, width), bf16),
+            VMEM((2, 2, here // 2, width), bf16),
+            VMEM((2, 2, here // 2, width), bf16),
+            DMA((16,)), DMA((16,)), DMA((12,)), DMA((12,)), DMA((12,)), DMA((12,)),
+            DMA((2,)), DMA((2,)), DMA, DMA((12,)), DMA((12,)),
+        ],
+        compiler_params=pltpu.CompilerParams(
+            collective_id=3, has_side_effects=True, vmem_limit_bytes=VMEM_LIMIT
+        ),
+    )(grads, first_parts, mixed_parts, resid, unit, scale, gains, first_sum)
 
 
 def mm(a, b, ca, cb):
     return lax.dot_general(a, b, (((ca,), (cb,)), ((), ())), preferred_element_type=f32)
-
-
-def to_quarters(quarters):
-    yl, c = lax.axis_index("yl"), lax.axis_index("c")
-    one = lax.ppermute(lax.dynamic_index_in_dim(quarters, c, 0, False), PAIR, SAME)
-    two = lax.ppermute(lax.dynamic_index_in_dim(quarters, 1 - c, 0, False), PAIR, CROSS)
-    low = jnp.where(yl == 0, one, two)
-    high = jnp.where(yl == 0, two, one)
-    return jnp.concatenate([low, high], axis=0)
 
 
 def from_quarters(rows):
@@ -53,38 +724,11 @@
     return jnp.stack([jnp.where(c == 0, one, two), jnp.where(c == 0, two, one)])
 
 
-def gather_ring(block):
-    got = [block]
-    for k in (2, 1, 3):
-        got.append(lax.ppermute(block, RING, turn(-k)))
-    return jnp.concatenate(got, axis=0)
-
-
-def sum_ring(parts):
-    blocks = parts.reshape(4, -1, parts.shape[1])
-    total = blocks[0]
-    low = blocks.astype(bf16)
-    for place, k in ((1, 2), (2, 1), (3, 3)):
-        total = total + lax.ppermute(
-            low[place], RING, turn(k)
-        ).astype(f32)
-    return total
-
-
 def unit_of(values):
     centered = values - jnp.mean(values, -1, keepdims=True)
     variance = jnp.mean(centered * centered, -1, keepdims=True)
     inverse = lax.rsqrt(variance + EPSILON)
     return centered * inverse, inverse
-
-
-def normalize_back(incoming, unit_rows, inverse, gain):
-    grad_unit = incoming * gain
-    return inverse * (
-        grad_unit
-        - jnp.mean(grad_unit, -1, keepdims=True)
-        - unit_rows * jnp.mean(grad_unit * unit_rows, -1, keepdims=True)
-    )
 
 
 def rotate(values, cosine, sine):
@@ -124,9 +768,12 @@
     extra = jnp.pad(jnp.concatenate([norm_high, norm_low], 1), ((0, 0), (0, EXTRA - 8)))
     extra_q = bias_q + extra[None]
 
-    first = to_quarters(jnp.concatenate([qkv_q, out_q, extra_q], axis=2))
-    second = to_quarters(jnp.concatenate([gu_q, down_q], axis=2))
-    first = lax.all_gather(first, SPREAD, axis=0, tiled=True)
+    first, second, token_rows, cot_rows = first_gather(
+        jnp.concatenate([qkv_q, out_q, extra_q], axis=2),
+        jnp.concatenate([gu_q, down_q], axis=2),
+        tokens,
+        cotangent,
+    )
     second = lax.all_gather(second, SPREAD, axis=0, tiled=True)
     w_qkv, w_out = first[:, : 3 * hq], first[:, 3 * hq : 4 * hq]
     extras = first[:, 4 * hq :]
@@ -135,9 +782,7 @@
     norm_table = (extras[:, :4].astype(f32) + extras[:, 4:8].astype(f32)).T
     bias = extras.reshape(HEAD_DIM, rows, EXTRA)[:, 0, 8 : 8 + 3 * heads].T.reshape(3 * hq)
 
-    token_rows = gather_ring(tokens).astype(f32)
-    cot_rows = gather_ring(cotangent)
-    unit_rows, inverse_rows = unit_of(token_rows)
+    unit_rows, inverse_rows = unit_of(token_rows.astype(f32))
     unit_one, scale_one = unit_rows[:here], inverse_rows[:here]
     normed_one = (unit_rows * norm_table[0] + norm_table[1]).astype(bf16)
     projected = mm(normed_one, w_qkv, 1, 0) + bias.astype(f32)
@@ -160,31 +805,38 @@
     soft_low = soft.astype(bf16)
     head_mix = jnp.einsum("bhst,bthd->bshd", soft_low, value_heads, preferred_element_type=f32)
     head_mix = head_mix.reshape(2 * length, hq).astype(bf16)
-    first_sum = tokens.astype(f32) + sum_ring(mm(head_mix, w_out, 1, 1))
-
-    unit_two, scale_two = unit_of(first_sum)
-    normed_two = gather_ring((unit_two * norm_table[2] + norm_table[3]).astype(bf16))
+
+    first_sum, unit_two, scale_two, normed_two = second_norm(
+        mm(head_mix, w_out, 1, 1).astype(bf16), tokens, norm_table[2:]
+    )
     gate_up = mm(normed_two, w_gu, 1, 0)
     gate_pre, up_pre = gate_up[:, :fq], gate_up[:, fq:]
     sigmoid = jax.nn.sigmoid(gate_pre)
     activated = gate_pre * sigmoid
     hidden = (activated * up_pre).astype(bf16)
     grad_down = mm(cot_rows, hidden, 0, 0).astype(bf16)
-    down_sums = lax.psum_scatter(grad_down, SPREAD, scatter_dimension=0, tiled=True)
-    mixed = (first_sum + sum_ring(mm(hidden, w_down, 1, 1))).astype(bf16)
+    mixed_parts = mm(hidden, w_down, 1, 1).astype(bf16)
     grad_hidden = mm(cot_rows, w_down, 1, 0)
     grad_gate = grad_hidden * up_pre * sigmoid * (1.0 + gate_pre * (1.0 - sigmoid))
     grad_pair = jnp.concatenate([grad_gate, grad_hidden * activated], 1).astype(bf16)
     grad_gu = mm(normed_two, grad_pair, 0, 0).astype(bf16)
-    gu_sums = lax.psum_scatter(grad_gu, SPREAD, scatter_dimension=0, tiled=True)
-    grad_second = sum_ring(mm(grad_pair, w_gu, 1, 1))
-    grad_resid = cotangent.astype(f32) + normalize_back(
-        grad_second, unit_two, scale_two, norm_table[2]
-    )
-    gain_two = jnp.sum(grad_second * unit_two, 0)
-    shift_two = jnp.sum(grad_second, 0)
-
-    resid_rows = gather_ring(grad_resid.astype(bf16))
+    second_cores = jnp.concatenate([grad_gu, grad_down], 1).reshape(16, 2, 2 * rows, 3 * fq)
+    core = lax.axis_index("c")
+    arriving = lax.ppermute(
+        lax.dynamic_index_in_dim(second_cores, 1 - core, 1, False), "c", [(0, 1), (1, 0)]
+    )
+    second_parts = mm(grad_pair, w_gu, 1, 1).astype(bf16)
+    second_chip = (
+        lax.dynamic_index_in_dim(second_cores, core, 1, False).astype(f32) + arriving.astype(f32)
+    ).astype(bf16)
+    second_parts, second_chip = lax.optimization_barrier((second_parts, second_chip))
+    second_sums = lax.psum_scatter(
+        second_chip.reshape(width // 2, 3 * fq), ("z", "x"), scatter_dimension=0, tiled=True
+    )
+    grad_resid, second_terms, resid_rows = second_norm_back(
+        second_parts, cotangent, unit_two, scale_two, norm_table[2:]
+    )
+
     grad_mix = mm(resid_rows, w_out, 1, 0).astype(bf16).reshape(2, length, heads, HEAD_DIM)
     grad_out = mm(resid_rows, head_mix, 0, 0).astype(bf16)
     grad_soft = jnp.einsum("bshd,bthd->bhst", grad_mix, value_heads, preferred_element_type=f32)
@@ -210,19 +862,24 @@
     gain_one = jnp.sum(first_parts * unit_rows, 0)
     shift_one = jnp.sum(first_parts, 0)
     grad_bias = jnp.sum(grad_proj.astype(f32), 0).reshape(3 * heads, HEAD_DIM).T
-    norm_terms = jnp.stack([gain_one, shift_one, gain_two, shift_two], 1)
+    norm_terms = jnp.concatenate([jnp.stack([gain_one, shift_one]), second_terms], 0).T
     grad_extra = jnp.pad(norm_terms, ((0, 0), (0, EXTRA - 4))) + jnp.pad(
         grad_bias[:, None, :], ((0, 0), (0, rows - 1), (8, EXTRA - 8 - 3 * heads))
     ).reshape(width, EXTRA)
     grad_first = jnp.concatenate([grad_qkv, grad_out, grad_extra.astype(bf16)], 1)
-    first_sums = lax.psum_scatter(grad_first, SPREAD, scatter_dimension=0, tiled=True)
-    grad_input = grad_resid + normalize_back(
-        sum_ring(first_parts), unit_one, scale_one, norm_table[0]
-    )
-
-    down_back = from_quarters(down_sums)
-    gu_back = from_quarters(gu_sums)
-    first_back = from_quarters(first_sums)
+    first_back, grad_input, mixed = last_sum(
+        grad_first,
+        first_parts.astype(bf16),
+        mixed_parts,
+        grad_resid,
+        unit_one,
+        scale_one,
+        norm_table[:2],
+        first_sum,
+    )
+
+    second_back = from_quarters(second_sums)
+    gu_back, down_back = second_back[:, :, : 2 * fq], second_back[:, :, 2 * fq :]
     out_down = down_back.transpose(0, 2, 1).reshape(2 * fq, rows).astype(f32)
     out_gu = (
         gu_back.reshape(2, rows, 2, fq).transpose(2, 1, 0, 3).reshape(2, rows, 2 * fq).astype(f32)

time: 618 us -> 436 us (0.71)
  waiting for transfers between devices: 341 us -> 5.04 us
  Pallas kernels: 0 us -> 199 us
  starting transfers between devices: 54.8 us -> 6.7 us
  local copies, waits for them, and re-layouts: 65 us -> 71.5 us
    pallas_call x0 -> x4, Pallas kernels: none -> 199 us  [the longest x1 55.6 us: first_gather(): pl.pallas_call(first_gather_kernel, out_shape=(jax.ShapeDtypeStruct((64 *...]
    reduce_scatter x3 -> x1, waiting for transfers between devices: 163 us -> 0.01 us  [shards(): lax.psum_scatter(second_chip.reshape(width // 2, 3 * fq), ('z', 'x'), sca...]
    ppermute x28 -> x1, waiting for transfers between devices: 158 us -> 2.45 us  [shards(): lax.ppermute(lax.dynamic_index_in_dim(second_cores, 1 - core, 1, False),...]
    ppermute x28 -> x1, starting transfers between devices: 40.2 us -> 0.01 us  [shards(): lax.ppermute(lax.dynamic_index_in_dim(second_cores, 1 - core, 1, False),...]
    all_gather x1 -> x0, waiting for transfers between devices: 14.8 us -> none  [shards(): first = lax.all_gather(first, SPREAD, axis=0, tiled=True)]
    pallas_call x0 -> x1, local copies, waits for them, and re-layouts: none -> 13 us  [first_gather(): pl.pallas_call(first_gather_kernel, out_shape=(jax.ShapeDtypeStruct((64 *...]
    unnamed x128 -> x79, local copies, waits for them, and re-layouts: 24.2 us -> 11.5 us
    concatenate x3 -> x4, other arithmetic: 1.6 us -> 8.46 us  [the longest x1 6.86 us: shards(): jnp.concatenate([grad_gu, grad_down], 1).reshape(16, 2, 2 * rows, 3 * fq)]
  transfers between devices with their start and end apart: 41 -> 7, of which waited for: 22 -> 2; matrix products, arithmetic and copies ran while one was open for 24% -> 33% of each run, Pallas kernels for 0% -> 34%
where the time goes in v2:
time: 436 us; the launch traced here: 428 us
  Pallas kernels  199 us (46%)
  matrix products  99.2 us (23%)
  local copies, waits for them, and re-layouts  71.5 us (16%)
  other arithmetic  30.7 us (7%)
  between operations  15.2 us (3%)
  starting transfers between devices  6.7 us (2%)
  waiting for transfers between devices  5.04 us (1%)
    dot_general x12, matrix products, mm(): lax.dot_general(a, b, (((ca,), (cb,)), ((), ())), preferred_element_type=...  85.8 us
    pallas_call x1, Pallas kernels, first_gather(): pl.pallas_call(first_gather_kernel, out_shape=(jax.ShapeDtypeStruct((64 *...  55.6 us
    pallas_call x1, Pallas kernels, last_sum(): pl.pallas_call(last_sum_kernel, out_shape=(jax.ShapeDtypeStruct((2, rows,...  54.3 us
    pallas_call x1, Pallas kernels, second_norm(): pl.pallas_call(second_norm_kernel, out_shape=(jax.ShapeDtypeStruct((here,...  45.4 us
    pallas_call x1, Pallas kernels, second_norm_back(): pl.pallas_call(second_norm_back_kernel, out_shape=(jax.ShapeDtypeStruct((...  44.1 us
    pallas_call x1, local copies, waits for them, and re-layouts, first_gather(): pl.pallas_call(first_gather_kernel, out_shape=(jax.ShapeDtypeStruct((64 *...  13 us
    unnamed x79, local copies, waits for them, and re-layouts  11.5 us
  transfers between devices with their start and end apart: 7, of which 2 were waited for; matrix products, arithmetic and copies ran while one was open for 33% of the time, Pallas kernels for 34%

profile of v2, /device:TPU:0, one launch (start us, length us, event | category | flops | bytes accessed | tf_op | source)
XLA Modules:
  0.0 427.6 jit_solution(14352830273115699343)
XLA Ops:
  7.2 3.4 collective-permute-start
  10.6 0.8 reshape.251
  11.4 0.8 copy.195
  12.3 0.9 copy.194
  13.2 1.1 reshape.248
  14.3 1.1 reshape.253
  16.0 0.8 pad_maximum_fusion.5.two_q
  17.7 0.7 pad_maximum_fusion.10.one_q
  18.4 55.6 %shard_map.143 = (bf16[2048,2176]{1,0:T(8,128)(2,1)}, bf16[64,4224]{1,0:T(8,128)(2,1)}, bf16[512,2048]{1,0:T(8,128)(2,1)}, bf16[512,2048]{1,0:T(8,128)(2,1)}) custom-call(bf16[2,32,2176]{2,1,0:T(8,128)(2,1)} %pad_maximum_fusion.10.one_q, bf16[2,32,4224]{2,1,0:T(8,128)(2,1)} %pad_maximum_fusion.5.two_q, bf16[128,2048]{1,0:T(8,128)(2,1)} %tokens.3, ...), custom_call_target="tpu_custom_call" | custom-call | tf_op jit(solution)/shard_map/pallas_call | solution.py:414
  74.5 0.8 fusion.53
  75.3 0.8 broadcast_compare_fusion
  76.1 1.1 slice.133
  77.1 13.0 %copy.128 = bf16[2048,2176]{0,1:T(8,128)(2,1)} copy(bf16[2048,2176]{1,0:T(8,128)(2,1)} %get-tuple-element.25) | data formatting | bytes 17825792 | tf_op jit(solution)/shard_map/pallas_call | solution.py:414
  91.5 0.8 add_bitcast_fusion
  93.0 8.1 %fusion.17 = f32[512,1536]{1,0:T(8,128)} fusion(bf16[2048,2176]{1,0:T(8,128)(2,1)} %get-tuple-element.25, f32[1536]{0:T(1024)S(1)} %reshape.269, f32[2048]{0:T(1024)S(1)} %bitcast.189, f32[2048]{0:T(1024)S(1)} %bitcast.187, bf16[512,2048]{1,0:T(8,128)(2,1)S(1)} %copy-done.1, f32[512]{0:T(512)S(1)} %add_rsqrt_fusion, f32[512]{0:T(512)S(1)} %broadcast_multiply_fusion), kind=kOutput, calls=%fused_computation.32 | convolution fusion | flops 3228303360 | bytes 11560960 | tf_op jit(solution)/shard_map/dot_general | solution.py:712
  101.1 5.5 %reshape.280 = f32[2,256,3,8,64]{4,3,2,1,0:T(8,128)} reshape(f32[512,1536]{1,0:T(8,128)} %fusion.17) | data formatting | bytes 6291456 | tf_op jit(solution)/shard_map/reshape | solution.py:794
  106.6 2.4 slice.182
  108.9 1.4 copy.175
  110.3 4.5 %fusion.64 = (f32[2,256,1,8,64]{4,3,2,1,0:T(8,128)}, f32[2,256,1,8,64]{4,3,2,1,0:T(8,128)}) fusion(f32[2,256,3,8,64]{4,3,2,1,0:T(8,128)} %reshape.280), kind=kLoop, calls=%fused_computation.142 | loop fusion | bytes 4194304 | tf_op jit(solution)/shard_map/slice | solution.py:796
  114.9 2.2 copy.173
  117.1 0.8 slice.272
  117.8 3.1 copy.174
  121.0 1.2 slice.271
  122.2 1.7 subtract_convert_fusion.3
  123.9 5.4 %fusion.67 = (f32[2,8,256]{2,1,0:T(8,128)}, f32[2,8,256,256]{2,3,1,0:T(8,128)}) fusion(pred[2,256,256]{1,2,0:T(8,128)(4,1)} %broadcast_compare_fusion, bf16[2,256,8,48]{1,3,2,0:T(8,128)(2,1)S(1)} %slice.271, bf16[2,256,8,8]{1,3,2,0:T(8,128)(2,1)} %get-tuple-element.99, bf16[2,256,8,8]{1,3,2,0:T(8,128)(2,1)} %get-tuple-element.100, ...), kind=kOutput, calls=%fused_computation.145 | convolution fusion | flops 141558016 | bytes 5390336 | tf_op jit(solution)/shard_map/sub | solution.py:803
  129.3 2.7 fusion.39
  132.6 4.4 %convolution_convert_fusion.4.parts = bf16[512,2048]{1,0:T(8,128)(2,1)} fusion(bf16[512,512]{0,1:T(8,128)(2,1)S(1)} %bitcast.176, bf16[2048,2176]{1,0:T(8,128)(2,1)} %get-tuple-element.25), kind=kOutput, calls=%fused_computation.37 | convolution fusion | flops 1074790400 | bytes 4718592 | tf_op jit(solution)/shard_map/dot_general | solution.py:712
  137.7 45.4 %shard_map.144 = (f32[128,2048]{1,0:T(8,128)}, f32[128,2048]{1,0:T(8,128)}, f32[128,1]{1,0:T(8,128)}, bf16[512,2048]{1,0:T(8,128)(2,1)}) custom-call(bf16[512,2048]{1,0:T(8,128)(2,1)} %convolution_convert_fusion.4.parts, bf16[128,2048]{1,0:T(8,128)(2,1)} %tokens.3, f32[2,2048]{1,0:T(2,128)} %get-tuple-element.96.gains), custom_call_target="tpu_custom_call" | custom-call | tf_op jit(solution)/shard_map/pallas_call | solution.py:142
  183.1 10.5 %fusion.4 = f32[512,2816]{1,0:T(8,128)S(1)} fusion(bf16[512,2048]{1,0:T(8,128)(2,1)} %get-tuple-element.28, bf16[2048,4224]{1,0:T(8,128)(2,1)} %all-gather.2.cloned.1.call-done), kind=kOutput, calls=%fused_computation.7 | convolution fusion | flops 5905580032 | bytes 19398656 | tf_op jit(solution)/shard_map/dot_general | solution.py:712
  193.6 8.5 %multiply_convert_fusion.3 = (bf16[512,1408]{1,0:T(8,128)(2,1)}, bf16[512,1408]{1,0:T(8,128)(2,1)}, bf16[512,1408]{1,0:T(8,128)(2,1)S(1)}) fusion(f32[512,2816]{1,0:T(8,128)S(1)} %fusion.4, bf16[512,2048]{1,0:T(8,128)(2,1)S(1)} %copy-done.30, bf16[2048,4224]{1,0:T(8,128)(2,1)} %all-gather.2.cloned.1.call-done), kind=kOutput, calls=%fused_computation.42 | convolution fusion | flops 2963603456 | bytes 17956864 | tf_op jit(solution)/shard_map/dot_general | solution.py:712
  202.2 3.7 convolution_convert_fusion.2
  205.9 8.6 %convolution_convert_fusion = bf16[2048,2816]{1,0:T(8,128)(2,1)S(1)} fusion(bf16[512,2048]{1,0:T(8,128)(2,1)} %get-tuple-element.28, bf16[512,1408]{1,0:T(8,128)(2,1)} %get-tuple-element.77, bf16[512,1408]{1,0:T(8,128)(2,1)} %get-tuple-element.76), kind=kOutput, calls=%fused_computation.4 | convolution fusion | flops 5917114368 | bytes 16515072 | tf_op jit(solution)/shard_map/dot_general | solution.py:712
  214.5 6.9 %pad_maximum_fusion = bf16[2048,4224]{1,0:T(8,128)(2,1)} fusion(bf16[2048,1408]{1,0:T(8,128)(2,1)S(1)} %convolution_convert_fusion.2, bf16[2048,2816]{1,0:T(8,128)(2,1)S(1)} %convolution_convert_fusion), kind=kLoop, calls=%fused_computation.1 | loop fusion | flops 34603008 | bytes 34603008 | tf_op jit(solution)/shard_map/concatenate | solution.py:823
  221.4 7.4 %dynamic-slice_bitcast_fusion = bf16[16,64,4224]{2,1,0:T(8,128)(2,1)} fusion(bf16[16,2,64,4224]{3,2,1,0:T(8,128)(2,1)} %bitcast.154, s32[]{:T(128)S(6)} %select_n.89), kind=kLoop, calls=%fused_computation.10 | loop fusion | bytes 17301508 | tf_op jit(solution)/shard_map/jit(dynamic_index_in_dim)/squeeze | solution.py:826
  228.8 11.4 %fusion.21.parts = bf16[512,2048]{1,0:T(8,128)(2,1)} fusion(bf16[2048,4224]{1,0:T(8,128)(2,1)} %all-gather.2.cloned.1.call-done, bf16[512,1408]{1,0:T(8,128)(2,1)} %get-tuple-element.77, bf16[512,1408]{1,0:T(8,128)(2,1)} %get-tuple-element.76), kind=kOutput, calls=%fused_computation.35 | convolution fusion | flops 5912395776 | bytes 16515072 | tf_op jit(solution)/shard_map/dot_general | solution.py:712
  240.2 2.5 collective-permute-done.1
  242.7 8.1 %fusion.1 = bf16[16,64,4224]{2,1,0:T(8,128)(2,1)} fusion(bf16[16,64,4224]{2,1,0:T(8,128)(2,1)} %collective-permute-done.1, bf16[16,2,64,4224]{3,2,1,0:T(8,128)(2,1)S(1)} %bitcast.155, s32[]{:T(128)S(6)} %select_n.88), kind=kLoop, calls=%fused_computation.3 | loop fusion | flops 17301504 | bytes 25952260 | tf_op jit(solution)/shard_map/convert_element_type | solution.py:831
  251.5 0.7 copy.151.scale
  252.2 7.8 %fusion.24.mixed_parts = bf16[512,2048]{1,0:T(8,128)(2,1)} fusion(bf16[512,1408]{1,0:T(8,128)(2,1)} %copy-done.31, bf16[2048,4224]{1,0:T(8,128)(2,1)} %all-gather.2.cloned.1.call-done), kind=kOutput, calls=%fused_computation.38 | convolution fusion | flops 2953838592 | bytes 9306112 | tf_op jit(solution)/shard_map/dot_general | solution.py:712
  260.0 44.1 %shard_map.145 = (f32[128,2048]{1,0:T(8,128)}, f32[2,2048]{1,0:T(2,128)}, bf16[512,2048]{1,0:T(8,128)(2,1)}) custom-call(bf16[512,2048]{1,0:T(8,128)(2,1)} %fusion.21.parts, bf16[128,2048]{1,0:T(8,128)(2,1)} %cotangent.3, f32[128,2048]{1,0:T(8,128)} %get-tuple-element.30.unit, f32[128,1]{1,0:T(8,128)} %get-tuple-element.31.scale, ...), custom_call_target="tpu_custom_call" | custom-call | tf_op jit(solution)/shard_map/pallas_call | solution.py:199
  304.1 4.3 %fusion.36 = bf16[512,512]{1,0:T(8,128)(2,1)} fusion(bf16[512,2048]{1,0:T(8,128)(2,1)} %get-tuple-element.32, bf16[2048,2176]{1,0:T(8,128)(2,1)} %get-tuple-element.25), kind=kOutput, calls=%fused_computation.56 | convolution fusion | flops 1074003968 | bytes 4718592 | tf_op jit(solution)/shard_map/dot_general | solution.py:712
  308.5 1.8 reshape.281
  310.3 1.4 copy.139
  311.7 3.2 fusion.40
  315.6 0.8 multiply_reduce_fusion.1
  316.5 0.9 multiply_convert_fusion
  318.3 0.8 fusion.34
  320.8 1.2 copy-done.3
  322.4 10.1 %multiply_reduce_fusion = (f32[2048]{0:T(1024)S(1)}, f32[2048]{0:T(1024)S(1)}, bf16[512,2048]{1,0:T(8,128)(2,1)}, f32[512,2048]{1,0:T(8,128)}) fusion(f32[512]{0:T(512)S(1)} %copy-done.29, f32[512]{0:T(512)S(1)} %copy-done.27, bf16[512,2048]{1,0:T(8,128)(2,1)S(1)} %copy-done.1, bf16[512,1536]{0,1:T(8,128)(2,1)} %copy-done.3, ...), kind=kOutput, calls=%fused_computation.26 | convolution fusion | flops 3228561408 | bytes 16273408 | tf_op jit(solution)/shard_map/dot_general | solution.py:712
  333.0 2.3 slice.193.unit
  335.5 3.1 convolution_convert_fusion.3
  338.8 5.2 %convolution_convert_fusion.1 = bf16[2048,1536]{1,0:T(8,128)(2,1)S(1)} fusion(bf16[512,1536]{0,1:T(8,128)(2,1)S(1)} %copy-done.4, f32[2048]{0:T(1024)S(1)} %bitcast.190, f32[2048]{0:T(1024)S(1)} %bitcast.188, bf16[512,2048]{1,0:T(8,128)(2,1)S(1)} %copy-done.1, f32[512]{0:T(512)S(1)} %copy-done.29, f32[512]{0:T(512)S(1)} %copy-done.27), kind=kOutput, calls=%fused_computation.11 | convolution fusion | flops 3230662656 | bytes 9981952 | tf_op jit(solution)/shard_map/dot_general | solution.py:712
  344.0 3.8 pad_maximum_fusion.1.grads
  347.8 54.3 %shard_map.146 = (bf16[2,32,2176]{2,1,0:T(8,128)(2,1)}, f32[128,2048]{1,0:T(8,128)}, bf16[128,2048]{1,0:T(8,128)(2,1)}) custom-call(bf16[2048,2176]{1,0:T(8,128)(2,1)} %pad_maximum_fusion.1.grads, bf16[512,2048]{1,0:T(8,128)(2,1)} %get-tuple-element.81.first_parts, bf16[512,2048]{1,0:T(8,128)(2,1)} %fusion.24.mixed_parts, ...), custom_call_target="tpu_custom_call" | custom-call | tf_op jit(solution)/shard_map/pallas_call | solution.py:677
  403.8 2.5 collective-permute-start.2
  406.3 0.8 convert_bitcast_fusion.1
  407.8 1.1 dynamic-slice_bitcast_fusion.1
  409.7 1.0 slice_convert_fusion.4
  411.2 1.1 reshape.271
  412.9 2.5 collective-permute-done.4
  415.6 0.8 copy.179
  417.3 1.4 reshape.273
  418.8 0.8 copy.200
  419.6 1.0 copy.201
  (146 shorter events, 15.6 us)
Async XLA Ops:
  7.2 10.1 %copy-start.25 = (f32[4,16]{1,0:T(4,128)S(1)}, f32[4,16]{1,0:T(4,128)}, u32[]{:S(2)}) copy-start(f32[4,16]{1,0:T(4,128)} %param.10) | copy-start | bytes 772
  7.2 175.9 %all-gather.2.cloned.1.call-start = ((), (), s32[]{:S(2)}) async-start(), calls=%async_computation.1 | async-start | bytes 17842176 | tf_op jit(solution)/shard_map/all_gather | solution.py:777
  7.2 10.1 %collective-permute-start = (f32[4,16]{1,0:T(4,128)}, f32[4,16]{1,0:T(4,128)S(1)}, u32[]{:S(2)}, u32[]{:S(2)}) collective-permute-start(f32[4,16]{1,0:T(4,128)} %param.10), channel_id=1, source_target_pairs={{0,1},{1,0},{2,3},{3,2},{4,5},{5,4},{6,7},{7,6},{8,9},{9,8},{10,11... | collective-permute-start | bytes 776 | tf_op jit(solution)/shard_map/ppermute | solution.py:758
  74.0 333.8 %reduce-scatter.2.cloned.1.call-start = ((), (), s32[]{:S(2)}) async-start(), calls=%async_computation.2 | async-start | bytes 9191424 | tf_op jit(solution)/shard_map/reduce_scatter | solution.py:833
  77.1 13.2 %copy-start.1 = (bf16[512,2048]{1,0:T(8,128)(2,1)S(1)}, bf16[512,2048]{1,0:T(8,128)(2,1)}, u32[]{:S(2)}) copy-start(bf16[512,2048]{1,0:T(8,128)(2,1)} %get-tuple-element.24) | copy-start | bytes 6291460
  90.8 10.3 %copy-start.26 = (f32[512]{0:T(512)}, f32[512]{0:T(512)S(1)}, u32[]{:S(2)}) copy-start(f32[512]{0:T(512)S(1)} %broadcast_multiply_fusion) | copy-start | bytes 6148
  91.5 9.6 %copy-start.28 = (f32[512]{0:T(512)}, f32[512]{0:T(512)S(1)}, u32[]{:S(2)}) copy-start(f32[512]{0:T(512)S(1)} %add_rsqrt_fusion) | copy-start | bytes 6148
  92.3 0.6 copy-start.16
  93.0 8.1 %copy-start.21 = (f32[1,2048]{1,0:T(1,128)}, f32[1,2048]{1,0:T(1,128)S(1)}, u32[]{:S(2)}) copy-start(f32[1,2048]{1,0:T(1,128)S(1)} %get-tuple-element.101) | copy-start | bytes 24580
  93.0 8.1 %copy-start.23 = (f32[1,2048]{1,0:T(1,128)}, f32[1,2048]{1,0:T(1,128)S(1)}, u32[]{:S(2)}) copy-start(f32[1,2048]{1,0:T(1,128)S(1)} %get-tuple-element.102) | copy-start | bytes 24580
  123.9 5.4 %copy-start.7 = (bf16[2,256,1,8,64]{1,4,3,0,2:T(8,128)(2,1)S(1)}, bf16[2,256,1,8,64]{1,4,3,0,2:T(8,128)(2,1)}, u32[]{:S(2)}) copy-start(bf16[2,256,1,8,64]{1,4,3,0,2:T(8,128)(2,1)} %copy.175) | copy-start | bytes 1572868
  132.6 4.5 %copy-start.10 = (bf16[64,8,2,256]{3,1,2,0:T(8,128)(2,1)}, bf16[64,8,2,256]{3,1,2,0:T(8,128)(2,1)S(1)}, u32[]{:S(2)}) copy-start(bf16[64,8,2,256]{3,1,2,0:T(8,128)(2,1)S(1)} %copy.181) | copy-start | bytes 1572868
  132.6 4.5 %copy-start.17 = (f32[4,2048]{1,0:T(4,128)S(1)}, f32[4,2048]{1,0:T(4,128)}, u32[]{:S(2)}) copy-start(f32[4,2048]{1,0:T(4,128)} %copy-done.16) | copy-start | bytes 98308
  183.1 10.5 %copy-start.30 = (bf16[512,2048]{1,0:T(8,128)(2,1)S(1)}, bf16[512,2048]{1,0:T(8,128)(2,1)}, u32[]{:S(2)}) copy-start(bf16[512,2048]{1,0:T(8,128)(2,1)} %get-tuple-element.26) | copy-start | bytes 6291460
  202.2 3.8 copy-start.31
  228.8 13.9 %collective-permute-start.1 = (bf16[16,64,4224]{2,1,0:T(8,128)(2,1)}, bf16[16,64,4224]{2,1,0:T(8,128)(2,1)}, u32[]{:S(2)}, u32[]{:S(2)}) collective-permute-start(bf16[16,64,4224]{2,1,0:T(8,128)(2,1)} %dynamic-slice_bitcast_fusion), channel_id=1, source_target_pairs={{0,2},{2,0},{1,3},{3,1},{4,6},{6,4},{5,7},{7,5},{8,10},{10,8},{9,1... | collective-permute-start | bytes 25952264 | tf_op jit(solution)/shard_map/ppermute | solution.py:825
  228.8 13.9 %copy-start = (bf16[2048,4224]{1,0:T(8,128)(2,1)S(1)}, bf16[2048,4224]{1,0:T(8,128)(2,1)}, u32[]{:S(2)}) copy-start(bf16[2048,4224]{1,0:T(8,128)(2,1)} %pad_maximum_fusion) | copy-start | bytes 51904516
  311.7 3.9 copy-start.2
  311.7 3.9 copy-start.8
  311.7 3.9 copy-start.9
  311.7 3.9 copy-start.19
  316.4 1.0 copy-start.5
  316.5 1.0 copy-start.14
  316.5 1.0 copy-start.15
  317.5 0.8 copy-start.12
  317.5 0.9 copy-start.13
  317.5 1.7 copy-start.18
  319.9 2.5 copy-start.27
  319.9 2.5 copy-start.29
  320.8 1.2 copy-start.3
  322.4 10.2 %copy-start.20 = (f32[2,2048]{1,0:T(2,128)S(1)}, f32[2,2048]{1,0:T(2,128)}, u32[]{:S(2)}) copy-start(f32[2,2048]{1,0:T(2,128)} %get-tuple-element.33) | copy-start | bytes 49156
  335.5 3.3 copy-start.4
  335.5 3.3 copy-start.22
  335.5 3.3 copy-start.24
  403.8 8.5 %collective-permute-start.2 = (f32[4,16]{1,0:T(4,128)S(1)}, f32[4,16]{1,0:T(4,128)S(1)}, u32[]{:S(2)}, u32[]{:S(2)}) collective-permute-start(f32[4,16]{1,0:T(4,128)S(1)} %bitcast.194), channel_id=1, source_target_pairs={{0,1},{1,0},{2,3},{3,2},{4,5},{5,4},{6,7},{7,6},{8,9},{9,8},{10,11... | collective-permute-start | bytes 776 | tf_op jit(solution)/shard_map/ppermute | solution.py:907
  408.9 6.5 %collective-permute-start.4 = (bf16[32,4224]{1,0:T(8,128)(2,1)S(1)}, bf16[32,4224]{1,0:T(8,128)(2,1)S(1)}, u32[]{:S(2)}, u32[]{:S(2)}) collective-permute-start(bf16[32,4224]{1,0:T(8,128)(2,1)S(1)} %get-tuple-element.93), channel_id=1, source_target_pairs={{4,0},{0,2},{6,4},{2,6},{5,1},{1,3},{7,5},{3,7},{12,8},{8,10},{14,... | collective-permute-start | bytes 811016 | tf_op jit(solution)/shard_map/ppermute | solution.py:721
  409.0 6.4 %collective-permute-start.3 = (bf16[32,4224]{1,0:T(8,128)(2,1)S(1)}, bf16[32,4224]{1,0:T(8,128)(2,1)S(1)}, u32[]{:S(2)}, u32[]{:S(2)}) collective-permute-start(bf16[32,4224]{1,0:T(8,128)(2,1)S(1)} %get-tuple-element.94), channel_id=1, source_target_pairs={{0,0},{4,2},{2,4},{6,6},{1,1},{5,3},{3,5},{7,7},{8,8},{12,10},{10,... | collective-permute-start | bytes 811016 | tf_op jit(solution)/shard_map/ppermute | solution.py:718
  412.3 6.5 %copy-start.11 = (bf16[128,2048]{1,0:T(8,128)(2,1)S(1)}, bf16[128,2048]{1,0:T(8,128)(2,1)}, u32[]{:S(2)}) copy-start(bf16[128,2048]{1,0:T(8,128)(2,1)} %get-tuple-element.124) | copy-start | bytes 1572868
  415.5 4.1 copy-start.6
Sparse Core Ops, SparseCore 0:
  74.2 72.4 all-gather.1
  250.9 83.6 reduce-scatter.1

commit v3 on v2

--- a/solution.py
+++ b/solution.py
@@ -2,6 +2,7 @@
 
 import jax
 import jax.numpy as jnp
+import numpy as np
 from jax import lax
 from jax.experimental import pallas as pl
 from jax.experimental.pallas import tpu as pltpu
@@ -15,16 +16,10 @@
 
 GRID = ("z", "x", "yl", "c", "yh")
 ROWS = ("z", "x", "yl", "c")
-SPREAD = ("z", "x", "c")
-PAIR = ("yl", "c")
 EXTRA = 128
-
-SAME = [(0, 0), (1, 2), (2, 1), (3, 3)]
-CROSS = [(0, 2), (1, 0), (2, 3), (3, 1)]
 
 bf16 = jnp.bfloat16
 f32 = jnp.float32
-
 
 MESH = pl.DeviceIdType.MESH
 VMEM = pltpu.VMEM
@@ -154,62 +149,6 @@
             collective_id=1, has_side_effects=True, vmem_limit_bytes=VMEM_LIMIT
         ),
     )(parts, tokens, gains)
-
-
-def second_norm_back_kernel(
-    parts, cotangent, unit, scale, gains, resid, sums, spread, mid, sent, far, near, send, recv
-):
-    sems = (send, recv)
-    greet([at_y(1), at_y(3)])
-    finish, copies = ring_sum(parts, mid, sent, far, near, sems)
-    half = cotangent.shape[0] // 2
-    halves = []
-    for top in range(2):
-        rows = pl.ds(top * half, half)
-        total = finish(top)
-        unit_rows = unit[rows]
-        incoming = total * gains[0:1]
-        result = cotangent[rows].astype(f32) + scale[rows] * (
-            incoming
-            - jnp.mean(incoming, -1, keepdims=True)
-            - unit_rows * jnp.mean(incoming * unit_rows, -1, keepdims=True)
-        )
-        resid[rows] = result
-        spread[rows] = result.astype(bf16)
-        halves.append(ring_gather_half(spread, top, sems, 6))
-        both = jnp.concatenate(
-            [
-                jnp.sum(total * unit_rows, 0, keepdims=True),
-                jnp.sum(total, 0, keepdims=True),
-            ],
-            0,
-        )
-        sums[...] = both if top == 0 else sums[...] + both
-    passed = ring_gather_pass(spread, halves, sems, 6)
-    for copy in passed + [halves[1][0], halves[0][1]]:
-        copy.wait_recv()
-    for copy in copies + halves[0] + halves[1] + passed:
-        copy.wait_send()
-
-
-def second_norm_back(parts, cotangent, unit, scale, gains):
-    here, width = cotangent.shape
-    half = here // 2
-    full = pl.BlockSpec(memory_space=VMEM)
-    return pl.pallas_call(
-        second_norm_back_kernel,
-        out_shape=(
-            jax.ShapeDtypeStruct((here, width), f32),
-            jax.ShapeDtypeStruct((2, width), f32),
-            jax.ShapeDtypeStruct((4 * here, width), bf16),
-        ),
-        in_specs=[full] * 5,
-        out_specs=(full,) * 3,
-        scratch_shapes=[VMEM((2, half, width), bf16)] * 4 + [DMA((12,)), DMA((12,))],
-        compiler_params=pltpu.CompilerParams(
-            collective_id=2, has_side_effects=True, vmem_limit_bytes=VMEM_LIMIT
-        ),
-    )(parts, cotangent, unit, scale, gains)
 
 
 def pair_moves():
@@ -432,7 +371,7 @@
 
 
 def last_sum_kernel(
-    grads, first_parts, mixed_parts, resid, unit, scale, gains, first_sum,
+    grads, first_parts, mixed_parts, resid, tokens, stats, gains, first_sum,
     result, grad_tokens, mixed,
     sib, mid, sent, far, near, stage, mid2, sent2, far2, near2, packed,
     ymid, ysent, yfar, ynear,
@@ -567,8 +506,9 @@
     for top in range(2):
         rng = pl.ds(top * here, here)
         incoming = finish(top) * gains[0:1]
-        unit_rows = unit[rng]
-        grad_tokens[rng] = resid[rng] + scale[rng] * (
+        inverse = stats[1, rng]
+        unit_rows = (tokens[rng].astype(f32) - stats[0, rng]) * inverse
+        grad_tokens[rng] = resid[rng] + inverse * (
             incoming
             - jnp.mean(incoming, -1, keepdims=True)
             - unit_rows * jnp.mean(incoming * unit_rows, -1, keepdims=True)
@@ -668,7 +608,7 @@
     return finish
 
 
-def last_sum(grads, first_parts, mixed_parts, resid, unit, scale, gains, first_sum):
+def last_sum(grads, first_parts, mixed_parts, resid, tokens, stats, gains, first_sum):
     rows = grads.shape[0] // 64
     wide = grads.shape[1]
     here, width = resid.shape
@@ -705,51 +645,479 @@
         compiler_params=pltpu.CompilerParams(
             collective_id=3, has_side_effects=True, vmem_limit_bytes=VMEM_LIMIT
         ),
-    )(grads, first_parts, mixed_parts, resid, unit, scale, gains, first_sum)
-
-
-def mm(a, b, ca, cb):
+    )(grads, first_parts, mixed_parts, resid, tokens, stats, gains, first_sum)
+
+
+def tables():
+    half = ROTARY // 2
+    position = np.arange(256, dtype=np.float32)
+    frequency = np.power(np.float32(10000.0), -np.arange(half, dtype=np.float32) * np.float32(2.0 / ROTARY))
+    angles = position[:, None] * frequency[None, :].astype(np.float32)
+    cosine, sine = np.cos(angles), np.sin(angles)
+    own = np.ones((256, 2, HEAD_DIM), np.float32)
+    up = np.zeros((256, 2, HEAD_DIM), np.float32)
+    down = np.zeros((256, 2, HEAD_DIM), np.float32)
+    for head in range(2):
+        own[:, head, :half] = cosine
+        own[:, head, half:ROTARY] = cosine
+        up[:, head, :half] = -sine
+        down[:, head, half:ROTARY] = sine
+    return np.concatenate([a.reshape(256, 128) for a in (own, up, down)], 1)
+
+
+def dot(a, b, ca, cb):
     return lax.dot_general(a, b, (((ca,), (cb,)), ((), ())), preferred_element_type=f32)
+
+
+def turn_heads(value, table, sign):
+    own, up, down = table[:, :128], table[:, 128:256], table[:, 256:]
+    return value * own + sign * (
+        pltpu.roll(value, 120, 1) * up + pltpu.roll(value, 8, 1) * down
+    )
+
+
+def half_of_place(place):
+    y = lax.axis_index("yh") * 2 + lax.axis_index("yl")
+    return ((y + (0, 2, 1, 3)[place]) % 4) // 2
+
+
+def causal_mask(sequence, here):
+    length = 2 * here
+    first = half_of_place(2 * sequence)
+
+    def position(dim):
+        index = lax.broadcasted_iota(jnp.int32, (length, length), dim)
+        return jnp.where(index < here, index + first * here, index - first * here)
+
+    return position(0) >= position(1)
+
+
+def soft_of(queries, keys, mask):
+    scores = dot(queries, keys, 1, 1) * SCALE
+    scores = jnp.where(mask, scores, -1000000000.0)
+    powers = jnp.exp(scores - jnp.max(scores, -1, keepdims=True))
+    return powers * (1.0 / jnp.sum(powers, -1, keepdims=True))
+
+
+def read_extras(one, first_column, norm_table, bias):
+    total = None
+    for group in range(one.shape[0] // 128):
+        block = one[pl.ds(group * 128, 128), pl.ds(first_column, 128)].astype(f32)
+        block = block[0:32] + block[32:64] + block[64:96] + block[96:128]
+        norm_table[:, pl.ds(group * 128, 128)] = block[12:16] + block[16:20]
+        total = block[0:12] if total is None else total + block[0:12]
+    bias[...] = total
+
+
+def attention_forward_kernel(token_rows, one, table, normed, stats, qkv, head_mix, parts, norm_table, bias):
+    here = token_rows.shape[0] // 4
+    hq = head_mix.shape[1]
+    read_extras(one, 4 * hq, norm_table, bias)
+
+    def norm_rows(k, _):
+        rng = pl.ds(pl.multiple_of(k * here, here), here)
+        values = token_rows[rng].astype(f32)
+        mean = jnp.mean(values, -1, keepdims=True)
+        centered = values - mean
+        inverse = lax.rsqrt(jnp.mean(centered * centered, -1, keepdims=True) + EPSILON)
+        stats[0, rng] = mean
+        stats[1, rng] = inverse
+        normed[rng] = (centered * inverse * norm_table[0:1] + norm_table[1:2]).astype(bf16)
+        return 0
+
+    lax.fori_loop(0, 4, norm_rows, 0)
+    wide = 256
+
+    def project(k, _):
+        cols = pl.ds(pl.multiple_of(k * wide, wide), wide)
+        value = dot(normed[...], one[:, cols], 1, 0)
+        shift = jnp.concatenate(
+            [bias[pl.ds(2 * k, 1)], bias[pl.ds(2 * k + 1, 1)]], 1
+        )
+        value = value + shift
+
+        @pl.when(k < 2 * hq // wide)
+        def _():
+            for place in range(4):
+                rng = pl.ds(place * here, here)
+                turn = table[pl.ds(pl.multiple_of(half_of_place(place) * here, here), here)]
+                for pair in range(wide // 128):
+                    qkv[rng, pl.ds(pl.multiple_of(k * wide + pair * 128, 128), 128)] = turn_heads(
+                        value[place * here : (place + 1) * here, pair * 128 : (pair + 1) * 128],
+                        turn,
+                        1.0,
+                    ).astype(bf16)
+
+        @pl.when(k >= 2 * hq // wide)
+        def _():
+            qkv[:, cols] = value.astype(bf16)
+
+        return 0
+
+    lax.fori_loop(0, 3 * hq // wide, project, 0)
+    for sequence in range(2):
+        mask = causal_mask(sequence, here)
+        rng = pl.ds(sequence * 2 * here, 2 * here)
+
+        def heads(k, _):
+            def pair(t):
+                return qkv[rng, pl.ds(pl.multiple_of(t * hq + k * 128, 128), 128)]
+
+            q, key, value = pair(0), pair(1), pair(2)
+            mixes = []
+            for head in range(2):
+                cut = slice(head * HEAD_DIM, (head + 1) * HEAD_DIM)
+                soft = soft_of(q[:, cut], key[:, cut], mask).astype(bf16)
+                mixes.append(dot(soft, value[:, cut], 1, 0))
+            head_mix[rng, pl.ds(pl.multiple_of(k * 128, 128), 128)] = jnp.concatenate(
+                mixes, 1
+            ).astype(bf16)
+            return 0
+
+        lax.fori_loop(0, hq // 128, heads, 0)
+
+    def out_project(k, _):
+        rng = pl.ds(pl.multiple_of(k * wide, wide), wide)
+        parts[:, rng] = dot(head_mix[...], one[rng, pl.ds(3 * hq, hq)], 1, 1).astype(bf16)
+        return 0
+
+    lax.fori_loop(0, one.shape[0] // wide, out_project, 0)
+
+
+def attention_forward(token_rows, one, table):
+    tokens, width = token_rows.shape
+    hq = (one.shape[1] - EXTRA) // 4
+    full = pl.BlockSpec(memory_space=VMEM)
+    return pl.pallas_call(
+        attention_forward_kernel,
+        out_shape=(
+            jax.ShapeDtypeStruct((tokens, width), bf16),
+            jax.ShapeDtypeStruct((2, tokens, 1), f32),
+            jax.ShapeDtypeStruct((tokens, 3 * hq), bf16),
+            jax.ShapeDtypeStruct((tokens, hq), bf16),
+            jax.ShapeDtypeStruct((tokens, width), bf16),
+            jax.ShapeDtypeStruct((4, width), f32),
+        ),
+        in_specs=[full] * 3,
+        out_specs=(full,) * 6,
+        scratch_shapes=[VMEM((12, 128), f32)],
+        compiler_params=pltpu.CompilerParams(vmem_limit_bytes=VMEM_LIMIT),
+    )(token_rows, one, table)
+
+
+def attention_backward_kernel(
+    resid, one, normed, stats, qkv, head_mix, token_rows, table, second_terms,
+    grads, first_parts, grad_mix, grad_proj,
+):
+    here = resid.shape[0] // 4
+    hq = head_mix.shape[1]
+    wide = 256
+
+    def mix_back(k, _):
+        cols = pl.ds(pl.multiple_of(k * wide, wide), wide)
+        grad_mix[:, cols] = dot(
+            resid[...], one[:, pl.ds(pl.multiple_of(3 * hq + k * wide, wide), wide)], 1, 0
+        ).astype(bf16)
+        return 0
+
+    lax.fori_loop(0, hq // wide, mix_back, 0)
+
+    def out_back(k, _):
+        rng = pl.ds(pl.multiple_of(k * wide, wide), wide)
+        grads[rng, pl.ds(3 * hq, hq)] = dot(resid[:, rng], head_mix[...], 0, 0).astype(bf16)
+        return 0
+
+    lax.fori_loop(0, one.shape[0] // wide, out_back, 0)
+    for sequence in range(2):
+        mask = causal_mask(sequence, here)
+        rng = pl.ds(sequence * 2 * here, 2 * here)
+        turn = jnp.concatenate(
+            [
+                table[pl.ds(pl.multiple_of(half_of_place(2 * sequence + k) * here, here), here)]
+                for k in range(2)
+            ],
+            0,
+        )
+
+        def heads(k, _):
+            def pair(t):
+                return pl.ds(pl.multiple_of(t * hq + k * 128, 128), 128)
+
+            q, key, value = qkv[rng, pair(0)], qkv[rng, pair(1)], qkv[rng, pair(2)]
+            mix = grad_mix[rng, pair(0)]
+            results = ([], [], [])
+            for head in range(2):
+                cut = slice(head * HEAD_DIM, (head + 1) * HEAD_DIM)
+                soft = soft_of(q[:, cut], key[:, cut], mask)
+                grad_soft = dot(mix[:, cut], value[:, cut], 1, 1)
+                row_dot = jnp.sum(grad_soft * soft, -1, keepdims=True)
+                grad_score = (soft * (grad_soft - row_dot)).astype(bf16)
+                results[0].append(dot(grad_score, key[:, cut], 1, 0) * SCALE)
+                results[1].append(dot(grad_score, q[:, cut], 0, 0) * SCALE)
+                results[2].append(dot(soft.astype(bf16), mix[:, cut], 0, 0))
+            for t in range(3):
+                both = jnp.concatenate(results[t], 1)
+                if t < 2:
+                    both = turn_heads(both, turn, -1.0)
+                grad_proj[rng, pair(t)] = both.astype(bf16)
+            return 0
+
+        lax.fori_loop(0, hq // 128, heads, 0)
+
+    bias_rows = [
+        jnp.sum(grad_proj[:, pl.ds(k * 128, 128)].astype(f32), 0, keepdims=True)
+        for k in range(3 * hq // 128)
+    ]
+    mean, inverse = stats[0], stats[1]
+
+    def weights_back(k, _):
+        rng = pl.ds(pl.multiple_of(k * wide, wide), wide)
+        grads[rng, pl.ds(0, 3 * hq)] = dot(normed[:, rng], grad_proj[...], 0, 0).astype(bf16)
+        part = dot(grad_proj[...], one[rng, pl.ds(0, 3 * hq)], 1, 1)
+        first_parts[:, rng] = part.astype(bf16)
+        unit = (token_rows[:, rng].astype(f32) - mean) * inverse
+        gain = jnp.sum(part * unit, 0, keepdims=True)
+        shift = jnp.sum(part, 0, keepdims=True)
+        for tile in range(wide // 128):
+            cut = slice(tile * 128, (tile + 1) * 128)
+            lanes = pl.ds(pl.multiple_of(k * wide + tile * 128, 128), 128)
+            block = jnp.concatenate(
+                bias_rows
+                + [
+                    gain[:, cut],
+                    shift[:, cut],
+                    second_terms[:, lanes],
+                    jnp.zeros((16, 128), f32),
+                ],
+                0,
+            ).astype(bf16)
+            for copy in range(4):
+                start = pl.multiple_of(k * wide + tile * 128 + copy * 32, 32)
+                grads[pl.ds(start, 32), pl.ds(4 * hq, 128)] = block
+        return 0
+
+    lax.fori_loop(0, one.shape[0] // wide, weights_back, 0)
+
+
+def attention_backward(resid, one, normed, stats, qkv, head_mix, token_rows, table, second_terms):
+    tokens, width = token_rows.shape
+    hq = head_mix.shape[1]
+    full = pl.BlockSpec(memory_space=VMEM)
+    return pl.pallas_call(
+        attention_backward_kernel,
+        out_shape=(
+            jax.ShapeDtypeStruct(one.shape, bf16),
+            jax.ShapeDtypeStruct((tokens, width), bf16),
+        ),
+        in_specs=[full] * 9,
+        out_specs=(full,) * 2,
+        scratch_shapes=[VMEM((tokens, hq), bf16), VMEM((tokens, 3 * hq), bf16)],
+        compiler_params=pltpu.CompilerParams(vmem_limit_bytes=VMEM_LIMIT),
+    )(resid, one, normed, stats, qkv, head_mix, token_rows, table, second_terms)
+
+
+def feed_forward_kernel(
+    normed, cot_rows, cotangent, unit, scale, gains, weights,
+    resid, sums, spread, mixed_parts, chip,
+    held, pair, hidden, normed_t, cot_t, parts, sib, mid, sent, far, near,
+    load_sem, store_sem, core_send, core_recv, y_send, y_recv,
+):
+    columns, width = held.shape[1] // 3, held.shape[0]
+    wide = 256
+    rows = sib.shape[1]
+    c = lax.axis_index("c")
+    y_sems, core_sems = (y_send, y_recv), (core_send, core_recv)
+    whole, rest = columns // wide, columns % wide
+
+    def load(k, which, size):
+        start = pl.multiple_of(which * columns + k * wide, 128)
+        cut = pl.ds(start, size)
+        return pltpu.make_async_copy(weights.at[:, cut], held.at[:, cut], load_sem.at[k, which])
+
+    for k in range(whole + (rest > 0)):
+        for which in range(3):
+            load(k, which, wide if k < whole else rest).start()
+
+    def flip(k, _):
+        rng = pl.ds(pl.multiple_of(k * wide, wide), wide)
+        normed_t[rng] = normed[:, rng].T
+        cot_t[rng] = cot_rows[:, rng].T
+        return 0
+
+    lax.fori_loop(0, width // wide, flip, 0)
+    greet([at_y(1), at_y(3), sibling()])
+
+    def ahead(k, size):
+        def cut(which):
+            return pl.ds(pl.multiple_of(which * columns + k * wide, 128), size)
+
+        for which in range(3):
+            load(k, which, size).wait()
+        gate = dot(normed[...], held[:, cut(0)], 1, 0)
+        up = dot(normed[...], held[:, cut(1)], 1, 0)
+        grad_hidden = dot(cot_rows[...], held[:, cut(2)], 1, 0)
+        sigmoid = jax.nn.sigmoid(gate)
+        activated = gate * sigmoid
+        hidden[:, cut(0)] = (activated * up).astype(bf16)
+        pair[:, cut(0)] = (
+            grad_hidden * up * sigmoid * (1.0 + gate * (1.0 - sigmoid))
+        ).astype(bf16)
+        pair[:, cut(1)] = (grad_hidden * activated).astype(bf16)
+        return 0
+
+    lax.fori_loop(0, whole, lambda k, _: ahead(k, wide), 0)
+    if rest:
+        ahead(whole, rest)
+
+    def second_back(k, _):
+        rng = pl.ds(pl.multiple_of(k * wide, wide), wide)
+        parts[:, rng] = dot(pair[...], held[rng, pl.ds(0, 2 * columns)], 1, 1).astype(bf16)
+        return 0
+
+    lax.fori_loop(0, width // wide, second_back, 0)
+    started = ring_sum_start(parts, mid, near, y_sems, 0)
+
+    def mix(k, _):
+        rng = pl.ds(pl.multiple_of(k * wide, wide), wide)
+        mixed_parts[:, rng] = dot(
+            hidden[...], held[rng, pl.ds(2 * columns, columns)], 1, 1
+        ).astype(bf16)
+        return 0
+
+    lax.fori_loop(0, width // wide, mix, 0)
+    middle = ring_sum_middle(parts, started, mid, sent, far, y_sems, 0)
+
+    def to_core(block):
+        theirs = pl.ds(pl.multiple_of((2 * block + 1 - c) * rows, rows), rows)
+        return remote(held.at[theirs], sib.at[block], core_sems, block, sibling())
+
+    def weights_back(k, _):
+        rng = pl.ds(pl.multiple_of(k * wide, wide), wide)
+        held[rng, pl.ds(0, 2 * columns)] = dot(normed_t[rng], pair[...], 1, 0).astype(bf16)
+        held[rng, pl.ds(2 * columns, columns)] = dot(cot_t[rng], hidden[...], 1, 0).astype(bf16)
+        for block in range(wide // (2 * rows)):
+            to_core(k * (wide // (2 * rows)) + block).start()
+        return 0
+
+    lax.fori_loop(0, width // wide, weights_back, 0)
+    finish = ring_sum_finish(parts, started, middle, far, near)
+    half = cotangent.shape[0] // 2
+    halves = []
+    for top in range(2):
+        here = pl.ds(top * half, half)
+        total = finish(top)
+        unit_rows = unit[here]
+        incoming = total * gains[0:1]
+        result = cotangent[here].astype(f32) + scale[here] * (
+            incoming
+            - jnp.mean(incoming, -1, keepdims=True)
+            - unit_rows * jnp.mean(incoming * unit_rows, -1, keepdims=True)
+        )
+        resid[here] = result
+        spread[here] = result.astype(bf16)
+        halves.append(ring_gather_half(spread, top, y_sems, 6))
+        both = jnp.concatenate(
+            [
+                jnp.sum(total * unit_rows, 0, keepdims=True),
+                jnp.sum(total, 0, keepdims=True),
+            ],
+            0,
+        )
+        sums[...] = both if top == 0 else sums[...] + both
+
+    blocks = sib.shape[0]
+
+    def store(block):
+        ours = pl.ds(pl.multiple_of((2 * block + c) * rows, rows), rows)
+        return pltpu.make_async_copy(held.at[ours], chip.at[block], store_sem.at[block])
+
+    def add_core(block, _):
+        to_core(block).wait_recv()
+        ours = pl.ds(pl.multiple_of((2 * block + c) * rows, rows), rows)
+        held[ours] = (held[ours].astype(f32) + sib[block].astype(f32)).astype(bf16)
+        store(block).start()
+        return 0
+
+    lax.fori_loop(0, blocks // 2, add_core, 0)
+    passed = ring_gather_pass(spread, halves, y_sems, 6)
+    lax.fori_loop(blocks // 2, blocks, add_core, 0)
+
+    def drain(block, _):
+        to_core(block).wait_send()
+        store(block).wait()
+        return 0
+
+    lax.fori_loop(0, blocks, drain, 0)
+    for copy in passed + [halves[1][0], halves[0][1]]:
+        copy.wait_recv()
+    for copy in started + middle + halves[0] + halves[1] + passed:
+        copy.wait_send()
+
+
+def feed_forward(normed, cot_rows, cotangent, unit, scale, gains, weights):
+    tokens, width = normed.shape
+    here = cotangent.shape[0]
+    columns = weights.shape[1] // 3
+    blocks, rows = 16, width // 32
+    full = pl.BlockSpec(memory_space=VMEM)
+    anywhere = pl.BlockSpec(memory_space=pl.ANY)
+    tiles = -(-columns // 256)
+    return pl.pallas_call(
+        feed_forward_kernel,
+        out_shape=(
+            jax.ShapeDtypeStruct((here, width), f32),
+            jax.ShapeDtypeStruct((2, width), f32),
+            jax.ShapeDtypeStruct((tokens, width), bf16),
+            jax.ShapeDtypeStruct((tokens, width), bf16),
+            jax.ShapeDtypeStruct((blocks, rows, 3 * columns), bf16),
+        ),
+        in_specs=[full] * 6 + [anywhere],
+        out_specs=(full,) * 4 + (anywhere,),
+        scratch_shapes=[
+            VMEM((width, 3 * columns), bf16),
+            VMEM((tokens, 2 * columns), bf16),
+            VMEM((tokens, columns), bf16),
+            VMEM((width, tokens), bf16),
+            VMEM((width, tokens), bf16),
+            VMEM((tokens, width), bf16),
+            VMEM((blocks, rows, 3 * columns), bf16),
+        ]
+        + [VMEM((2, here // 2, width), bf16)] * 4
+        + [DMA((tiles, 3)), DMA((blocks,)), DMA((blocks,)), DMA((blocks,)), DMA((12,)), DMA((12,))],
+        compiler_params=pltpu.CompilerParams(
+            collective_id=2, has_side_effects=True, vmem_limit_bytes=VMEM_LIMIT
+        ),
+    )(normed, cot_rows, cotangent, unit, scale, gains, weights)
+
+
+SAME = [(0, 0), (1, 2), (2, 1), (3, 3)]
+CROSS = [(0, 2), (1, 0), (2, 3), (3, 1)]
 
 
 def from_quarters(rows):
     yl, c = lax.axis_index("yl"), lax.axis_index("c")
-    halves = rows.reshape(2, 32, rows.shape[1])
+    halves = rows.reshape(2, rows.shape[0] // 2, rows.shape[1])
     one = lax.ppermute(
-        lax.dynamic_index_in_dim(halves, yl, 0, False), PAIR, [(b, a) for a, b in SAME]
+        lax.dynamic_index_in_dim(halves, yl, 0, False), ("yl", "c"), [(b, a) for a, b in SAME]
     )
     two = lax.ppermute(
-        lax.dynamic_index_in_dim(halves, 1 - yl, 0, False), PAIR, [(b, a) for a, b in CROSS]
+        lax.dynamic_index_in_dim(halves, 1 - yl, 0, False),
+        ("yl", "c"),
+        [(b, a) for a, b in CROSS],
     )
     return jnp.stack([jnp.where(c == 0, one, two), jnp.where(c == 0, two, one)])
-
-
-def unit_of(values):
-    centered = values - jnp.mean(values, -1, keepdims=True)
-    variance = jnp.mean(centered * centered, -1, keepdims=True)
-    inverse = lax.rsqrt(variance + EPSILON)
-    return centered * inverse, inverse
-
-
-def rotate(values, cosine, sine):
-    half = ROTARY // 2
-    low, high = values[..., :half], values[..., half:ROTARY]
-    return jnp.concatenate(
-        [low * cosine - high * sine, high * cosine + low * sine, values[..., ROTARY:]], -1
-    )
 
 
 def shards(
     tokens, cotangent, norm_params, qkv_weight, qkv_bias, out_weight, gate_up_weight, down_weight
 ):
-    yl, yh = lax.axis_index("yl"), lax.axis_index("yh")
-    y = yh * 2 + yl
+    yl, yh, c = lax.axis_index("yl"), lax.axis_index("yh"), lax.axis_index("c")
+    mine = ((lax.axis_index("z") * 4 + lax.axis_index("x")) * 2 + yl) * 2 + c
     rows = qkv_weight.shape[1]
     hq = qkv_weight.shape[2] // 2
     fq = gate_up_weight.shape[2] // 2
     heads = hq // HEAD_DIM
-    here = tokens.shape[0]
-    length = 2 * here
+    pairs = 3 * heads // 2
 
     qkv_q = qkv_weight.reshape(3, rows, 2, hq).transpose(2, 1, 0, 3).reshape(2, rows, 3 * hq)
     out_q = out_weight.T.reshape(rows, 2, hq).transpose(1, 0, 2)
@@ -760,122 +1128,48 @@
         yh == 0,
         jnp.concatenate([norm_params, other], 1),
         jnp.concatenate([other, norm_params], 1),
-    ).T
-    norm_high = norm_rows.astype(bf16)
+    )
+    norm_high = lax.optimization_barrier(norm_rows.astype(bf16))
     norm_low = (norm_rows - norm_high.astype(f32)).astype(bf16)
-    bias_q = qkv_bias.reshape(3, 2, heads).transpose(1, 0, 2).reshape(2, 1, 3 * heads)
-    bias_q = jnp.pad(bias_q, ((0, 0), (0, rows - 1), (8, EXTRA - 8 - 3 * heads)))
-    extra = jnp.pad(jnp.concatenate([norm_high, norm_low], 1), ((0, 0), (0, EXTRA - 8)))
-    extra_q = bias_q + extra[None]
-
-    first, second, token_rows, cot_rows = first_gather(
+    lanes = jnp.arange(EXTRA)
+    norm_extra = jnp.where(
+        lanes // rows == mine % 4,
+        jnp.tile(jnp.concatenate([norm_high, norm_low], 0), (1, EXTRA // rows)),
+        0,
+    )
+    bias_q = qkv_bias.reshape(3, 2, heads).transpose(1, 0, 2).reshape(2, pairs, 2, 1)
+    bias_extra = jnp.where(jnp.arange(HEAD_DIM) == mine, bias_q, 0).reshape(2, pairs, EXTRA)
+    extra_q = jnp.concatenate(
+        [
+            bias_extra,
+            jnp.broadcast_to(norm_extra[None], (2, *norm_extra.shape)),
+            jnp.zeros((2, rows - pairs - 8, EXTRA), bf16),
+        ],
+        1,
+    )
+    one, second, token_rows, cot_rows = first_gather(
         jnp.concatenate([qkv_q, out_q, extra_q], axis=2),
         jnp.concatenate([gu_q, down_q], axis=2),
         tokens,
         cotangent,
     )
-    second = lax.all_gather(second, SPREAD, axis=0, tiled=True)
-    w_qkv, w_out = first[:, : 3 * hq], first[:, 3 * hq : 4 * hq]
-    extras = first[:, 4 * hq :]
-    w_gu, w_down = second[:, : 2 * fq], second[:, 2 * fq :]
-    width = extras.shape[0]
-    norm_table = (extras[:, :4].astype(f32) + extras[:, 4:8].astype(f32)).T
-    bias = extras.reshape(HEAD_DIM, rows, EXTRA)[:, 0, 8 : 8 + 3 * heads].T.reshape(3 * hq)
-
-    unit_rows, inverse_rows = unit_of(token_rows.astype(f32))
-    unit_one, scale_one = unit_rows[:here], inverse_rows[:here]
-    normed_one = (unit_rows * norm_table[0] + norm_table[1]).astype(bf16)
-    projected = mm(normed_one, w_qkv, 1, 0) + bias.astype(f32)
-    place = jnp.stack([((y + k) % 4) // 2 for k in (0, 2, 1, 3)])
-    position = (place[:, None] * here + jnp.arange(here)[None, :]).reshape(2, length)
-    frequency = jnp.power(10000.0, -jnp.arange(ROTARY // 2).astype(f32) * (2.0 / ROTARY))
-    angles = position.astype(f32)[:, :, None] * frequency
-    cosine, sine = jnp.cos(angles)[:, :, None, :], jnp.sin(angles)[:, :, None, :]
-    split = projected.reshape(2, length, 3, heads, HEAD_DIM)
-    queries = rotate(split[:, :, 0], cosine, sine).astype(bf16)
-    key_heads = rotate(split[:, :, 1], cosine, sine).astype(bf16)
-    value_heads = split[:, :, 2].astype(bf16)
-    causal = position[:, :, None] >= position[:, None, :]
-    scores = (
-        jnp.einsum("bshd,bthd->bhst", queries, key_heads, preferred_element_type=f32) * SCALE
-    )
-    scores = jnp.where(causal[:, None], scores, -1000000000.0)
-    powers = jnp.exp(scores - jnp.max(scores, -1, keepdims=True))
-    soft = powers / jnp.sum(powers, -1, keepdims=True)
-    soft_low = soft.astype(bf16)
-    head_mix = jnp.einsum("bhst,bthd->bshd", soft_low, value_heads, preferred_element_type=f32)
-    head_mix = head_mix.reshape(2 * length, hq).astype(bf16)
-
-    first_sum, unit_two, scale_two, normed_two = second_norm(
-        mm(head_mix, w_out, 1, 1).astype(bf16), tokens, norm_table[2:]
-    )
-    gate_up = mm(normed_two, w_gu, 1, 0)
-    gate_pre, up_pre = gate_up[:, :fq], gate_up[:, fq:]
-    sigmoid = jax.nn.sigmoid(gate_pre)
-    activated = gate_pre * sigmoid
-    hidden = (activated * up_pre).astype(bf16)
-    grad_down = mm(cot_rows, hidden, 0, 0).astype(bf16)
-    mixed_parts = mm(hidden, w_down, 1, 1).astype(bf16)
-    grad_hidden = mm(cot_rows, w_down, 1, 0)
-    grad_gate = grad_hidden * up_pre * sigmoid * (1.0 + gate_pre * (1.0 - sigmoid))
-    grad_pair = jnp.concatenate([grad_gate, grad_hidden * activated], 1).astype(bf16)
-    grad_gu = mm(normed_two, grad_pair, 0, 0).astype(bf16)
-    second_cores = jnp.concatenate([grad_gu, grad_down], 1).reshape(16, 2, 2 * rows, 3 * fq)
-    core = lax.axis_index("c")
-    arriving = lax.ppermute(
-        lax.dynamic_index_in_dim(second_cores, 1 - core, 1, False), "c", [(0, 1), (1, 0)]
-    )
-    second_parts = mm(grad_pair, w_gu, 1, 1).astype(bf16)
-    second_chip = (
-        lax.dynamic_index_in_dim(second_cores, core, 1, False).astype(f32) + arriving.astype(f32)
-    ).astype(bf16)
-    second_parts, second_chip = lax.optimization_barrier((second_parts, second_chip))
+    second = lax.all_gather(second, ("z", "x", "c"), axis=0, tiled=True)
+    table = jnp.asarray(tables())
+    normed_one, stats, qkv, head_mix, parts, norm_table = attention_forward(
+        token_rows, one, table
+    )
+    first_sum, unit_two, scale_two, normed_two = second_norm(parts, tokens, norm_table[2:])
+    grad_resid, second_terms, resid_rows, mixed_parts, chip = feed_forward(
+        normed_two, cot_rows, cotangent, unit_two, scale_two, norm_table[2:], second
+    )
     second_sums = lax.psum_scatter(
-        second_chip.reshape(width // 2, 3 * fq), ("z", "x"), scatter_dimension=0, tiled=True
-    )
-    grad_resid, second_terms, resid_rows = second_norm_back(
-        second_parts, cotangent, unit_two, scale_two, norm_table[2:]
-    )
-
-    grad_mix = mm(resid_rows, w_out, 1, 0).astype(bf16).reshape(2, length, heads, HEAD_DIM)
-    grad_out = mm(resid_rows, head_mix, 0, 0).astype(bf16)
-    grad_soft = jnp.einsum("bshd,bthd->bhst", grad_mix, value_heads, preferred_element_type=f32)
-    row_dot = jnp.sum(grad_soft * soft, -1, keepdims=True)
-    grad_score = (soft * (grad_soft - row_dot)).astype(bf16)
-    grad_query = (
-        jnp.einsum("bhst,bthd->bshd", grad_score, key_heads, preferred_element_type=f32) * SCALE
-    )
-    grad_key = (
-        jnp.einsum("bhst,bshd->bthd", grad_score, queries, preferred_element_type=f32) * SCALE
-    )
-    grad_value = jnp.einsum("bhst,bshd->bthd", soft_low, grad_mix, preferred_element_type=f32)
-    grad_proj = jnp.concatenate(
-        [
-            rotate(grad_query, cosine, -sine).reshape(2 * length, hq),
-            rotate(grad_key, cosine, -sine).reshape(2 * length, hq),
-            grad_value.reshape(2 * length, hq),
-        ],
-        1,
-    ).astype(bf16)
-    grad_qkv = mm(normed_one, grad_proj, 0, 0).astype(bf16)
-    first_parts = mm(grad_proj, w_qkv, 1, 1)
-    gain_one = jnp.sum(first_parts * unit_rows, 0)
-    shift_one = jnp.sum(first_parts, 0)
-    grad_bias = jnp.sum(grad_proj.astype(f32), 0).reshape(3 * heads, HEAD_DIM).T
-    norm_terms = jnp.concatenate([jnp.stack([gain_one, shift_one]), second_terms], 0).T
-    grad_extra = jnp.pad(norm_terms, ((0, 0), (0, EXTRA - 4))) + jnp.pad(
-        grad_bias[:, None, :], ((0, 0), (0, rows - 1), (8, EXTRA - 8 - 3 * heads))
-    ).reshape(width, EXTRA)
-    grad_first = jnp.concatenate([grad_qkv, grad_out, grad_extra.astype(bf16)], 1)
+        chip.reshape(-1, 3 * fq), ("z", "x"), scatter_dimension=0, tiled=True
+    )
+    grads, first_parts = attention_backward(
+        resid_rows, one, normed_one, stats, qkv, head_mix, token_rows, table, second_terms
+    )
     first_back, grad_input, mixed = last_sum(
-        grad_first,
-        first_parts.astype(bf16),
-        mixed_parts,
-        grad_resid,
-        unit_one,
-        scale_one,
-        norm_table[:2],
-        first_sum,
+        grads, first_parts, mixed_parts, grad_resid, tokens, stats, norm_table[:2], first_sum
     )
 
     second_back = from_quarters(second_sums)
@@ -896,15 +1190,22 @@
     )
     extra_back = first_back[:, :, 4 * hq :].astype(f32)
     out_bias = (
-        extra_back[:, 0, 8 : 8 + 3 * heads]
+        lax.dynamic_index_in_dim(
+            extra_back[:, :pairs].reshape(2, pairs, 2, HEAD_DIM), mine, 3, False
+        )
         .reshape(2, 3, heads)
         .transpose(1, 0, 2)
         .reshape(3, 2 * heads, 1)
     )
-    norm_back = (extra_back[0, :, :4] + extra_back[1, :, :4]).T.reshape(4, 2, rows // 2)
-    mine = lax.dynamic_index_in_dim(norm_back, yh, 1, False)
-    theirs = lax.dynamic_index_in_dim(norm_back, 1 - yh, 1, False)
-    out_norm = mine + lax.ppermute(theirs, "yh", [(0, 1), (1, 0)])
+    norm_back = lax.dynamic_index_in_dim(
+        (extra_back[0] + extra_back[1])[pairs : pairs + 4].reshape(4, EXTRA // rows, rows),
+        mine % 4,
+        1,
+        False,
+    ).reshape(4, 2, rows // 2)
+    kept = lax.dynamic_index_in_dim(norm_back, yh, 1, False)
+    sent = lax.dynamic_index_in_dim(norm_back, 1 - yh, 1, False)
+    out_norm = kept + lax.ppermute(sent, "yh", [(0, 1), (1, 0)])
     return (mixed, grad_input, out_norm, out_qkv, out_bias, out_out, out_gu, out_down)
 
 

time: 436 us -> 335 us (0.77); the launches traced: 428 us -> 335 us
  matrix products: 99.2 us -> 0 us
  Pallas kernels: 199 us -> 286 us
  local copies, waits for them, and re-layouts: 71.5 us -> 15.7 us
  other arithmetic: 30.7 us -> 5.06 us
    dot_general x17 -> x0, matrix products: 93.8 us -> none  [the longest x12 85.8 us: mm(): lax.dot_general(a, b, (((ca,), (cb,)), ((), ())), preferred_element_type=...]
    pallas_call x1 -> x3, Pallas kernels: 44.1 us -> 127 us  [the longest x1 66.8 us: feed_forward(): pl.pallas_call(feed_forward_kernel, out_shape=(jax.ShapeDtypeStruct((here...]
    slice x13 -> x3, local copies, waits for them, and re-layouts: 14 us -> 0.01 us  [the longest x2 0.01 us: shards(): extra_back[:, :pairs].reshape(2, pairs, 2, HEAD_DIM)]
    pallas_call x1 -> x0, local copies, waits for them, and re-layouts: 13 us -> none  [first_gather(): pl.pallas_call(first_gather_kernel, out_shape=(jax.ShapeDtypeStruct((64 *...]
    concatenate x5 -> x1, other arithmetic: 10.8 us -> 0.01 us  [shards(): jnp.concatenate([norm_high, norm_low], 0)]
    unnamed x79 -> x12, local copies, waits for them, and re-layouts: 11.5 us -> 1.79 us
    convert_element_type x6 -> x1, other arithmetic: 9.18 us -> 0.08 us  [shards(): norm_high = lax.optimization_barrier(norm_rows.astype(bf16))]
    reshape x8 -> x6, local copies, waits for them, and re-layouts: 10.4 us -> 1.76 us  [the longest x1 0.76 us: shards(): qkv_bias.reshape(3, 2, heads).transpose(1, 0, 2).reshape(2, pairs, 2, 1)]
  transfers between devices with their start and end apart: 7 -> 6, of which waited for: 2 -> 2; matrix products, arithmetic and copies ran while one was open for 33% -> 4% of each run, Pallas kernels for 34% -> 49%
where the time goes in v3:
time: 335 us
  Pallas kernels  286 us (85%)
  local copies, waits for them, and re-layouts  15.7 us (5%)
  between operations  14.4 us (4%)
  starting transfers between devices  7.21 us (2%)
  waiting for transfers between devices  6.83 us (2%)
  other arithmetic  5.06 us (2%)
    pallas_call x1, Pallas kernels, feed_forward(): pl.pallas_call(feed_forward_kernel, out_shape=(jax.ShapeDtypeStruct((here...  66.8 us
    pallas_call x1, Pallas kernels, last_sum(): pl.pallas_call(last_sum_kernel, out_shape=(jax.ShapeDtypeStruct((2, rows,...  58.8 us
    pallas_call x1, Pallas kernels, first_gather(): pl.pallas_call(first_gather_kernel, out_shape=(jax.ShapeDtypeStruct((64 *...  55.6 us
    pallas_call x1, Pallas kernels, second_norm(): pl.pallas_call(second_norm_kernel, out_shape=(jax.ShapeDtypeStruct((here,...  44.1 us
    pallas_call x1, Pallas kernels, attention_backward(): pl.pallas_call(attention_backward_kernel, out_shape=(jax.ShapeDtypeStruct...  35.6 us
    pallas_call x1, Pallas kernels, attention_forward(): pl.pallas_call(attention_forward_kernel, out_shape=(jax.ShapeDtypeStruct(...  24.9 us
  transfers between devices with their start and end apart: 6, of which 2 were waited for; matrix products, arithmetic and copies ran while one was open for 4% of the time, Pallas kernels for 49%

profile of v3, /device:TPU:0, one launch (start us, length us, event | category | flops | bytes accessed | tf_op | source)
XLA Modules:
  0.0 334.9 jit_solution(10484991394722481485)
XLA Ops:
  7.2 0.0 copy-start.2
  7.2 0.0 all-gather.2.cloned.1.call-start
  7.2 3.4 %collective-permute-start = (f32[4,16]{1,0:T(4,128)}, f32[4,16]{1,0:T(4,128)S(1)}, u32[]{:S(2)}, u32[]{:S(2)}) collective-permute-start(f32[4,16]{1,0:T(4,128)} %param.11), channel_id=1, source_target_pairs={{0,1},{1,0},{2,3},{3,2},{4,5},{5,4},{6,7},{7,6},{8,9},{9,8},{10,11... | collective-permute-start | bytes 776 | tf_op jit(solution)/shard_map/ppermute | solution.py:1126
  10.6 0.1 broadcast_in_dim.40
  10.7 0.8 reshape.113
  11.5 0.1 broadcast_in_dim.42
  11.6 0.1 broadcast_in_dim.43
  11.7 0.1 broadcast_in_dim.44
  11.7 1.1 reshape.110
  12.8 0.2 copy.68
  13.0 0.0 copy-start.3
  13.0 0.0 copy-start.4
  13.0 1.1 reshape.114
  14.1 0.4 copy.67
  14.5 0.2 reshape.115
  14.8 0.8 pad_maximum_fusion.two_q
  15.6 0.3 reshape.111
  15.9 0.0 collective-permute-done
  15.9 0.0 copy-done.4
  16.0 0.1 fusion.3
  16.0 0.1 subtract_convert_fusion
  16.1 0.1 tile.10
  16.3 0.8 maximum_maximum_fusion.one_q
  17.0 55.6 %shard_map.152 = (bf16[2048,2176]{1,0:T(8,128)(2,1)}, bf16[64,4224]{1,0:T(8,128)(2,1)}, bf16[512,2048]{1,0:T(8,128)(2,1)}, bf16[512,2048]{1,0:T(8,128)(2,1)}) custom-call(bf16[2,32,2176]{2,1,0:T(8,128)(2,1)} %maximum_maximum_fusion.one_q, bf16[2,32,4224]{2,1,0:T(8,128)(2,1)} %pad_maximum_fusion.two_q, bf16[128,2048]{1,0:T(8,128)(2,1)} %tokens.5, ...), custom_call_target="tpu_custom_call" | custom-call | tf_op jit(solution)/shard_map/pallas_call | solution.py:353
  72.6 0.0 all-gather.2.cloned.1.call-update
  72.7 0.2 reduce-scatter.2.cloned.1.call-start
  72.9 24.9 %shard_map.153 = (bf16[512,2048]{1,0:T(8,128)(2,1)}, f32[2,512,1]{2,1,0:T(8,128)}, bf16[512,1536]{1,0:T(8,128)(2,1)}, bf16[512,512]{1,0:T(8,128)(2,1)}, bf16[512,2048]{1,0:T(8,128)(2,1)}, /*index=5*/f32[4,2048]{1,0:T(4,128)}) custom-call(bf16[512,2048]{1,0:T(8,128)(2,1)} %get-tuple-element.32.token_rows, bf16[2048,2176]{1,0:T(8,128)(2,1)} %get-tuple-element.33.one, ...), custom_call_target="tpu_custom_call" | custom-call | tf_op jit(solution)/shard_map/pallas_call | solution.py:791
  97.8 1.5 fusion.5
  99.3 44.1 %shard_map.154 = (f32[128,2048]{1,0:T(8,128)}, f32[128,2048]{1,0:T(8,128)}, f32[128,1]{1,0:T(8,128)}, bf16[512,2048]{1,0:T(8,128)(2,1)}) custom-call(bf16[512,2048]{1,0:T(8,128)(2,1)} %get-tuple-element.34.parts, bf16[128,2048]{1,0:T(8,128)(2,1)} %tokens.5, f32[2,2048]{1,0:T(2,128)} %get-tuple-element.87.gains), custom_call_target="tpu_custom_call" | custom-call | tf_op jit(solution)/shard_map/pallas_call | solution.py:137
  143.4 1.9 all-gather.2.cloned.1.call-done.weights
  145.3 66.8 %shard_map.155 = (f32[128,2048]{1,0:T(8,128)}, f32[2,2048]{1,0:T(2,128)}, bf16[512,2048]{1,0:T(8,128)(2,1)}, bf16[512,2048]{1,0:T(8,128)(2,1)}, bf16[16,64,4224]{2,1,0:T(8,128)(2,1)}) custom-call(bf16[512,2048]{1,0:T(8,128)(2,1)} %get-tuple-element.36.normed, bf16[512,2048]{1,0:T(8,128)(2,1)} %get-tuple-element.37.cot_rows, bf16[128,2048]{1,0:T(8,128)(2,1)} %cotangent.3, ...), custom_call_target="tpu_custom_call" | custom-call | tf_op jit(solution)/shard_map/pallas_call | solution.py:1065
  212.1 0.0 reduce-scatter.2.cloned.1.call-update
  212.1 35.6 %shard_map.156 = (bf16[2048,2176]{1,0:T(8,128)(2,1)}, bf16[512,2048]{1,0:T(8,128)(2,1)}) custom-call(bf16[512,2048]{1,0:T(8,128)(2,1)} %get-tuple-element.41.resid, bf16[2048,2176]{1,0:T(8,128)(2,1)} %get-tuple-element.33.one, bf16[512,2048]{1,0:T(8,128)(2,1)} %get-tuple-element.42.normed, f32[2,512,1]{2,1,0:T(8,128)} %get-tuple-element.43.stats, ...), custom_call_target="tpu_custom_call" | custom-call | tf_op jit(solution)/shard_map/pallas_call | solution.py:906
  247.6 58.8 %shard_map.157 = (bf16[2,32,2176]{2,1,0:T(8,128)(2,1)}, f32[128,2048]{1,0:T(8,128)}, bf16[128,2048]{1,0:T(8,128)(2,1)}) custom-call(bf16[2048,2176]{1,0:T(8,128)(2,1)} %get-tuple-element.47.grads, bf16[512,2048]{1,0:T(8,128)(2,1)} %get-tuple-element.48.first_parts, bf16[512,2048]{1,0:T(8,128)(2,1)} %get-tuple-element.49.mixed_parts, ...), custom_call_target="tpu_custom_call" | custom-call | tf_op jit(solution)/shard_map/pallas_call | solution.py:617
  306.5 1.0 slice_convert_fusion
  307.4 0.3 reshape.128
  307.7 0.3 copy.49
  308.0 1.1 reshape.124
  309.1 0.7 slice_convert_fusion.1
  309.9 0.1 reshape.117
  310.0 0.1 reshape.118
  310.1 2.5 collective-permute-start.1
  312.6 1.1 dynamic-slice_bitcast_fusion
  313.7 0.7 collective-permute-start.2
  314.4 0.4 collective-permute-start.3
  314.7 0.8 convert_bitcast_fusion.1
  315.6 0.7 copy.60
  316.3 0.1 reshape.119
  316.4 0.1 constant_dynamic-slice_fusion
  316.5 0.3 copy.51
  316.8 0.1 reshape.120
  316.8 0.7 reshape.130
  317.5 0.0 collective-permute-done.1
  317.5 0.6 add.56
  318.1 0.0 collective-permute-done.2
  318.1 4.9 %collective-permute-done.3 = bf16[32,4224]{1,0:T(8,128)(2,1)S(1)} collective-permute-done((bf16[32,4224]{1,0:T(8,128)(2,1)S(1)}, bf16[32,4224]{1,0:T(8,128)(2,1)S(1)}, u32[]{:S(2)}, u32[]{:S(2)}) %collective-permute-start.3) | collective-permute-done | bytes 270368 | tf_op jit(solution)/shard_map/ppermute | solution.py:1103
  323.0 0.1 select_bitcast_fusion
  323.1 0.1 fusion.1
  323.1 0.8 copy.61
  323.9 0.4 reshape.129
  324.3 0.6 copy.54
  324.9 1.4 reshape.126
  326.3 0.8 copy.73
  327.1 1.0 copy.74
  (28 shorter events, 0.2 us)
Async XLA Ops:
  7.2 7.6 %copy-start.2 = (bf16[2816,32]{0,1:T(8,128)(2,1)S(1)}, bf16[2816,32]{0,1:T(8,128)(2,1)}, u32[]{:S(2)}) copy-start(bf16[2816,32]{0,1:T(8,128)(2,1)} %param.16) | copy-start | bytes 540676
  7.2 138.1 %all-gather.2.cloned.1.call-start = ((), (), s32[]{:S(2)}) async-start(), calls=%async_computation.1 | async-start | bytes 17842176 | tf_op jit(solution)/shard_map/all_gather | solution.py:1156
  7.2 8.7 %collective-permute-start = (f32[4,16]{1,0:T(4,128)}, f32[4,16]{1,0:T(4,128)S(1)}, u32[]{:S(2)}, u32[]{:S(2)}) collective-permute-start(f32[4,16]{1,0:T(4,128)} %param.11), channel_id=1, source_target_pairs={{0,1},{1,0},{2,3},{3,2},{4,5},{5,4},{6,7},{7,6},{8,9},{9,8},{10,11... | collective-permute-start | bytes 776 | tf_op jit(solution)/shard_map/ppermute | solution.py:1126
  13.0 2.9 copy-start.3
  13.0 2.9 copy-start.4
  72.7 240.0 %reduce-scatter.2.cloned.1.call-start = ((), (), s32[]{:S(2)}) async-start(), calls=%async_computation.2 | async-start | bytes 9191424 | tf_op jit(solution)/shard_map/reduce_scatter | solution.py:1165
  310.1 7.4 %collective-permute-start.1 = (f32[4,16]{1,0:T(4,128)S(1)}, f32[4,16]{1,0:T(4,128)S(1)}, u32[]{:S(2)}, u32[]{:S(2)}) collective-permute-start(f32[4,16]{1,0:T(4,128)S(1)} %bitcast.73), channel_id=1, source_target_pairs={{0,1},{1,0},{2,3},{3,2},{4,5},{5,4},{6,7},{7,6},{8,9},{9,8},{10,11... | collective-permute-start | bytes 776 | tf_op jit(solution)/shard_map/ppermute | solution.py:1208
  313.7 4.4 %collective-permute-start.2 = (bf16[32,4224]{1,0:T(8,128)(2,1)S(1)}, bf16[32,4224]{1,0:T(8,128)(2,1)S(1)}, u32[]{:S(2)}, u32[]{:S(2)}) collective-permute-start(bf16[32,4224]{1,0:T(8,128)(2,1)S(1)} %get-tuple-element.83), channel_id=1, source_target_pairs={{0,0},{4,2},{2,4},{6,6},{1,1},{5,3},{3,5},{7,7},{8,8},{12,10},{10,... | collective-permute-start | bytes 811016 | tf_op jit(solution)/shard_map/ppermute | solution.py:1100
  314.4 8.6 %collective-permute-start.3 = (bf16[32,4224]{1,0:T(8,128)(2,1)S(1)}, bf16[32,4224]{1,0:T(8,128)(2,1)S(1)}, u32[]{:S(2)}, u32[]{:S(2)}) collective-permute-start(bf16[32,4224]{1,0:T(8,128)(2,1)S(1)} %get-tuple-element.82), channel_id=1, source_target_pairs={{4,0},{0,2},{6,4},{2,6},{5,1},{1,3},{7,5},{3,7},{12,8},{8,10},{14,... | collective-permute-start | bytes 811016 | tf_op jit(solution)/shard_map/ppermute | solution.py:1103
  323.9 2.4 copy-start.1
  324.3 2.8 copy-start
Sparse Core Ops, SparseCore 0:
  72.8 72.4 all-gather.1
  212.2 90.5 reduce-scatter.1

commit v4 on v3

--- a/solution.py
+++ b/solution.py
@@ -61,12 +61,6 @@
         device_id=device,
         device_id_type=MESH,
     )
-
-
-def ring_sum(parts, mid, sent, far, near, sems):
-    started = ring_sum_start(parts, mid, near, sems, 0)
-    middle = ring_sum_middle(parts, started, mid, sent, far, sems, 0)
-    return ring_sum_finish(parts, started, middle, far, near), started + middle
 
 
 def ring_gather_half(out, top, sems, base):
@@ -106,51 +100,6 @@
     return passed
 
 
-def second_norm_kernel(parts, tokens, gains, summed, unit, scale, normed, mid, sent, far, near, send, recv):
-    sems = (send, recv)
-    greet([at_y(1), at_y(3)])
-    finish, copies = ring_sum(parts, mid, sent, far, near, sems)
-    half = tokens.shape[0] // 2
-    halves = []
-    for top in range(2):
-        rows = pl.ds(top * half, half)
-        total = tokens[rows].astype(f32) + finish(top)
-        summed[rows] = total
-        centered = total - jnp.mean(total, -1, keepdims=True)
-        inverse = lax.rsqrt(jnp.mean(centered * centered, -1, keepdims=True) + EPSILON)
-        unit_rows = centered * inverse
-        unit[rows] = unit_rows
-        scale[rows] = inverse
-        normed[rows] = (unit_rows * gains[0:1] + gains[1:2]).astype(bf16)
-        halves.append(ring_gather_half(normed, top, sems, 6))
-    passed = ring_gather_pass(normed, halves, sems, 6)
-    for copy in passed + [halves[1][0], halves[0][1]]:
-        copy.wait_recv()
-    for copy in copies + halves[0] + halves[1] + passed:
-        copy.wait_send()
-
-
-def second_norm(parts, tokens, gains):
-    here, width = tokens.shape
-    half = here // 2
-    full = pl.BlockSpec(memory_space=VMEM)
-    return pl.pallas_call(
-        second_norm_kernel,
-        out_shape=(
-            jax.ShapeDtypeStruct((here, width), f32),
-            jax.ShapeDtypeStruct((here, width), f32),
-            jax.ShapeDtypeStruct((here, 1), f32),
-            jax.ShapeDtypeStruct((4 * here, width), bf16),
-        ),
-        in_specs=[full] * 3,
-        out_specs=(full,) * 4,
-        scratch_shapes=[VMEM((2, half, width), bf16)] * 4 + [DMA((12,)), DMA((12,))],
-        compiler_params=pltpu.CompilerParams(
-            collective_id=1, has_side_effects=True, vmem_limit_bytes=VMEM_LIMIT
-        ),
-    )(parts, tokens, gains)
-
-
 def pair_moves():
     yl, c = lax.axis_index("yl"), lax.axis_index("c")
     return {"yl": c, "c": yl}, {"yl": 1 - c, "c": yl}
@@ -188,186 +137,6 @@
         copy = remote(src, dst, sems, index, device)
         copy.wait_recv()
         copy.wait_send()
-
-
-def first_gather_kernel(
-    one_q, two_q, tokens, cotangent, one, two, token_rows, cot_rows,
-    pair_send, pair_recv, local_sem, y_send, y_recv, send, recv, core_send, core_recv,
-):
-    z, x = lax.axis_index("z"), lax.axis_index("x")
-    yl, c = lax.axis_index("yl"), lax.axis_index("c")
-    pair_sems, y_sems, sems, core_sems = (
-        (pair_send, pair_recv),
-        (y_send, y_recv),
-        (send, recv),
-        (core_send, core_recv),
-    )
-    rows = one_q.shape[1]
-    here = tokens.shape[0]
-    piece = rows // 2
-    same, cross = pair_moves()
-    token_rows[pl.ds(0, here)] = tokens[...]
-    cot_rows[pl.ds(0, here)] = cotangent[...]
-    greet(everyone_near())
-
-    def start_of(dz, dx, half):
-        return (((z + dz) % 4) * 4 + (x + dx) % 4) * 4 * rows + c * 2 * rows + half * rows
-
-    target = ((z * 4 + x) * 4 + yl * 2 + c) * rows
-    moves = [
-        (one_q.at[c], one.at[pl.ds(target, rows)], 0, same),
-        (one_q.at[1 - c], one.at[pl.ds(target, rows)], 1, cross),
-        (two_q.at[c], two.at[pl.ds(c * rows, rows)], 2, same),
-        (two_q.at[1 - c], two.at[pl.ds(c * rows, rows)], 3, cross),
-    ]
-
-    def launch(k):
-        src, dst, index, device = moves[k]
-        if device is same:
-            stay_or_go(src, dst, pair_sems, index, device, local_sem.at[index // 2])
-        else:
-            remote(src, dst, pair_sems, index, device).start()
-
-    def land(k):
-        src, dst, index, device = moves[k]
-        if device is same:
-            stay_or_go_wait(src, dst, pair_sems, index, device, local_sem.at[index // 2])
-        else:
-            copy = remote(src, dst, pair_sems, index, device)
-            copy.wait_recv()
-            copy.wait_send()
-
-    launch(0)
-    launch(1)
-    y_halves = {}
-    y_passed = {}
-    for top in range(2):
-        y_halves[0, top] = ring_gather_half(token_rows, top, y_sems, 0)
-    land(0)
-    land(1)
-
-    done = []
-
-    def index_of(half, df, dg, part):
-        return ((half * 4 + df % 4) * 4 + dg % 4) * 2 + part
-
-    def block(half, df, dg):
-        return start_of(df, dg, half) if half == 0 else start_of(dg, df, half)
-
-    def push(half, df, dg, axis, step, part):
-        along_z = (half == 0) == (axis == 0)
-        device = at_z(step) if along_z else at_x(step)
-        to = (df - step, dg) if axis == 0 else (df, dg - step)
-        rng = pl.ds(block(half, df, dg) + part * piece, piece)
-        copy = remote(one.at[rng], one.at[rng], sems, index_of(half, *to, part), device)
-        copy.start()
-        done.append(copy)
-
-    def arrived(half, df, dg, part):
-        rng = pl.ds(block(half, df, dg) + part * piece, piece)
-        remote(one.at[rng], one.at[rng], sems, index_of(half, df, dg, part), at_z(1)).wait_recv()
-
-    def to_sibling(half, df, dg):
-        rng = pl.ds(block(half, df, dg), rows)
-        copy = remote(
-            one.at[rng], one.at[rng], core_sems, (half * 4 + df % 4) * 4 + dg % 4, sibling()
-        )
-        copy.start()
-        done.append(copy)
-        core.append(copy)
-
-    core = []
-    for axis in range(2):
-        for half in range(2):
-            for part in range(2):
-                push(half, 0, 0, axis, 1, part)
-                push(half, 0, 0, axis, -1, 1 - part)
-    launch(2)
-    launch(3)
-    for half in range(2):
-        to_sibling(half, 0, 0)
-    for half in range(2):
-        arrived(half, 3, 0, 0)
-        push(half, 3, 0, 0, 1, 0)
-        arrived(half, 1, 0, 1)
-        push(half, 1, 0, 0, -1, 1)
-    for half in range(2):
-        arrived(half, 3, 0, 1)
-        arrived(half, 1, 0, 0)
-        for df in (3, 1):
-            for part in range(2):
-                push(half, df, 0, 1, 1, part)
-                push(half, df, 0, 1, -1, 1 - part)
-            to_sibling(half, df, 0)
-    y_passed[0] = ring_gather_pass(token_rows, [y_halves[0, 0], y_halves[0, 1]], y_sems, 0)
-    for top in range(2):
-        y_halves[1, top] = ring_gather_half(cot_rows, top, y_sems, 6)
-
-    def second_axis(df):
-        for half in range(2):
-            arrived(half, df, 3, 0)
-            push(half, df, 3, 1, 1, 0)
-            arrived(half, df, 1, 1)
-            push(half, df, 1, 1, -1, 1)
-        for half in range(2):
-            arrived(half, df, 3, 1)
-            to_sibling(half, df, 3)
-            arrived(half, df, 1, 0)
-            to_sibling(half, df, 1)
-
-    second_axis(0)
-    for half in range(2):
-        arrived(half, 2, 0, 0)
-        arrived(half, 2, 0, 1)
-        for part in range(2):
-            push(half, 2, 0, 1, 1, part)
-            push(half, 2, 0, 1, -1, 1 - part)
-        to_sibling(half, 2, 0)
-    second_axis(3)
-    second_axis(1)
-    y_passed[1] = ring_gather_pass(cot_rows, [y_halves[1, 0], y_halves[1, 1]], y_sems, 6)
-    second_axis(2)
-    for df in (0, 3, 1, 2):
-        for half in range(2):
-            for part in range(2):
-                arrived(half, df, 2, part)
-            to_sibling(half, df, 2)
-    land(2)
-    land(3)
-    for which in range(2):
-        for copy in y_passed[which] + [y_halves[which, 1][0], y_halves[which, 0][1]]:
-            copy.wait_recv()
-        for copy in y_passed[which] + y_halves[which, 0] + y_halves[which, 1]:
-            copy.wait_send()
-    for copy in core:
-        copy.wait_recv()
-    for copy in done:
-        copy.wait_send()
-
-
-def first_gather(one_q, two_q, tokens, cotangent):
-    rows = one_q.shape[1]
-    here, width = tokens.shape
-    anywhere = pl.BlockSpec(memory_space=pl.ANY)
-    full = pl.BlockSpec(memory_space=VMEM)
-    return pl.pallas_call(
-        first_gather_kernel,
-        out_shape=(
-            jax.ShapeDtypeStruct((64 * rows, one_q.shape[2]), bf16),
-            jax.ShapeDtypeStruct((2 * rows, two_q.shape[2]), bf16),
-            jax.ShapeDtypeStruct((4 * here, width), bf16),
-            jax.ShapeDtypeStruct((4 * here, width), bf16),
-        ),
-        in_specs=[full] * 4,
-        out_specs=(anywhere, anywhere, full, full),
-        scratch_shapes=[
-            DMA((4,)), DMA((4,)), DMA((2,)), DMA((12,)), DMA((12,)),
-            DMA((64,)), DMA((64,)), DMA((32,)), DMA((32,)),
-        ],
-        compiler_params=pltpu.CompilerParams(
-            collective_id=0, has_side_effects=True, vmem_limit_bytes=VMEM_LIMIT
-        ),
-    )(one_q, two_q, tokens, cotangent)
 
 
 def last_sum_kernel(
@@ -709,102 +478,6 @@
     bias[...] = total
 
 
-def attention_forward_kernel(token_rows, one, table, normed, stats, qkv, head_mix, parts, norm_table, bias):
-    here = token_rows.shape[0] // 4
-    hq = head_mix.shape[1]
-    read_extras(one, 4 * hq, norm_table, bias)
-
-    def norm_rows(k, _):
-        rng = pl.ds(pl.multiple_of(k * here, here), here)
-        values = token_rows[rng].astype(f32)
-        mean = jnp.mean(values, -1, keepdims=True)
-        centered = values - mean
-        inverse = lax.rsqrt(jnp.mean(centered * centered, -1, keepdims=True) + EPSILON)
-        stats[0, rng] = mean
-        stats[1, rng] = inverse
-        normed[rng] = (centered * inverse * norm_table[0:1] + norm_table[1:2]).astype(bf16)
-        return 0
-
-    lax.fori_loop(0, 4, norm_rows, 0)
-    wide = 256
-
-    def project(k, _):
-        cols = pl.ds(pl.multiple_of(k * wide, wide), wide)
-        value = dot(normed[...], one[:, cols], 1, 0)
-        shift = jnp.concatenate(
-            [bias[pl.ds(2 * k, 1)], bias[pl.ds(2 * k + 1, 1)]], 1
-        )
-        value = value + shift
-
-        @pl.when(k < 2 * hq // wide)
-        def _():
-            for place in range(4):
-                rng = pl.ds(place * here, here)
-                turn = table[pl.ds(pl.multiple_of(half_of_place(place) * here, here), here)]
-                for pair in range(wide // 128):
-                    qkv[rng, pl.ds(pl.multiple_of(k * wide + pair * 128, 128), 128)] = turn_heads(
-                        value[place * here : (place + 1) * here, pair * 128 : (pair + 1) * 128],
-                        turn,
-                        1.0,
-                    ).astype(bf16)
-
-        @pl.when(k >= 2 * hq // wide)
-        def _():
-            qkv[:, cols] = value.astype(bf16)
-
-        return 0
-
-    lax.fori_loop(0, 3 * hq // wide, project, 0)
-    for sequence in range(2):
-        mask = causal_mask(sequence, here)
-        rng = pl.ds(sequence * 2 * here, 2 * here)
-
-        def heads(k, _):
-            def pair(t):
-                return qkv[rng, pl.ds(pl.multiple_of(t * hq + k * 128, 128), 128)]
-
-            q, key, value = pair(0), pair(1), pair(2)
-            mixes = []
-            for head in range(2):
-                cut = slice(head * HEAD_DIM, (head + 1) * HEAD_DIM)
-                soft = soft_of(q[:, cut], key[:, cut], mask).astype(bf16)
-                mixes.append(dot(soft, value[:, cut], 1, 0))
-            head_mix[rng, pl.ds(pl.multiple_of(k * 128, 128), 128)] = jnp.concatenate(
-                mixes, 1
-            ).astype(bf16)
-            return 0
-
-        lax.fori_loop(0, hq // 128, heads, 0)
-
-    def out_project(k, _):
-        rng = pl.ds(pl.multiple_of(k * wide, wide), wide)
-        parts[:, rng] = dot(head_mix[...], one[rng, pl.ds(3 * hq, hq)], 1, 1).astype(bf16)
-        return 0
-
-    lax.fori_loop(0, one.shape[0] // wide, out_project, 0)
-
-
-def attention_forward(token_rows, one, table):
-    tokens, width = token_rows.shape
-    hq = (one.shape[1] - EXTRA) // 4
-    full = pl.BlockSpec(memory_space=VMEM)
-    return pl.pallas_call(
-        attention_forward_kernel,
-        out_shape=(
-            jax.ShapeDtypeStruct((tokens, width), bf16),
-            jax.ShapeDtypeStruct((2, tokens, 1), f32),
-            jax.ShapeDtypeStruct((tokens, 3 * hq), bf16),
-            jax.ShapeDtypeStruct((tokens, hq), bf16),
-            jax.ShapeDtypeStruct((tokens, width), bf16),
-            jax.ShapeDtypeStruct((4, width), f32),
-        ),
-        in_specs=[full] * 3,
-        out_specs=(full,) * 6,
-        scratch_shapes=[VMEM((12, 128), f32)],
-        compiler_params=pltpu.CompilerParams(vmem_limit_bytes=VMEM_LIMIT),
-    )(token_rows, one, table)
-
-
 def attention_backward_kernel(
     resid, one, normed, stats, qkv, head_mix, token_rows, table, second_terms,
     grads, first_parts, grad_mix, grad_proj,
@@ -1090,6 +763,383 @@
     )(normed, cot_rows, cotangent, unit, scale, gains, weights)
 
 
+def cube():
+    yl, c, yh = lax.axis_index("yl"), lax.axis_index("c"), lax.axis_index("yh")
+    return [
+        {"yl": (yl + a) % 2, "c": (c + b) % 2, "yh": (yh + d) % 2}
+        for a in range(2)
+        for b in range(2)
+        for d in range(2)
+        if a + b + d
+    ]
+
+
+class Spread:
+    def __init__(self, out, rows, sems, core_sems):
+        self.out, self.rows, self.sems, self.core_sems = out, rows, sems, core_sems
+        self.done, self.core = [], []
+
+    def cut(self, half, df, dg, part=None):
+        z, x = lax.axis_index("z"), lax.axis_index("x")
+        dz, dx = (df, dg) if half == 0 else (dg, df)
+        place = ((z + dz) % 4) * 4 + (x + dx) % 4
+        start = (place * 4 + lax.axis_index("c") * 2 + half) * self.rows
+        piece = self.rows // 2
+        if part is None:
+            return self.out.at[pl.ds(pl.multiple_of(start, self.rows), self.rows)]
+        return self.out.at[pl.ds(pl.multiple_of(start + part * piece, piece), piece)]
+
+    def index(self, half, df, dg, part):
+        return ((half * 4 + df % 4) * 4 + dg % 4) * 2 + part
+
+    def push(self, half, df, dg, axis, step, part):
+        device = at_z(step) if (half == 0) == (axis == 0) else at_x(step)
+        to = (df - step, dg) if axis == 0 else (df, dg - step)
+        ref = self.cut(half, df, dg, part)
+        copy = remote(ref, ref, self.sems, self.index(half, *to, part), device)
+        copy.start()
+        self.done.append(copy)
+
+    def arrived(self, half, df, dg, part):
+        ref = self.cut(half, df, dg, part)
+        remote(ref, ref, self.sems, self.index(half, df, dg, part), at_z(1)).wait_recv()
+
+    def to_sibling(self, half, df, dg):
+        ref = self.cut(half, df, dg)
+        copy = remote(ref, ref, self.core_sems, (half * 4 + df % 4) * 4 + dg % 4, sibling())
+        copy.start()
+        self.done.append(copy)
+        self.core.append(copy)
+
+    def push_all(self, half, df, dg, axis):
+        for part in range(2):
+            self.push(half, df, dg, axis, 1, part)
+            self.push(half, df, dg, axis, -1, 1 - part)
+
+    def start(self):
+        for axis in range(2):
+            for half in range(2):
+                self.push_all(half, 0, 0, axis)
+        for half in range(2):
+            self.to_sibling(half, 0, 0)
+
+    def first_pass(self):
+        for half in range(2):
+            self.arrived(half, 3, 0, 0)
+            self.push(half, 3, 0, 0, 1, 0)
+            self.arrived(half, 1, 0, 1)
+            self.push(half, 1, 0, 0, -1, 1)
+
+    def first_rest(self):
+        for half in range(2):
+            self.arrived(half, 3, 0, 1)
+            self.arrived(half, 1, 0, 0)
+            for df in (3, 1):
+                self.push_all(half, df, 0, 1)
+                self.to_sibling(half, df, 0)
+
+    def first_far(self):
+        for half in range(2):
+            self.arrived(half, 2, 0, 0)
+            self.arrived(half, 2, 0, 1)
+            self.push_all(half, 2, 0, 1)
+            self.to_sibling(half, 2, 0)
+
+    def second_pass(self, df):
+        for half in range(2):
+            self.arrived(half, df, 3, 0)
+            self.push(half, df, 3, 1, 1, 0)
+            self.arrived(half, df, 1, 1)
+            self.push(half, df, 1, 1, -1, 1)
+        for half in range(2):
+            self.arrived(half, df, 3, 1)
+            self.to_sibling(half, df, 3)
+            self.arrived(half, df, 1, 0)
+            self.to_sibling(half, df, 1)
+
+    def second_far(self, df):
+        for half in range(2):
+            for part in range(2):
+                self.arrived(half, df, 2, part)
+            self.to_sibling(half, df, 2)
+
+    def land(self):
+        for copy in self.core:
+            copy.wait_recv()
+
+    def close(self):
+        for copy in self.done:
+            copy.wait_send()
+
+
+def forward_kernel(
+    qkv_weight, out_weight, gate_up_weight, down_weight, extra, tokens, cotangent, table,
+    one_out, two, token_rows, cot_rows, normed, stats, qkv, head_mix, norm_table,
+    summed, unit, scale, normed_two,
+    one_q, two_q, one, norm_in, bias, parts, mid, sent, far, near,
+    pair_send, pair_recv, local_sem, y_send, y_recv,
+    send_one, recv_one, core_send_one, core_recv_one,
+    send_two, recv_two, core_send_two, core_recv_two,
+):
+    z, x = lax.axis_index("z"), lax.axis_index("x")
+    yl, c, yh = lax.axis_index("yl"), lax.axis_index("c"), lax.axis_index("yh")
+    rows, here = one_q.shape[1], tokens.shape[0]
+    hq, fq = qkv_weight.shape[2] // 2, gate_up_weight.shape[2] // 2
+    pair_sems, y_sems = (pair_send, pair_recv), (y_send, y_recv)
+    for q in range(2):
+        for t in range(3):
+            one_q[q, :, t * hq : (t + 1) * hq] = qkv_weight[t, :, q * hq : (q + 1) * hq]
+        one_q[q, :, 3 * hq : 4 * hq] = out_weight[:, q * hq : (q + 1) * hq]
+        one_q[q, :, 4 * hq :] = extra[q]
+    token_rows[pl.ds(0, here)] = tokens[...]
+    greet([at_z(1), at_z(3), at_x(1), at_x(3)] + cube())
+
+    same, cross = pair_moves()
+    mine = pl.ds(pl.multiple_of((z * 4 + x) * 4 * rows + (yl * 2 + c) * rows, rows), rows)
+    moves = [
+        (one_q.at[c], one.at[mine], 0, same),
+        (one_q.at[1 - c], one.at[mine], 1, cross),
+        (two_q.at[c], two.at[mine], 2, same),
+        (two_q.at[1 - c], two.at[mine], 3, cross),
+    ]
+
+    def launch(k):
+        src, dst, index, device = moves[k]
+        if device is same:
+            stay_or_go(src, dst, pair_sems, index, device, local_sem.at[index // 2])
+        else:
+            remote(src, dst, pair_sems, index, device).start()
+
+    def land(k):
+        src, dst, index, device = moves[k]
+        if device is same:
+            stay_or_go_wait(src, dst, pair_sems, index, device, local_sem.at[index // 2])
+        else:
+            copy = remote(src, dst, pair_sems, index, device)
+            copy.wait_recv()
+            copy.wait_send()
+
+    norm_moves = [
+        remote(
+            one_q.at[0, :, pl.ds(4 * hq, EXTRA)],
+            norm_in.at[c],
+            pair_sems,
+            4 + which,
+            {"yl": target["yl"], "c": target["c"], "yh": 1 - yh},
+        )
+        for which, target in enumerate((same, cross))
+    ]
+    launch(0)
+    launch(1)
+    for move in norm_moves:
+        move.start()
+    token_halves = [ring_gather_half(token_rows, top, y_sems, 0) for top in range(2)]
+    for q in range(2):
+        for t in range(2):
+            two_q[q, :, t * fq : (t + 1) * fq] = gate_up_weight[t, :, q * fq : (q + 1) * fq]
+        two_q[q, :, 2 * fq :] = down_weight[:, q * fq : (q + 1) * fq]
+    cot_rows[pl.ds(0, here)] = cotangent[...]
+    land(0)
+    land(1)
+    for move in norm_moves:
+        move.wait_recv()
+    own = (z * 4 + x) * 4 + 2 * c
+    for core in range(2):
+        block = pl.ds(pl.multiple_of((own + core) * rows, rows), rows)
+        came = norm_in[core].astype(f32)
+        place = lax.broadcasted_iota(jnp.int32, came.shape, 0)
+        held = one[block, pl.ds(4 * hq, EXTRA)].astype(f32)
+        one[block, pl.ds(4 * hq, EXTRA)] = (
+            held + jnp.where((place >= 12) & (place < 20), came, 0.0)
+        ).astype(bf16)
+    first = Spread(one, rows, (send_one, recv_one), (core_send_one, core_recv_one))
+    second = Spread(two, rows, (send_two, recv_two), (core_send_two, core_recv_two))
+    first.start()
+    launch(2)
+    launch(3)
+    first.first_pass()
+    first.first_rest()
+    token_passed = ring_gather_pass(token_rows, token_halves, y_sems, 0)
+    first.second_pass(0)
+    first.first_far()
+    first.second_pass(3)
+    first.second_pass(1)
+    land(2)
+    land(3)
+    second.start()
+    first.second_pass(2)
+    for df in (0, 3, 1, 2):
+        first.second_far(df)
+    for copy in token_passed + [token_halves[1][0], token_halves[0][1]]:
+        copy.wait_recv()
+    cot_halves = [ring_gather_half(cot_rows, top, y_sems, 6) for top in range(2)]
+    first.land()
+    keep = pltpu.make_async_copy(one, one_out, local_sem.at[2])
+    keep.start()
+
+    read_extras(one, 4 * hq, norm_table, bias)
+
+    def norm_rows(k, _):
+        rng = pl.ds(pl.multiple_of(k * here, here), here)
+        values = token_rows[rng].astype(f32)
+        mean = jnp.mean(values, -1, keepdims=True)
+        centered = values - mean
+        inverse = lax.rsqrt(jnp.mean(centered * centered, -1, keepdims=True) + EPSILON)
+        stats[0, rng] = mean
+        stats[1, rng] = inverse
+        normed[rng] = (centered * inverse * norm_table[0:1] + norm_table[1:2]).astype(bf16)
+        return 0
+
+    lax.fori_loop(0, 4, norm_rows, 0)
+    second.first_pass()
+    wide = 256
+
+    def project(k, _):
+        cols = pl.ds(pl.multiple_of(k * wide, wide), wide)
+        value = dot(normed[...], one[:, cols], 1, 0)
+        value = value + jnp.concatenate([bias[pl.ds(2 * k, 1)], bias[pl.ds(2 * k + 1, 1)]], 1)
+
+        @pl.when(k < 2 * hq // wide)
+        def _():
+            for place in range(4):
+                rng = pl.ds(place * here, here)
+                turn = table[pl.ds(pl.multiple_of(half_of_place(place) * here, here), here)]
+                for pair in range(wide // 128):
+                    qkv[rng, pl.ds(pl.multiple_of(k * wide + pair * 128, 128), 128)] = turn_heads(
+                        value[place * here : (place + 1) * here, pair * 128 : (pair + 1) * 128],
+                        turn,
+                        1.0,
+                    ).astype(bf16)
+
+        @pl.when(k >= 2 * hq // wide)
+        def _():
+            qkv[:, cols] = value.astype(bf16)
+
+        return 0
+
+    lax.fori_loop(0, 3 * hq // wide, project, 0)
+    second.first_rest()
+    cot_passed = ring_gather_pass(cot_rows, cot_halves, y_sems, 6)
+    for sequence in range(2):
+        mask = causal_mask(sequence, here)
+        rng = pl.ds(sequence * 2 * here, 2 * here)
+
+        def heads(k, _):
+            def pair(t):
+                return qkv[rng, pl.ds(pl.multiple_of(t * hq + k * 128, 128), 128)]
+
+            q, key, value = pair(0), pair(1), pair(2)
+            mixes = []
+            for head in range(2):
+                cut = slice(head * HEAD_DIM, (head + 1) * HEAD_DIM)
+                soft = soft_of(q[:, cut], key[:, cut], mask).astype(bf16)
+                mixes.append(dot(soft, value[:, cut], 1, 0))
+            head_mix[rng, pl.ds(pl.multiple_of(k * 128, 128), 128)] = jnp.concatenate(
+                mixes, 1
+            ).astype(bf16)
+            return 0
+
+        lax.fori_loop(0, hq // 128, heads, 0, unroll=2)
+        if sequence == 0:
+            second.second_pass(0)
+    second.first_far()
+
+    def out_project(k, _):
+        rng = pl.ds(pl.multiple_of(k * wide, wide), wide)
+        parts[:, rng] = dot(head_mix[...], one[rng, pl.ds(3 * hq, hq)], 1, 1).astype(bf16)
+        return 0
+
+    lax.fori_loop(0, one.shape[0] // wide, out_project, 0)
+    for copy in cot_passed + [cot_halves[1][0], cot_halves[0][1]]:
+        copy.wait_recv()
+
+    started = ring_sum_start(parts, mid, near, y_sems, 12)
+    second.second_pass(3)
+    middle = ring_sum_middle(parts, started, mid, sent, far, y_sems, 12)
+    second.second_pass(1)
+    finish = ring_sum_finish(parts, started, middle, far, near)
+    half = here // 2
+    halves = []
+    for top in range(2):
+        rng = pl.ds(top * half, half)
+        total = tokens[rng].astype(f32) + finish(top)
+        summed[rng] = total
+        centered = total - jnp.mean(total, -1, keepdims=True)
+        inverse = lax.rsqrt(jnp.mean(centered * centered, -1, keepdims=True) + EPSILON)
+        unit_rows = centered * inverse
+        unit[rng] = unit_rows
+        scale[rng] = inverse
+        normed_two[rng] = (unit_rows * norm_table[2:3] + norm_table[3:4]).astype(bf16)
+        halves.append(ring_gather_half(normed_two, top, y_sems, 18))
+    second.second_pass(2)
+    passed = ring_gather_pass(normed_two, halves, y_sems, 18)
+    for df in (0, 3, 1, 2):
+        second.second_far(df)
+    for copy in passed + [halves[1][0], halves[0][1]]:
+        copy.wait_recv()
+    second.land()
+    keep.wait()
+    for move in norm_moves:
+        move.wait_send()
+    for copies in token_halves + cot_halves + halves + [
+        token_passed, cot_passed, started, middle, passed
+    ]:
+        for copy in copies:
+            copy.wait_send()
+    first.close()
+    second.close()
+
+
+def forward(qkv_weight, out_weight, gate_up_weight, down_weight, extra, tokens, cotangent, table):
+    here, width = tokens.shape
+    rows = qkv_weight.shape[1]
+    hq, fq = qkv_weight.shape[2] // 2, gate_up_weight.shape[2] // 2
+    full = pl.BlockSpec(memory_space=VMEM)
+    anywhere = pl.BlockSpec(memory_space=pl.ANY)
+    one_wide, two_wide = 4 * hq + EXTRA, 3 * fq
+
+    def shape(*dims, dtype=bf16):
+        return jax.ShapeDtypeStruct(dims, dtype)
+
+    return pl.pallas_call(
+        forward_kernel,
+        out_shape=(
+            shape(width, one_wide),
+            shape(width, two_wide),
+            shape(4 * here, width),
+            shape(4 * here, width),
+            shape(4 * here, width),
+            shape(2, 4 * here, 1, dtype=f32),
+            shape(4 * here, 3 * hq),
+            shape(4 * here, hq),
+            shape(4, width, dtype=f32),
+            shape(here, width, dtype=f32),
+            shape(here, width, dtype=f32),
+            shape(here, 1, dtype=f32),
+            shape(4 * here, width),
+        ),
+        in_specs=[full] * 8,
+        out_specs=(anywhere, anywhere) + (full,) * 11,
+        scratch_shapes=[
+            VMEM((2, rows, one_wide), bf16),
+            VMEM((2, rows, two_wide), bf16),
+            VMEM((width, one_wide), bf16),
+            VMEM((2, rows, EXTRA), bf16),
+            VMEM((12, 128), f32),
+            VMEM((4 * here, width), bf16),
+        ]
+        + [VMEM((2, here // 2, width), bf16)] * 4
+        + [
+            DMA((6,)), DMA((6,)), DMA((3,)), DMA((24,)), DMA((24,)),
+            DMA((64,)), DMA((64,)), DMA((32,)), DMA((32,)),
+            DMA((64,)), DMA((64,)), DMA((32,)), DMA((32,)),
+        ],
+        compiler_params=pltpu.CompilerParams(
+            collective_id=0, has_side_effects=True, vmem_limit_bytes=VMEM_LIMIT
+        ),
+    )(qkv_weight, out_weight, gate_up_weight, down_weight, extra, tokens, cotangent, table)
+
+
 SAME = [(0, 0), (1, 2), (2, 1), (3, 3)]
 CROSS = [(0, 2), (1, 0), (2, 3), (3, 1)]
 
@@ -1119,27 +1169,17 @@
     heads = hq // HEAD_DIM
     pairs = 3 * heads // 2
 
-    qkv_q = qkv_weight.reshape(3, rows, 2, hq).transpose(2, 1, 0, 3).reshape(2, rows, 3 * hq)
-    out_q = out_weight.T.reshape(rows, 2, hq).transpose(1, 0, 2)
-    gu_q = gate_up_weight.reshape(2, rows, 2, fq).transpose(2, 1, 0, 3).reshape(2, rows, 2 * fq)
-    down_q = down_weight.T.reshape(rows, 2, fq).transpose(1, 0, 2)
-    other = lax.ppermute(norm_params, "yh", [(0, 1), (1, 0)])
-    norm_rows = jnp.where(
-        yh == 0,
-        jnp.concatenate([norm_params, other], 1),
-        jnp.concatenate([other, norm_params], 1),
-    )
-    norm_high = lax.optimization_barrier(norm_rows.astype(bf16))
-    norm_low = (norm_rows - norm_high.astype(f32)).astype(bf16)
-    lanes = jnp.arange(EXTRA)
+    norm_high = lax.optimization_barrier(norm_params.astype(bf16))
+    norm_low = (norm_params - norm_high.astype(f32)).astype(bf16)
+    share = norm_params.shape[1]
     norm_extra = jnp.where(
-        lanes // rows == mine % 4,
-        jnp.tile(jnp.concatenate([norm_high, norm_low], 0), (1, EXTRA // rows)),
+        jnp.arange(EXTRA) // share == mine % 4 * 2 + yh,
+        jnp.tile(jnp.concatenate([norm_high, norm_low], 0), (1, EXTRA // share)),
         0,
     )
     bias_q = qkv_bias.reshape(3, 2, heads).transpose(1, 0, 2).reshape(2, pairs, 2, 1)
     bias_extra = jnp.where(jnp.arange(HEAD_DIM) == mine, bias_q, 0).reshape(2, pairs, EXTRA)
-    extra_q = jnp.concatenate(
+    extra = jnp.concatenate(
         [
             bias_extra,
             jnp.broadcast_to(norm_extra[None], (2, *norm_extra.shape)),
@@ -1147,18 +1187,13 @@
         ],
         1,
     )
-    one, second, token_rows, cot_rows = first_gather(
-        jnp.concatenate([qkv_q, out_q, extra_q], axis=2),
-        jnp.concatenate([gu_q, down_q], axis=2),
-        tokens,
-        cotangent,
-    )
-    second = lax.all_gather(second, ("z", "x", "c"), axis=0, tiled=True)
     table = jnp.asarray(tables())
-    normed_one, stats, qkv, head_mix, parts, norm_table = attention_forward(
-        token_rows, one, table
-    )
-    first_sum, unit_two, scale_two, normed_two = second_norm(parts, tokens, norm_table[2:])
+    (
+        one, second, token_rows, cot_rows, normed_one, stats, qkv, head_mix, norm_table,
+        first_sum, unit_two, scale_two, normed_two,
+    ) = forward(
+        qkv_weight, out_weight.T, gate_up_weight, down_weight.T, extra, tokens, cotangent, table
+    )
     grad_resid, second_terms, resid_rows, mixed_parts, chip = feed_forward(
         normed_two, cot_rows, cotangent, unit_two, scale_two, norm_table[2:], second
     )

time: 335 us -> 319 us (0.952)
  Pallas kernels: 286 us -> 278 us
  starting transfers between devices: 7.21 us -> 3.01 us
    pallas_call x3 -> x1, Pallas kernels: 125 us -> 117 us  [forward(): pl.pallas_call(forward_kernel, out_shape=(shape(width, one_wide), shape(w...]
    ppermute x1 -> x0, starting transfers between devices: 3.36 us -> none  [shards(): other = lax.ppermute(norm_params, 'yh', [(0, 1), (1, 0)])]
  transfers between devices with their start and end apart: 6 -> 4, of which waited for: 2 -> 1; matrix products, arithmetic and copies ran while one was open for 4% -> 2% of each run, Pallas kernels for 49% -> 30%
where the time goes in v4:
time: 319 us; the launch traced here: 318 us
  Pallas kernels  278 us (87%)
  between operations  14.3 us (4%)
  local copies, waits for them, and re-layouts  12.5 us (4%)
  other arithmetic  5.27 us (2%)
  waiting for transfers between devices  4.93 us (2%)
    pallas_call x1, Pallas kernels, forward(): pl.pallas_call(forward_kernel, out_shape=(shape(width, one_wide), shape(w...  117 us
    pallas_call x1, Pallas kernels, feed_forward(): pl.pallas_call(feed_forward_kernel, out_shape=(jax.ShapeDtypeStruct((here...  64.7 us
    pallas_call x1, Pallas kernels, last_sum(): pl.pallas_call(last_sum_kernel, out_shape=(jax.ShapeDtypeStruct((2, rows,...  61.2 us
    pallas_call x1, Pallas kernels, attention_backward(): pl.pallas_call(attention_backward_kernel, out_shape=(jax.ShapeDtypeStruct...  35.3 us
  transfers between devices with their start and end apart: 4, of which 1 were waited for; matrix products, arithmetic and copies ran while one was open for 2% of the time, Pallas kernels for 30%

profile of v4, /device:TPU:0, one launch (start us, length us, event | category | flops | bytes accessed | tf_op | source)
XLA Modules:
  0.0 318.4 jit_solution(12632005311649678858)
XLA Ops:
  7.2 0.0 reduce-scatter.2.cloned.1.call-start
  7.3 0.7 convert_element_type.58
  8.0 0.7 subtract_convert_fusion
  8.7 0.1 tile.10
  8.8 0.1 broadcast_in_dim.40
  8.9 0.8 reshape.92
  9.6 0.1 broadcast_in_dim.42
  9.7 0.1 broadcast_in_dim.43
  9.8 0.1 broadcast_in_dim.44
  10.0 0.6 pad_maximum_fusion.1.extra
  10.6 117.2 %shard_map.152 = (bf16[2048,2176]{1,0:T(8,128)(2,1)}, bf16[2048,4224]{1,0:T(8,128)(2,1)}, bf16[512,2048]{1,0:T(8,128)(2,1)}, bf16[512,2048]{1,0:T(8,128)(2,1)}, ...) custom-call(bf16[3,32,1024]{2,1,0:T(8,128)(2,1)} %qkv_weight.1, ...), custom_call_target="tpu_custom_call" | custom-call | tf_op jit(solution)/shard_map/pallas_call | solution.py:1104
  127.8 1.5 fusion.4
  129.3 64.7 %shard_map.153 = (f32[128,2048]{1,0:T(8,128)}, f32[2,2048]{1,0:T(2,128)}, bf16[512,2048]{1,0:T(8,128)(2,1)}, bf16[512,2048]{1,0:T(8,128)(2,1)}, bf16[16,64,4224]{2,1,0:T(8,128)(2,1)}) custom-call(bf16[512,2048]{1,0:T(8,128)(2,1)} %get-tuple-element.31.normed, bf16[512,2048]{1,0:T(8,128)(2,1)} %get-tuple-element.32.cot_rows, bf16[128,2048]{1,0:T(8,128)(2,1)} %cotangent.3, ...), custom_call_target="tpu_custom_call" | custom-call | tf_op jit(solution)/shard_map/pallas_call | solution.py:738
  194.0 0.0 reduce-scatter.2.cloned.1.call-update
  194.0 35.3 %shard_map.154 = (bf16[2048,2176]{1,0:T(8,128)(2,1)}, bf16[512,2048]{1,0:T(8,128)(2,1)}) custom-call(bf16[512,2048]{1,0:T(8,128)(2,1)} %get-tuple-element.37.resid, bf16[2048,2176]{1,0:T(8,128)(2,1)} %get-tuple-element.38.one, bf16[512,2048]{1,0:T(8,128)(2,1)} %get-tuple-element.39.normed, f32[2,512,1]{2,1,0:T(8,128)} %get-tuple-element.40.stats, ...), custom_call_target="tpu_custom_call" | custom-call | tf_op jit(solution)/shard_map/pallas_call | solution.py:579
  229.4 61.2 %shard_map.155 = (bf16[2,32,2176]{2,1,0:T(8,128)(2,1)}, f32[128,2048]{1,0:T(8,128)}, bf16[128,2048]{1,0:T(8,128)(2,1)}) custom-call(bf16[2048,2176]{1,0:T(8,128)(2,1)} %get-tuple-element.45.grads, bf16[512,2048]{1,0:T(8,128)(2,1)} %get-tuple-element.46.first_parts, bf16[512,2048]{1,0:T(8,128)(2,1)} %get-tuple-element.47.mixed_parts, ...), custom_call_target="tpu_custom_call" | custom-call | tf_op jit(solution)/shard_map/pallas_call | solution.py:386
  290.6 0.7 slice_convert_fusion.1
  291.3 0.1 reshape.93
  291.4 0.1 reshape.94
  291.5 1.9 collective-permute-start
  293.4 1.0 slice_convert_fusion
  294.4 0.3 reshape.104
  294.7 0.3 copy.39
  295.0 1.1 reshape.100
  296.1 0.0 reduce-scatter.2.cloned.1.call-done
  296.1 1.1 dynamic-slice_bitcast_fusion
  297.2 0.7 collective-permute-start.1
  297.8 0.4 collective-permute-start.2
  298.2 0.8 convert_bitcast_fusion.1
  299.1 0.7 copy.48
  299.7 0.1 reshape.95
  299.8 0.1 constant_dynamic-slice_fusion
  299.9 0.3 copy.41
  300.2 0.1 reshape.96
  300.3 0.7 reshape.106
  301.0 0.0 collective-permute-done
  301.0 0.6 add.60
  301.6 0.0 collective-permute-done.1
  301.6 4.9 %collective-permute-done.2 = bf16[32,4224]{1,0:T(8,128)(2,1)S(1)} collective-permute-done((bf16[32,4224]{1,0:T(8,128)(2,1)S(1)}, bf16[32,4224]{1,0:T(8,128)(2,1)S(1)}, u32[]{:S(2)}, u32[]{:S(2)}) %collective-permute-start.2) | collective-permute-done | bytes 270368 | tf_op jit(solution)/shard_map/ppermute | solution.py:1153
  306.5 0.1 select_bitcast_fusion
  306.6 0.1 fusion.1
  306.6 0.8 copy.49
  307.4 0.0 copy-start.1
  307.4 0.4 reshape.105
  307.8 0.0 copy-start
  307.8 0.6 copy.44
  308.4 1.4 reshape.102
  309.8 0.0 copy-done.1
  309.8 0.8 copy.53
  310.6 0.0 copy-done
  310.6 1.0 copy.54
  (19 shorter events, 0.1 us)
Async XLA Ops:
  7.2 288.9 %reduce-scatter.2.cloned.1.call-start = ((), (), s32[]{:S(2)}) async-start(), calls=%async_computation.1 | async-start | bytes 9191424 | tf_op jit(solution)/shard_map/reduce_scatter | solution.py:1200
  291.5 9.5 %collective-permute-start = (f32[4,16]{1,0:T(4,128)S(1)}, f32[4,16]{1,0:T(4,128)S(1)}, u32[]{:S(2)}, u32[]{:S(2)}) collective-permute-start(f32[4,16]{1,0:T(4,128)S(1)} %bitcast.49), channel_id=1, source_target_pairs={{0,1},{1,0},{2,3},{3,2},{4,5},{5,4},{6,7},{7,6},{8,9},{9,8},{10,11... | collective-permute-start | bytes 776 | tf_op jit(solution)/shard_map/ppermute | solution.py:1243
  297.2 4.4 %collective-permute-start.1 = (bf16[32,4224]{1,0:T(8,128)(2,1)S(1)}, bf16[32,4224]{1,0:T(8,128)(2,1)S(1)}, u32[]{:S(2)}, u32[]{:S(2)}) collective-permute-start(bf16[32,4224]{1,0:T(8,128)(2,1)S(1)} %get-tuple-element.81), channel_id=1, source_target_pairs={{0,0},{4,2},{2,4},{6,6},{1,1},{5,3},{3,5},{7,7},{8,8},{12,10},{10,... | collective-permute-start | bytes 811016 | tf_op jit(solution)/shard_map/ppermute | solution.py:1150
  297.8 8.6 %collective-permute-start.2 = (bf16[32,4224]{1,0:T(8,128)(2,1)S(1)}, bf16[32,4224]{1,0:T(8,128)(2,1)S(1)}, u32[]{:S(2)}, u32[]{:S(2)}) collective-permute-start(bf16[32,4224]{1,0:T(8,128)(2,1)S(1)} %get-tuple-element.80), channel_id=1, source_target_pairs={{4,0},{0,2},{6,4},{2,6},{5,1},{1,3},{7,5},{3,7},{12,8},{8,10},{14,... | collective-permute-start | bytes 811016 | tf_op jit(solution)/shard_map/ppermute | solution.py:1153
  307.4 2.4 copy-start.1
  307.8 2.8 copy-start
Sparse Core Ops, SparseCore 0:
  194.2 92.5 reduce-scatter.1

commit v5 on v4

--- a/solution.py
+++ b/solution.py
@@ -1,5 +1,3 @@
-import functools
-
 import jax
 import jax.numpy as jnp
 import numpy as np
@@ -105,14 +103,6 @@
     return {"yl": c, "c": yl}, {"yl": 1 - c, "c": yl}
 
 
-def diagonal():
-    return {"yl": 1 - lax.axis_index("yl"), "c": 1 - lax.axis_index("c")}
-
-
-def everyone_near():
-    return [at_z(1), at_z(3), at_x(1), at_x(3), at_y(1), at_y(3), sibling(), diagonal()]
-
-
 def stay_or_go(src, dst, sems, index, device, local_sem):
     yl, c = lax.axis_index("yl"), lax.axis_index("c")
 
@@ -136,190 +126,6 @@
     def _():
         copy = remote(src, dst, sems, index, device)
         copy.wait_recv()
-        copy.wait_send()
-
-
-def last_sum_kernel(
-    grads, first_parts, mixed_parts, resid, tokens, stats, gains, first_sum,
-    result, grad_tokens, mixed,
-    sib, mid, sent, far, near, stage, mid2, sent2, far2, near2, packed,
-    ymid, ysent, yfar, ynear,
-    core_send, core_recv, send, recv, send2, recv2, pair_send, pair_recv, local_sem, y_send, y_recv,
-):
-    z, x = lax.axis_index("z"), lax.axis_index("x")
-    yl, c = lax.axis_index("yl"), lax.axis_index("c")
-    core_sems, sems, sems2, pair_sems, y_sems = (
-        (core_send, core_recv),
-        (send, recv),
-        (send2, recv2),
-        (pair_send, pair_recv),
-        (y_send, y_recv),
-    )
-    rows = result.shape[1]
-    piece = rows // 2
-    greet(everyone_near())
-    done = []
-
-    def begin(copy):
-        copy.start()
-        done.append(copy)
-        return copy
-
-    def start_of(dz, dx, core):
-        return (((z + dz) % 4) * 4 + (x + dx) % 4) * 4 * rows + core * 2 * rows
-
-    order = []
-    for d in (2, 1, 3, 0):
-        for e in (2, 1, 3, 0):
-            for pair in ((d, e), (e, d)):
-                if pair not in order:
-                    order.append(pair)
-    core = {}
-    for dz, dx in order:
-        core[dz, dx] = begin(
-            remote(
-                grads.at[pl.ds(start_of(dz, dx, 1 - c), 2 * rows)],
-                sib.at[dz, dx],
-                core_sems,
-                dz * 4 + dx,
-                sibling(),
-            )
-        )
-    y_jobs = [
-        ring_sum_start(first_parts, ymid.at[0], ynear.at[0], y_sems, 0),
-        ring_sum_start(mixed_parts, ymid.at[1], ynear.at[1], y_sems, 6),
-    ]
-    summed = set()
-
-    def core_sum(dz, dx):
-        if (dz, dx) in summed:
-            return
-        summed.add((dz, dx))
-        core[dz, dx].wait_recv()
-        sib[dz, dx] = (
-            sib[dz, dx].astype(f32)
-            + grads[pl.ds(start_of(dz, dx, c), 2 * rows)].astype(f32)
-        ).astype(bf16)
-
-    def view(half, df, part):
-        rng = pl.ds(half * rows + part * piece, piece)
-        return sib.at[df, :, rng] if half == 0 else sib.at[:, df, rng]
-
-    def device(half, axis, step):
-        return at_z(step) if (half == 0) == (axis == 0) else at_x(step)
-
-    def ring_first(half, axis, src, mids, nears, some_sems):
-        base = half * 6
-        got = {}
-        for way, step in ((0, 1), (1, -1)):
-            got["first", way] = begin(
-                remote(src(2, way), mids.at[half, way], some_sems, base + way, device(half, axis, step))
-            )
-        return got
-
-    def ring_second(half, axis, src, nears, some_sems, got):
-        base = half * 6
-        for way, step in ((0, 1), (1, -1)):
-            got["second", way] = begin(
-                remote(
-                    src(step % 4, 1 - way), nears.at[half, way], some_sems, base + 2 + way,
-                    device(half, axis, step),
-                )
-            )
-
-    def ring_third(half, axis, src, mids, sents, fars, some_sems, got):
-        base = half * 6
-        for way, step in ((0, 1), (1, -1)):
-            got["first", way].wait_recv()
-            sents[half, way] = (
-                src(step % 4, way)[...].astype(f32) + mids[half, way].astype(f32)
-            ).astype(bf16)
-            got["third", way] = begin(
-                remote(
-                    sents.at[half, way], fars.at[half, way], some_sems, base + 4 + way,
-                    device(half, axis, step),
-                )
-            )
-
-    def ring_last(half, part, src, fars, nears, got):
-        got["third", part].wait_recv()
-        got["second", 1 - part].wait_recv()
-        return (
-            src(0, part)[...].astype(f32)
-            + fars[half, part].astype(f32)
-            + nears[half, 1 - part].astype(f32)
-        )
-
-    got = {}
-    sources = [functools.partial(view, half) for half in range(2)]
-    for half in range(2):
-        for d in (2, 1, 3, 0):
-            core_sum(*((2, d) if half == 0 else (d, 2)))
-        got[half] = ring_first(half, 0, sources[half], mid, near, sems)
-    for half in range(2):
-        for step in (1, 3):
-            for d in (2, 1, 3, 0):
-                core_sum(*((step, d) if half == 0 else (d, step)))
-        ring_second(half, 0, sources[half], near, sems, got[half])
-    y_more = [
-        ring_sum_middle(first_parts, y_jobs[0], ymid.at[0], ysent.at[0], yfar.at[0], y_sems, 0)
-    ]
-    for half in range(2):
-        ring_third(half, 0, sources[half], mid, sent, far, sems, got[half])
-    core_sum(0, 0)
-    y_more.append(
-        ring_sum_middle(mixed_parts, y_jobs[1], ymid.at[1], ysent.at[1], yfar.at[1], y_sems, 6)
-    )
-    finish = ring_sum_finish(first_parts, y_jobs[0], y_more[0], yfar.at[0], ynear.at[0])
-    here = grad_tokens.shape[0] // 2
-    for top in range(2):
-        rng = pl.ds(top * here, here)
-        incoming = finish(top) * gains[0:1]
-        inverse = stats[1, rng]
-        unit_rows = (tokens[rng].astype(f32) - stats[0, rng]) * inverse
-        grad_tokens[rng] = resid[rng] + inverse * (
-            incoming
-            - jnp.mean(incoming, -1, keepdims=True)
-            - unit_rows * jnp.mean(incoming * unit_rows, -1, keepdims=True)
-        )
-    for half in range(2):
-        for part in range(2):
-            stage[half, :, part * piece : (part + 1) * piece] = ring_last(
-                half, part, sources[half], far, near, got[half]
-            ).astype(bf16)
-
-    def stage_view(half, dg, part):
-        return stage.at[half, dg, pl.ds(part * piece, piece)]
-
-    sources = [functools.partial(stage_view, half) for half in range(2)]
-    got = {}
-    for half in range(2):
-        got[half] = ring_first(half, 1, sources[half], mid2, near2, sems2)
-    for half in range(2):
-        ring_second(half, 1, sources[half], near2, sems2, got[half])
-    for half in range(2):
-        ring_third(half, 1, sources[half], mid2, sent2, far2, sems2, got[half])
-    finish = ring_sum_finish(mixed_parts, y_jobs[1], y_more[1], yfar.at[1], ynear.at[1])
-    for top in range(2):
-        rng = pl.ds(top * here, here)
-        mixed[rng] = (first_sum[rng] + finish(top)).astype(bf16)
-    for half in range(2):
-        for part in range(2):
-            packed[half, part * piece : (part + 1) * piece] = ring_last(
-                half, part, sources[half], far2, near2, got[half]
-            ).astype(bf16)
-
-    home, away = {"yl": c, "c": yl}, {"yl": c, "c": 1 - yl}
-    stay_or_go(packed.at[yl], result.at[yl], pair_sems, 0, home, local_sem)
-    cross = remote(packed.at[1 - yl], result.at[yl], pair_sems, 1, away)
-    cross.start()
-    cross.wait_recv()
-    cross.wait_send()
-    stay_or_go_wait(packed.at[yl], result.at[yl], pair_sems, 0, home, local_sem)
-    for jobs in y_jobs + y_more:
-        for copy in jobs:
-            copy.wait_send()
-    for copy in done:
         copy.wait_send()
 
 
@@ -375,46 +181,6 @@
         )
 
     return finish
-
-
-def last_sum(grads, first_parts, mixed_parts, resid, tokens, stats, gains, first_sum):
-    rows = grads.shape[0] // 64
-    wide = grads.shape[1]
-    here, width = resid.shape
-    full = pl.BlockSpec(memory_space=VMEM)
-    piece = rows // 2
-    return pl.pallas_call(
-        last_sum_kernel,
-        out_shape=(
-            jax.ShapeDtypeStruct((2, rows, wide), bf16),
-            jax.ShapeDtypeStruct((here, width), f32),
-            jax.ShapeDtypeStruct((here, width), bf16),
-        ),
-        in_specs=[full] * 8,
-        out_specs=(full,) * 3,
-        scratch_shapes=[
-            VMEM((4, 4, 2 * rows, wide), bf16),
-            VMEM((2, 2, 4, piece, wide), bf16),
-            VMEM((2, 2, 4, piece, wide), bf16),
-            VMEM((2, 2, 4, piece, wide), bf16),
-            VMEM((2, 2, 4, piece, wide), bf16),
-            VMEM((2, 4, rows, wide), bf16),
-            VMEM((2, 2, piece, wide), bf16),
-            VMEM((2, 2, piece, wide), bf16),
-            VMEM((2, 2, piece, wide), bf16),
-            VMEM((2, 2, piece, wide), bf16),
-            VMEM((2, rows, wide), bf16),
-            VMEM((2, 2, here // 2, width), bf16),
-            VMEM((2, 2, here // 2, width), bf16),
-            VMEM((2, 2, here // 2, width), bf16),
-            VMEM((2, 2, here // 2, width), bf16),
-            DMA((16,)), DMA((16,)), DMA((12,)), DMA((12,)), DMA((12,)), DMA((12,)),
-            DMA((2,)), DMA((2,)), DMA, DMA((12,)), DMA((12,)),
-        ],
-        compiler_params=pltpu.CompilerParams(
-            collective_id=3, has_side_effects=True, vmem_limit_bytes=VMEM_LIMIT
-        ),
-    )(grads, first_parts, mixed_parts, resid, tokens, stats, gains, first_sum)
 
 
 def tables():
@@ -476,117 +242,6 @@
         norm_table[:, pl.ds(group * 128, 128)] = block[12:16] + block[16:20]
         total = block[0:12] if total is None else total + block[0:12]
     bias[...] = total
-
-
-def attention_backward_kernel(
-    resid, one, normed, stats, qkv, head_mix, token_rows, table, second_terms,
-    grads, first_parts, grad_mix, grad_proj,
-):
-    here = resid.shape[0] // 4
-    hq = head_mix.shape[1]
-    wide = 256
-
-    def mix_back(k, _):
-        cols = pl.ds(pl.multiple_of(k * wide, wide), wide)
-        grad_mix[:, cols] = dot(
-            resid[...], one[:, pl.ds(pl.multiple_of(3 * hq + k * wide, wide), wide)], 1, 0
-        ).astype(bf16)
-        return 0
-
-    lax.fori_loop(0, hq // wide, mix_back, 0)
-
-    def out_back(k, _):
-        rng = pl.ds(pl.multiple_of(k * wide, wide), wide)
-        grads[rng, pl.ds(3 * hq, hq)] = dot(resid[:, rng], head_mix[...], 0, 0).astype(bf16)
-        return 0
-
-    lax.fori_loop(0, one.shape[0] // wide, out_back, 0)
-    for sequence in range(2):
-        mask = causal_mask(sequence, here)
-        rng = pl.ds(sequence * 2 * here, 2 * here)
-        turn = jnp.concatenate(
-            [
-                table[pl.ds(pl.multiple_of(half_of_place(2 * sequence + k) * here, here), here)]
-                for k in range(2)
-            ],
-            0,
-        )
-
-        def heads(k, _):
-            def pair(t):
-                return pl.ds(pl.multiple_of(t * hq + k * 128, 128), 128)
-
-            q, key, value = qkv[rng, pair(0)], qkv[rng, pair(1)], qkv[rng, pair(2)]
-            mix = grad_mix[rng, pair(0)]
-            results = ([], [], [])
-            for head in range(2):
-                cut = slice(head * HEAD_DIM, (head + 1) * HEAD_DIM)
-                soft = soft_of(q[:, cut], key[:, cut], mask)
-                grad_soft = dot(mix[:, cut], value[:, cut], 1, 1)
-                row_dot = jnp.sum(grad_soft * soft, -1, keepdims=True)
-                grad_score = (soft * (grad_soft - row_dot)).astype(bf16)
-                results[0].append(dot(grad_score, key[:, cut], 1, 0) * SCALE)
-                results[1].append(dot(grad_score, q[:, cut], 0, 0) * SCALE)
-                results[2].append(dot(soft.astype(bf16), mix[:, cut], 0, 0))
-            for t in range(3):
-                both = jnp.concatenate(results[t], 1)
-                if t < 2:
-                    both = turn_heads(both, turn, -1.0)
-                grad_proj[rng, pair(t)] = both.astype(bf16)
-            return 0
-
-        lax.fori_loop(0, hq // 128, heads, 0)
-
-    bias_rows = [
-        jnp.sum(grad_proj[:, pl.ds(k * 128, 128)].astype(f32), 0, keepdims=True)
-        for k in range(3 * hq // 128)
-    ]
-    mean, inverse = stats[0], stats[1]
-
-    def weights_back(k, _):
-        rng = pl.ds(pl.multiple_of(k * wide, wide), wide)
-        grads[rng, pl.ds(0, 3 * hq)] = dot(normed[:, rng], grad_proj[...], 0, 0).astype(bf16)
-        part = dot(grad_proj[...], one[rng, pl.ds(0, 3 * hq)], 1, 1)
-        first_parts[:, rng] = part.astype(bf16)
-        unit = (token_rows[:, rng].astype(f32) - mean) * inverse
-        gain = jnp.sum(part * unit, 0, keepdims=True)
-        shift = jnp.sum(part, 0, keepdims=True)
-        for tile in range(wide // 128):
-            cut = slice(tile * 128, (tile + 1) * 128)
-            lanes = pl.ds(pl.multiple_of(k * wide + tile * 128, 128), 128)
-            block = jnp.concatenate(
-                bias_rows
-                + [
-                    gain[:, cut],
-                    shift[:, cut],
-                    second_terms[:, lanes],
-                    jnp.zeros((16, 128), f32),
-                ],
-                0,
-            ).astype(bf16)
-            for copy in range(4):
-                start = pl.multiple_of(k * wide + tile * 128 + copy * 32, 32)
-                grads[pl.ds(start, 32), pl.ds(4 * hq, 128)] = block
-        return 0
-
-    lax.fori_loop(0, one.shape[0] // wide, weights_back, 0)
-
-
-def attention_backward(resid, one, normed, stats, qkv, head_mix, token_rows, table, second_terms):
-    tokens, width = token_rows.shape
-    hq = head_mix.shape[1]
-    full = pl.BlockSpec(memory_space=VMEM)
-    return pl.pallas_call(
-        attention_backward_kernel,
-        out_shape=(
-            jax.ShapeDtypeStruct(one.shape, bf16),
-            jax.ShapeDtypeStruct((tokens, width), bf16),
-        ),
-        in_specs=[full] * 9,
-        out_specs=(full,) * 2,
-        scratch_shapes=[VMEM((tokens, hq), bf16), VMEM((tokens, 3 * hq), bf16)],
-        compiler_params=pltpu.CompilerParams(vmem_limit_bytes=VMEM_LIMIT),
-    )(resid, one, normed, stats, qkv, head_mix, token_rows, table, second_terms)
 
 
 def feed_forward_kernel(
@@ -874,9 +529,9 @@
 
 def forward_kernel(
     qkv_weight, out_weight, gate_up_weight, down_weight, extra, tokens, cotangent, table,
-    one_out, two, token_rows, cot_rows, normed, stats, qkv, head_mix, norm_table,
+    one_out, two, token_rows, cot_rows, stats, qkv, head_mix, norm_table,
     summed, unit, scale, normed_two,
-    one_q, two_q, one, norm_in, bias, parts, mid, sent, far, near,
+    one_q, two_q, one, norm_in, bias, normed, parts, mid, sent, far, near,
     pair_send, pair_recv, local_sem, y_send, y_recv,
     send_one, recv_one, core_send_one, core_recv_one,
     send_two, recv_two, core_send_two, core_recv_two,
@@ -1108,7 +763,6 @@
             shape(width, two_wide),
             shape(4 * here, width),
             shape(4 * here, width),
-            shape(4 * here, width),
             shape(2, 4 * here, 1, dtype=f32),
             shape(4 * here, 3 * hq),
             shape(4 * here, hq),
@@ -1119,13 +773,14 @@
             shape(4 * here, width),
         ),
         in_specs=[full] * 8,
-        out_specs=(anywhere, anywhere) + (full,) * 11,
+        out_specs=(anywhere, anywhere) + (full,) * 10,
         scratch_shapes=[
             VMEM((2, rows, one_wide), bf16),
             VMEM((2, rows, two_wide), bf16),
             VMEM((width, one_wide), bf16),
             VMEM((2, rows, EXTRA), bf16),
             VMEM((12, 128), f32),
+            VMEM((4 * here, width), bf16),
             VMEM((4 * here, width), bf16),
         ]
         + [VMEM((2, here // 2, width), bf16)] * 4
@@ -1140,22 +795,370 @@
     )(qkv_weight, out_weight, gate_up_weight, down_weight, extra, tokens, cotangent, table)
 
 
-SAME = [(0, 0), (1, 2), (2, 1), (3, 3)]
-CROSS = [(0, 2), (1, 0), (2, 3), (3, 1)]
-
-
-def from_quarters(rows):
-    yl, c = lax.axis_index("yl"), lax.axis_index("c")
-    halves = rows.reshape(2, rows.shape[0] // 2, rows.shape[1])
-    one = lax.ppermute(
-        lax.dynamic_index_in_dim(halves, yl, 0, False), ("yl", "c"), [(b, a) for a, b in SAME]
-    )
-    two = lax.ppermute(
-        lax.dynamic_index_in_dim(halves, 1 - yl, 0, False),
-        ("yl", "c"),
-        [(b, a) for a, b in CROSS],
-    )
-    return jnp.stack([jnp.where(c == 0, one, two), jnp.where(c == 0, two, one)])
+class Reduce:
+    def __init__(self, src, mid, far, near, sems, mid2, far2, near2, sems2):
+        self.src, self.rows = src, src.shape[2] // 2
+        self.rings = ((mid, far, near, sems), (mid2, far2, near2, sems2))
+        self.done, self.got = [], {}
+
+    def view(self, stage, half, d, part):
+        piece = self.rows // 2
+        rng = pl.ds(half * self.rows + part * piece, piece)
+        if stage == 0:
+            return self.src.at[d, :, rng] if half == 0 else self.src.at[:, d, rng]
+        return self.src.at[0, d, rng] if half == 0 else self.src.at[d, 0, rng]
+
+    def send(self, name, stage, half, way, src, dst, index):
+        step = (1, -1)[way]
+        device = at_z(step) if (half == 0) == (stage == 0) else at_x(step)
+        copy = remote(src, dst, self.rings[stage][3], half * 6 + index * 2 + way, device)
+        copy.start()
+        self.done.append(copy)
+        self.got[name, stage, half, way] = copy
+
+    def far_rows(self, stage, half):
+        mid = self.rings[stage][0]
+        for way in range(2):
+            self.send("mid", stage, half, way, self.view(stage, half, 2, way), mid.at[half, way], 0)
+
+    def near_rows(self, stage, half):
+        near = self.rings[stage][2]
+        for way in range(2):
+            src = self.view(stage, half, (1, 3)[way], 1 - way)
+            self.send("near", stage, half, way, src, near.at[half, way], 1)
+
+    def combine(self, stage, half):
+        mid, far = self.rings[stage][:2]
+        for way in range(2):
+            self.got["mid", stage, half, way].wait_recv()
+            ref = self.view(stage, half, (1, 3)[way], way)
+            ref[...] = (ref[...].astype(f32) + mid[half, way].astype(f32)).astype(bf16)
+            self.send("far", stage, half, way, ref, far.at[half, way], 2)
+
+    def settle(self, stage, half, out=None):
+        far, near = self.rings[stage][1:3]
+        piece = self.rows // 2
+        for part in range(2):
+            self.got["far", stage, half, part].wait_recv()
+            self.got["near", stage, half, 1 - part].wait_recv()
+            ref = self.view(stage, half, 0, part)
+            total = (
+                ref[...].astype(f32)
+                + far[half, part].astype(f32)
+                + near[half, 1 - part].astype(f32)
+            ).astype(bf16)
+            if out is None:
+                ref[...] = total
+            else:
+                out[half, pl.ds(part * piece, piece)] = total
+
+    def close(self):
+        for copy in self.done:
+            copy.wait_send()
+
+
+def backward_kernel(
+    one, resid_rows, chip, qkv, head_mix, token_rows, stats, table, second_terms, norm_table,
+    mixed_parts, resid, first_sum,
+    result_one, result_two, norm_back, grad_tokens, mixed,
+    held, spare, grad_mix, grad_proj, sib, mid_a, far_a, near_a, mid_b, far_b, near_b,
+    blocks, mid_c, far_c, near_c, mid_d, far_d, near_d, packed_one, packed_two,
+    ymid, ysent, yfar, ynear,
+    load_sem, block_sem, core_send, core_recv, send_a, recv_a, send_b, recv_b,
+    send_c, recv_c, send_d, recv_d, pair_send, pair_recv, local_sem, y_send, y_recv,
+):
+    z, x = lax.axis_index("z"), lax.axis_index("x")
+    yl, c, yh = lax.axis_index("yl"), lax.axis_index("c"), lax.axis_index("yh")
+    here = resid.shape[0]
+    rows = result_one.shape[1]
+    hq = head_mix.shape[1]
+    width = held.shape[0]
+    core_sems, pair_sems, y_sems = (core_send, core_recv), (pair_send, pair_recv), (y_send, y_recv)
+    wide = 256
+
+    def place_of(dz, dx):
+        return ((z + dz) % 4) * 4 + (x + dx) % 4
+
+    loads = [
+        pltpu.make_async_copy(
+            one.at[:, pl.ds(start, size)], held.at[:, pl.ds(start, size)], load_sem.at[k]
+        )
+        for k, (start, size) in enumerate(((3 * hq, hq), (0, 3 * hq)))
+    ]
+    loads.append(pltpu.make_async_copy(resid_rows, spare, load_sem.at[2]))
+    order = []
+    for d in (2, 1, 3, 0):
+        for e in (2, 1, 3, 0):
+            for pair in ((d, e), (e, d)):
+                if pair not in order:
+                    order.append(pair)
+    block_loads = {
+        (dz, dx): pltpu.make_async_copy(
+            chip.at[place_of(dz, dx)], blocks.at[dz, dx], block_sem.at[dz * 4 + dx]
+        )
+        for dz, dx in order
+    }
+    loads[2].start()
+    loads[0].start()
+    for pair in order:
+        block_loads[pair].start()
+    loads[1].start()
+    greet([at_z(1), at_z(3), at_x(1), at_x(3)] + cube())
+    mixed_started = ring_sum_start(mixed_parts, ymid.at[0], ynear.at[0], y_sems, 0)
+    second = Reduce(blocks, mid_c, far_c, near_c, (send_c, recv_c), mid_d, far_d, near_d, (send_d, recv_d))
+    first = Reduce(sib, mid_a, far_a, near_a, (send_a, recv_a), mid_b, far_b, near_b, (send_b, recv_b))
+    for pair in order:
+        block_loads[pair].wait()
+    for half in range(2):
+        second.far_rows(0, half)
+    for half in range(2):
+        second.near_rows(0, half)
+
+    loads[2].wait()
+    loads[0].wait()
+
+    def mix_back(k, _):
+        cols = pl.ds(pl.multiple_of(k * wide, wide), wide)
+        grad_mix[:, cols] = dot(
+            spare[...], held[:, pl.ds(pl.multiple_of(3 * hq + k * wide, wide), wide)], 1, 0
+        ).astype(bf16)
+        return 0
+
+    lax.fori_loop(0, hq // wide, mix_back, 0)
+
+    def out_back(k, _):
+        rng = pl.ds(pl.multiple_of(k * 2 * wide, 2 * wide), 2 * wide)
+        held[rng, pl.ds(3 * hq, hq)] = dot(spare[:, rng], head_mix[...], 0, 0).astype(bf16)
+        return 0
+
+    lax.fori_loop(0, width // (2 * wide), out_back, 0)
+    mixed_middle = ring_sum_middle(
+        mixed_parts, mixed_started, ymid.at[0], ysent.at[0], yfar.at[0], y_sems, 0
+    )
+    for sequence in range(2):
+        mask = causal_mask(sequence, here)
+        rng = pl.ds(sequence * 2 * here, 2 * here)
+        turn = jnp.concatenate(
+            [
+                table[pl.ds(pl.multiple_of(half_of_place(2 * sequence + k) * here, here), here)]
+                for k in range(2)
+            ],
+            0,
+        )
+
+        def heads(k, _):
+            def pair(t):
+                return pl.ds(pl.multiple_of(t * hq + k * 128, 128), 128)
+
+            q, key, value = qkv[rng, pair(0)], qkv[rng, pair(1)], qkv[rng, pair(2)]
+            mix = grad_mix[rng, pair(0)]
+            results = ([], [], [])
+            for head in range(2):
+                cut = slice(head * HEAD_DIM, (head + 1) * HEAD_DIM)
+                soft = soft_of(q[:, cut], key[:, cut], mask)
+                grad_soft = dot(mix[:, cut], value[:, cut], 1, 1)
+                row_dot = jnp.sum(grad_soft * soft, -1, keepdims=True)
+                grad_score = (soft * (grad_soft - row_dot)).astype(bf16)
+                results[0].append(dot(grad_score, key[:, cut], 1, 0) * SCALE)
+                results[1].append(dot(grad_score, q[:, cut], 0, 0) * SCALE)
+                results[2].append(dot(soft.astype(bf16), mix[:, cut], 0, 0))
+            for t in range(3):
+                both = jnp.concatenate(results[t], 1)
+                if t < 2:
+                    both = turn_heads(both, turn, -1.0)
+                grad_proj[rng, pair(t)] = both.astype(bf16)
+            return 0
+
+        lax.fori_loop(0, hq // 128, heads, 0, unroll=2)
+        second.combine(0, sequence)
+
+    bias_rows = [
+        jnp.sum(grad_proj[:, pl.ds(k * 128, 128)].astype(f32), 0, keepdims=True)
+        for k in range(3 * hq // 128)
+    ]
+    mean, inverse = stats[0], stats[1]
+    loads[1].wait()
+
+    def to_core(block):
+        theirs = pl.ds(pl.multiple_of((2 * block + 1 - c) * 2 * rows, 2 * rows), 2 * rows)
+        dz, dx = (block // 4 - z + 4) % 4, (block % 4 - x + 4) % 4
+        return remote(held.at[theirs], sib.at[dz, dx], core_sems, block, sibling())
+
+    def weights_back(k, _):
+        rng = pl.ds(pl.multiple_of(k * wide, wide), wide)
+        part = dot(grad_proj[...], held[rng, pl.ds(0, 3 * hq)], 1, 1)
+        spare[:, rng] = part.astype(bf16)
+        unit = (token_rows[:, rng].astype(f32) - mean) * inverse
+        normed = (unit * norm_table[0:1, rng] + norm_table[1:2, rng]).astype(bf16)
+        held[rng, pl.ds(0, 3 * hq)] = dot(normed, grad_proj[...], 0, 0).astype(bf16)
+        gain = jnp.sum(part * unit, 0, keepdims=True)
+        shift = jnp.sum(part, 0, keepdims=True)
+        for tile in range(wide // 128):
+            cut = slice(tile * 128, (tile + 1) * 128)
+            lanes = pl.ds(pl.multiple_of(k * wide + tile * 128, 128), 128)
+            extra = jnp.concatenate(
+                bias_rows
+                + [
+                    gain[:, cut],
+                    shift[:, cut],
+                    second_terms[:, lanes],
+                    jnp.zeros((rows - 16, 128), f32),
+                ],
+                0,
+            ).astype(bf16)
+            for copy in range(128 // rows):
+                start = pl.multiple_of(k * wide + tile * 128 + copy * rows, rows)
+                held[pl.ds(start, rows), pl.ds(4 * hq, EXTRA)] = extra
+        for block in range(wide // (4 * rows)):
+            to_core(k * (wide // (4 * rows)) + block).start()
+        return 0
+
+    lax.fori_loop(0, width // wide, weights_back, 0)
+    first_started = ring_sum_start(spare, ymid.at[1], ynear.at[1], y_sems, 6)
+
+    summed = set()
+
+    def core_sum(dz, dx):
+        if (dz, dx) in summed:
+            return
+        summed.add((dz, dx))
+        block = place_of(dz, dx)
+        to_core(block).wait_recv()
+        ours = pl.ds(pl.multiple_of((2 * block + c) * 2 * rows, 2 * rows), 2 * rows)
+        sib[dz, dx] = (sib[dz, dx].astype(f32) + held[ours].astype(f32)).astype(bf16)
+
+    for half in range(2):
+        for d in (2, 1, 3, 0):
+            core_sum(*((2, d) if half == 0 else (d, 2)))
+        first.far_rows(0, half)
+    for half in range(2):
+        for step in (1, 3):
+            for d in (2, 1, 3, 0):
+                core_sum(*((step, d) if half == 0 else (d, step)))
+        first.near_rows(0, half)
+    core_sum(0, 0)
+    for half in range(2):
+        second.settle(0, half)
+        second.far_rows(1, half)
+        second.near_rows(1, half)
+    first_middle = ring_sum_middle(
+        spare, first_started, ymid.at[1], ysent.at[1], yfar.at[1], y_sems, 6
+    )
+    for half in range(2):
+        first.combine(0, half)
+    for half in range(2):
+        second.combine(1, half)
+    half_here = here // 2
+    finish = ring_sum_finish(mixed_parts, mixed_started, mixed_middle, yfar.at[0], ynear.at[0])
+    for top in range(2):
+        rng = pl.ds(top * half_here, half_here)
+        mixed[rng] = (first_sum[rng] + finish(top)).astype(bf16)
+    finish = ring_sum_finish(spare, first_started, first_middle, yfar.at[1], ynear.at[1])
+    for top in range(2):
+        rng = pl.ds(top * half_here, half_here)
+        incoming = finish(top) * norm_table[0:1]
+        unit_rows = (token_rows[rng].astype(f32) - stats[0, rng]) * stats[1, rng]
+        grad_tokens[rng] = resid[rng] + stats[1, rng] * (
+            incoming
+            - jnp.mean(incoming, -1, keepdims=True)
+            - unit_rows * jnp.mean(incoming * unit_rows, -1, keepdims=True)
+        )
+
+    home, away = {"yl": c, "c": yl}, {"yl": c, "c": 1 - yl}
+    for half in range(2):
+        second.settle(1, half, packed_two)
+    stay_or_go(packed_two.at[yl], result_two.at[yl], pair_sems, 0, home, local_sem.at[0])
+    cross_two = remote(packed_two.at[1 - yl], result_two.at[yl], pair_sems, 1, away)
+    cross_two.start()
+    for half in range(2):
+        first.settle(0, half)
+        first.far_rows(1, half)
+        first.near_rows(1, half)
+    for half in range(2):
+        first.combine(1, half)
+    for half in range(2):
+        first.settle(1, half, packed_one)
+    stay_or_go(packed_one.at[yl], result_one.at[yl], pair_sems, 2, home, local_sem.at[1])
+    cross_one = remote(packed_one.at[1 - yl], result_one.at[yl], pair_sems, 3, away)
+    cross_one.start()
+    extras = pl.ds(4 * hq, EXTRA)
+    norm_moves = [
+        remote(
+            packed_one.at[core, :, extras],
+            norm_back.at[yl],
+            pair_sems,
+            4 + which,
+            {"yl": c, "c": core, "yh": 1 - yh},
+        )
+        for which, core in enumerate((yl, 1 - yl))
+    ]
+    for move in norm_moves:
+        move.start()
+    for copy in [cross_two, cross_one] + norm_moves:
+        copy.wait_recv()
+        copy.wait_send()
+    stay_or_go_wait(packed_two.at[yl], result_two.at[yl], pair_sems, 0, home, local_sem.at[0])
+    stay_or_go_wait(packed_one.at[yl], result_one.at[yl], pair_sems, 2, home, local_sem.at[1])
+    for copy in mixed_started + mixed_middle + first_started + first_middle:
+        copy.wait_send()
+
+    def drain(block, _):
+        to_core(block).wait_send()
+        return 0
+
+    lax.fori_loop(0, 16, drain, 0)
+    first.close()
+    second.close()
+
+
+def backward(
+    one, resid_rows, chip, qkv, head_mix, token_rows, stats, table, second_terms, norm_table,
+    mixed_parts, resid, first_sum,
+):
+    here, width = resid.shape
+    hq = head_mix.shape[1]
+    rows = width // 64
+    piece = rows // 2
+    one_wide, two_wide = one.shape[1], chip.shape[2]
+    full = pl.BlockSpec(memory_space=VMEM)
+    anywhere = pl.BlockSpec(memory_space=pl.ANY)
+
+    def rings(wide):
+        return [VMEM((2, 2, 4, piece, wide), bf16)] * 3 + [VMEM((2, 2, piece, wide), bf16)] * 3
+
+    return pl.pallas_call(
+        backward_kernel,
+        out_shape=(
+            jax.ShapeDtypeStruct((2, rows, one_wide), bf16),
+            jax.ShapeDtypeStruct((2, rows, two_wide), bf16),
+            jax.ShapeDtypeStruct((2, rows, EXTRA), bf16),
+            jax.ShapeDtypeStruct((here, width), f32),
+            jax.ShapeDtypeStruct((here, width), bf16),
+        ),
+        in_specs=[anywhere] * 3 + [full] * 10,
+        out_specs=(full,) * 5,
+        scratch_shapes=[
+            VMEM((width, one_wide), bf16),
+            VMEM((4 * here, width), bf16),
+            VMEM((4 * here, hq), bf16),
+            VMEM((4 * here, 3 * hq), bf16),
+            VMEM((4, 4, 2 * rows, one_wide), bf16),
+        ]
+        + rings(one_wide)
+        + [VMEM((4, 4, 2 * rows, two_wide), bf16)]
+        + rings(two_wide)
+        + [VMEM((2, rows, one_wide), bf16), VMEM((2, rows, two_wide), bf16)]
+        + [VMEM((2, 2, here // 2, width), bf16)] * 4
+        + [DMA((3,)), DMA((16,)), DMA((16,)), DMA((16,))]
+        + [DMA((12,))] * 8
+        + [DMA((6,)), DMA((6,)), DMA((2,)), DMA((12,)), DMA((12,))],
+        compiler_params=pltpu.CompilerParams(
+            collective_id=3, has_side_effects=True, vmem_limit_bytes=VMEM_LIMIT
+        ),
+    )(
+        one, resid_rows, chip, qkv, head_mix, token_rows, stats, table, second_terms, norm_table,
+        mixed_parts, resid, first_sum,
+    )
 
 
 def shards(
@@ -1189,7 +1192,7 @@
     )
     table = jnp.asarray(tables())
     (
-        one, second, token_rows, cot_rows, normed_one, stats, qkv, head_mix, norm_table,
+        one, second, token_rows, cot_rows, stats, qkv, head_mix, norm_table,
         first_sum, unit_two, scale_two, normed_two,
     ) = forward(
         qkv_weight, out_weight.T, gate_up_weight, down_weight.T, extra, tokens, cotangent, table
@@ -1197,17 +1200,11 @@
     grad_resid, second_terms, resid_rows, mixed_parts, chip = feed_forward(
         normed_two, cot_rows, cotangent, unit_two, scale_two, norm_table[2:], second
     )
-    second_sums = lax.psum_scatter(
-        chip.reshape(-1, 3 * fq), ("z", "x"), scatter_dimension=0, tiled=True
-    )
-    grads, first_parts = attention_backward(
-        resid_rows, one, normed_one, stats, qkv, head_mix, token_rows, table, second_terms
-    )
-    first_back, grad_input, mixed = last_sum(
-        grads, first_parts, mixed_parts, grad_resid, tokens, stats, norm_table[:2], first_sum
-    )
-
-    second_back = from_quarters(second_sums)
+    first_back, second_back, norm_other, grad_input, mixed = backward(
+        one, resid_rows, chip, qkv, head_mix, token_rows, stats, table, second_terms, norm_table,
+        mixed_parts, grad_resid, first_sum,
+    )
+
     gu_back, down_back = second_back[:, :, : 2 * fq], second_back[:, :, 2 * fq :]
     out_down = down_back.transpose(0, 2, 1).reshape(2 * fq, rows).astype(f32)
     out_gu = (
@@ -1232,15 +1229,10 @@
         .transpose(1, 0, 2)
         .reshape(3, 2 * heads, 1)
     )
-    norm_back = lax.dynamic_index_in_dim(
-        (extra_back[0] + extra_back[1])[pairs : pairs + 4].reshape(4, EXTRA // rows, rows),
-        mine % 4,
-        1,
-        False,
-    ).reshape(4, 2, rows // 2)
-    kept = lax.dynamic_index_in_dim(norm_back, yh, 1, False)
-    sent = lax.dynamic_index_in_dim(norm_back, 1 - yh, 1, False)
-    out_norm = kept + lax.ppermute(sent, "yh", [(0, 1), (1, 0)])
+    norm_sums = (extra_back + norm_other.astype(f32)).sum(0)[pairs : pairs + 4]
+    out_norm = lax.dynamic_index_in_dim(
+        norm_sums.reshape(4, EXTRA // share, share), mine % 4 * 2 + yh, 1, False
+    )
     return (mixed, grad_input, out_norm, out_qkv, out_bias, out_out, out_gu, out_down)
 
 

time: 319 us -> 290 us (0.909)
  between operations: 14.3 us -> 0.82 us
  Pallas kernels: 278 us -> 271 us
  waiting for transfers between devices: 4.93 us -> 0 us
    pallas_call x2 -> x1, Pallas kernels: 96.5 us -> 90 us  [backward(): pl.pallas_call(backward_kernel, out_shape=(jax.ShapeDtypeStruct((2, rows,...]
    ppermute x3 -> x0, waiting for transfers between devices: 4.91 us -> none  [the longest x1 4.91 us: from_quarters(): lax.ppermute(lax.dynamic_index_in_dim(halves, 1 - yl, 0, False), ('yl', '...]
  transfers between devices with their start and end apart: 4 -> 0, of which waited for: 1 -> 0; matrix products, arithmetic and copies ran while one was open for 2% -> 0% of each run, Pallas kernels for 30% -> 0%
where the time goes in v5:
time: 290 us; the launch traced here: 289 us
  Pallas kernels  271 us (93%)
  local copies, waits for them, and re-layouts  11.8 us (4%)
  other arithmetic  5.43 us (2%)
    pallas_call x1, Pallas kernels, forward(): pl.pallas_call(forward_kernel, out_shape=(shape(width, one_wide), shape(w...  117 us
    pallas_call x1, Pallas kernels, backward(): pl.pallas_call(backward_kernel, out_shape=(jax.ShapeDtypeStruct((2, rows,...  90 us
    pallas_call x1, Pallas kernels, feed_forward(): pl.pallas_call(feed_forward_kernel, out_shape=(jax.ShapeDtypeStruct((here...  64.6 us

profile of v5, /device:TPU:0, one launch (start us, length us, event | category | flops | bytes accessed | tf_op | source)
XLA Modules:
  0.0 289.2 jit_solution(15923332840166724159)
XLA Ops:
  0.7 0.1 broadcast_in_dim.40
  0.8 0.7 convert_element_type.61
  1.5 0.7 subtract_convert_fusion
  2.2 0.8 reshape.79
  2.9 0.1 broadcast_in_dim.42
  3.0 0.1 broadcast_in_dim.43
  3.1 0.1 broadcast_in_dim.44
  3.2 0.1 tile.10
  3.4 0.6 pad_maximum_fusion.extra
  4.0 116.7 %shard_map.152 = (bf16[2048,2176]{1,0:T(8,128)(2,1)}, bf16[2048,4224]{1,0:T(8,128)(2,1)}, bf16[512,2048]{1,0:T(8,128)(2,1)}, bf16[512,2048]{1,0:T(8,128)(2,1)}, ...) custom-call(bf16[3,32,1024]{2,1,0:T(8,128)(2,1)} %qkv_weight.1, ...), custom_call_target="tpu_custom_call" | custom-call | tf_op jit(solution)/shard_map/pallas_call | solution.py:759
  120.6 1.4 slice.24.gains
  122.0 64.6 %shard_map.153 = (f32[128,2048]{1,0:T(8,128)}, f32[2,2048]{1,0:T(2,128)}, bf16[512,2048]{1,0:T(8,128)(2,1)}, bf16[512,2048]{1,0:T(8,128)(2,1)}, bf16[16,64,4224]{2,1,0:T(8,128)(2,1)}) custom-call(bf16[512,2048]{1,0:T(8,128)(2,1)} %get-tuple-element.31.normed, bf16[512,2048]{1,0:T(8,128)(2,1)} %get-tuple-element.32.cot_rows, bf16[128,2048]{1,0:T(8,128)(2,1)} %cotangent.3, ...), custom_call_target="tpu_custom_call" | custom-call | tf_op jit(solution)/shard_map/pallas_call | solution.py:393
  186.6 90.0 %shard_map.154 = (bf16[2,32,2176]{2,1,0:T(8,128)(2,1)}, bf16[2,32,4224]{2,1,0:T(8,128)(2,1)}, bf16[2,32,128]{2,1,0:T(8,128)(2,1)}, f32[128,2048]{1,0:T(8,128)}, bf16[128,2048]{1,0:T(8,128)(2,1)}) custom-call(bf16[2048,2176]{1,0:T(8,128)(2,1)} %get-tuple-element.30.one, bf16[512,2048]{1,0:T(8,128)(2,1)} %get-tuple-element.37.resid_rows, ...), custom_call_target="tpu_custom_call" | custom-call | tf_op jit(solution)/shard_map/pallas_call | solution.py:1129
  276.6 0.0 copy-start.1
  276.6 0.8 add_reduce_fusion
  277.4 0.1 reshape.80
  277.5 0.6 constant_dynamic-slice_fusion.1
  278.1 0.7 slice_convert_fusion.2
  278.8 0.1 reshape.81
  278.9 0.1 constant_dynamic-slice_fusion
  279.0 0.3 copy.38
  279.3 0.1 reshape.82
  279.4 0.7 reshape.90
  280.0 0.8 convert_bitcast_fusion.1
  280.9 0.7 copy.44
  281.6 1.0 slice_convert_fusion.1
  282.5 0.3 reshape.88
  282.8 0.3 copy.36
  283.1 1.1 reshape.84
  284.2 0.0 copy-done.1
  284.2 0.8 copy.45
  285.0 0.0 copy-start.2
  285.0 0.4 reshape.89
  285.5 0.0 copy-start
  285.5 0.6 copy.41
  286.0 1.4 reshape.86
  287.5 0.0 copy-done.2
  287.5 0.8 copy.49
  288.3 0.0 copy-done
  288.3 1.0 copy.50
  (17 shorter events, 0.2 us)
Async XLA Ops:
  276.6 7.6 %copy-start.1 = (bf16[2,32,4224]{2,1,0:T(8,128)(2,1)S(1)}, bf16[2,32,4224]{2,1,0:T(8,128)(2,1)}, u32[]{:S(2)}) copy-start(bf16[2,32,4224]{2,1,0:T(8,128)(2,1)} %get-tuple-element.51) | copy-start | bytes 1622020
  285.0 2.4 copy-start.2
  285.5 2.8 copy-start

commit v6 on v5

--- a/solution.py
+++ b/solution.py
@@ -15,6 +15,7 @@
 GRID = ("z", "x", "yl", "c", "yh")
 ROWS = ("z", "x", "yl", "c")
 EXTRA = 128
+EARLY = 1408
 
 bf16 = jnp.bfloat16
 f32 = jnp.float32
@@ -244,23 +245,90 @@
     bias[...] = total
 
 
+class Reduce:
+    def __init__(self, view, rows, rings):
+        self.view, self.rows, self.rings = view, rows, rings
+        self.done, self.got = [], {}
+
+    def send(self, name, stage, half, way, src, dst, index):
+        step = (1, -1)[way]
+        device = at_z(step) if (half == 0) == (stage == 0) else at_x(step)
+        copy = remote(src, dst, self.rings[stage][3], half * 6 + index * 2 + way, device)
+        copy.start()
+        self.done.append(copy)
+        self.got[name, stage, half, way] = copy
+
+    def begin(self, stage):
+        mid, _, near, _ = self.rings[stage]
+        for half in range(2):
+            for way in range(2):
+                src = self.view(stage, half, 2, way)
+                self.send("mid", stage, half, way, src, mid.at[half, way], 0)
+        for half in range(2):
+            for way in range(2):
+                src = self.view(stage, half, (1, 3)[way], 1 - way)
+                self.send("near", stage, half, way, src, near.at[half, way], 1)
+
+    def combine(self, stage):
+        mid, far = self.rings[stage][:2]
+        for half in range(2):
+            for way in range(2):
+                self.got["mid", stage, half, way].wait_recv()
+                ref = self.view(stage, half, (1, 3)[way], way)
+                ref[...] = (ref[...].astype(f32) + mid[half, way].astype(f32)).astype(bf16)
+                self.send("far", stage, half, way, ref, far.at[half, way], 2)
+
+    def settle(self, stage, out=None):
+        far, near = self.rings[stage][1:3]
+        piece = self.rows // 2
+        for half in range(2):
+            for part in range(2):
+                self.got["far", stage, half, part].wait_recv()
+                self.got["near", stage, half, 1 - part].wait_recv()
+                ref = self.view(stage, half, 0, part)
+                total = (
+                    ref[...].astype(f32)
+                    + far[half, part].astype(f32)
+                    + near[half, 1 - part].astype(f32)
+                ).astype(bf16)
+                if out is None:
+                    ref[...] = total
+                else:
+                    out[half, pl.ds(part * piece, piece)] = total
+
+    def close(self):
+        for copy in self.done:
+            copy.wait_send()
+
+
+def ring_buffers(stage, piece, wide):
+    dims = (2, 2, 4, piece, wide) if stage == 0 else (2, 2, piece, wide)
+    return [VMEM(dims, bf16)] * 3 + [DMA((12,))] * 2
+
+
 def feed_forward_kernel(
-    normed, cot_rows, cotangent, unit, scale, gains, weights,
-    resid, sums, spread, mixed_parts, chip,
+    normed, cot_rows, cotangent, unit, scale, norm_table, weights,
+    resid, sums, spread, mixed_parts, chip, settled,
     held, pair, hidden, normed_t, cot_t, parts, sib, mid, sent, far, near,
+    rmid, rfar, rnear, r_send, r_recv,
     load_sem, store_sem, core_send, core_recv, y_send, y_recv,
 ):
-    columns, width = held.shape[1] // 3, held.shape[0]
+    columns, width = held.shape[3] // 3, normed.shape[1]
     wide = 256
     rows = sib.shape[1]
-    c = lax.axis_index("c")
+    sub = cotangent.shape[0] // 2
+    z, x, c = lax.axis_index("z"), lax.axis_index("x"), lax.axis_index("c")
     y_sems, core_sems = (y_send, y_recv), (core_send, core_recv)
     whole, rest = columns // wide, columns % wide
+    all_pair, all_hidden = pl.ds(0, 2 * columns), pl.ds(2 * columns, columns)
+    groups = (pl.ds(0, EARLY), pl.ds(EARLY, 3 * columns - EARLY))
 
     def load(k, which, size):
         start = pl.multiple_of(which * columns + k * wide, 128)
         cut = pl.ds(start, size)
-        return pltpu.make_async_copy(weights.at[:, cut], held.at[:, cut], load_sem.at[k, which])
+        return pltpu.make_async_copy(
+            weights.at[:, :, :, cut], held.at[:, :, :, cut], load_sem.at[k, which]
+        )
 
     for k in range(whole + (rest > 0)):
         for which in range(3):
@@ -273,77 +341,117 @@
         return 0
 
     lax.fori_loop(0, width // wide, flip, 0)
-    greet([at_y(1), at_y(3), sibling()])
-
-    def ahead(k, size):
+    greet([at_z(1), at_z(3), at_x(1), at_x(3), at_y(1), at_y(3), sibling()])
+
+    tall = width // 4
+
+    def tile(k, cut):
+        return k, slice(None), slice(None), cut
+
+    def ahead(part, k, size):
+        these = pl.ds(4 * part * sub, 4 * sub)
+
         def cut(which):
             return pl.ds(pl.multiple_of(which * columns + k * wide, 128), size)
 
-        for which in range(3):
-            load(k, which, size).wait()
-        gate = dot(normed[...], held[:, cut(0)], 1, 0)
-        up = dot(normed[...], held[:, cut(1)], 1, 0)
-        grad_hidden = dot(cot_rows[...], held[:, cut(2)], 1, 0)
+        def weight(which):
+            return held[:, :, :, cut(which)].reshape(width, size)
+
+        if part == 0:
+            for which in range(3):
+                load(k, which, size).wait()
+        gate = dot(normed[these], weight(0), 1, 0)
+        up = dot(normed[these], weight(1), 1, 0)
+        grad_hidden = dot(cot_rows[these], weight(2), 1, 0)
         sigmoid = jax.nn.sigmoid(gate)
         activated = gate * sigmoid
-        hidden[:, cut(0)] = (activated * up).astype(bf16)
-        pair[:, cut(0)] = (
+        hidden[these, cut(0)] = (activated * up).astype(bf16)
+        pair[these, cut(0)] = (
             grad_hidden * up * sigmoid * (1.0 + gate * (1.0 - sigmoid))
         ).astype(bf16)
-        pair[:, cut(1)] = (grad_hidden * activated).astype(bf16)
+        pair[these, cut(1)] = (grad_hidden * activated).astype(bf16)
         return 0
 
-    lax.fori_loop(0, whole, lambda k, _: ahead(k, wide), 0)
-    if rest:
-        ahead(whole, rest)
-
-    def second_back(k, _):
-        rng = pl.ds(pl.multiple_of(k * wide, wide), wide)
-        parts[:, rng] = dot(pair[...], held[rng, pl.ds(0, 2 * columns)], 1, 1).astype(bf16)
+    part_subs = [parts.at[pl.ds(4 * k * sub, 4 * sub)] for k in range(2)]
+    started, middle, halves, passed = [], [], [], []
+
+    def ring_middle(part):
+        middle.append(
+            ring_sum_middle(
+                part_subs[part], started[part], mid.at[part], sent.at[part], far.at[part],
+                y_sems, 6 * part,
+            )
+        )
+
+    for part in range(2):
+        lax.fori_loop(0, whole, lambda k, _: ahead(part, k, wide), 0)
+        if rest:
+            ahead(part, whole, rest)
+        if part == 1:
+            ring_middle(0)
+
+        def second_back(k, _):
+            rng = pl.ds(pl.multiple_of(k * tall, tall), tall)
+            weight = held[tile(k, all_pair)].reshape(tall, 2 * columns)
+            these = pl.ds(4 * part * sub, 4 * sub)
+            parts[these, rng] = dot(pair[these], weight, 1, 1).astype(bf16)
+            return 0
+
+        lax.fori_loop(0, 4, second_back, 0)
+        started.append(
+            ring_sum_start(part_subs[part], mid.at[part], near.at[part], y_sems, 6 * part)
+        )
+
+    def to_core(block, which):
+        theirs = pl.ds(pl.multiple_of((1 - c) * rows, rows), rows)
+        return remote(
+            held.at[block // 4, block % 4, theirs, groups[which]],
+            sib.at[block, :, groups[which]],
+            core_sems,
+            block + 16 * which,
+            sibling(),
+        )
+
+    ours = pl.ds(pl.multiple_of(c * rows, rows), rows)
+
+    def core_sum(block, which):
+        to_core(block, which).wait_recv()
+        mine = (block // 4, block % 4, ours, groups[which])
+        held[mine] = (
+            held[mine].astype(f32) + sib[block, :, groups[which]].astype(f32)
+        ).astype(bf16)
+
+    def early_weights(k, _):
+        rng = pl.ds(pl.multiple_of(k * tall, tall), tall)
+        grad = dot(normed_t[rng], pair[:, pl.ds(0, EARLY)], 1, 0).astype(bf16)
+        held[tile(k, groups[0])] = grad.reshape(4, 2 * rows, EARLY)
+        for block in range(4):
+            to_core(4 * k + block, 0).start()
+
+        @pl.when(k > 0)
+        def _():
+            for block in range(4):
+                core_sum(4 * k - 4 + block, 0)
+
         return 0
 
-    lax.fori_loop(0, width // wide, second_back, 0)
-    started = ring_sum_start(parts, mid, near, y_sems, 0)
-
-    def mix(k, _):
-        rng = pl.ds(pl.multiple_of(k * wide, wide), wide)
-        mixed_parts[:, rng] = dot(
-            hidden[...], held[rng, pl.ds(2 * columns, columns)], 1, 1
-        ).astype(bf16)
-        return 0
-
-    lax.fori_loop(0, width // wide, mix, 0)
-    middle = ring_sum_middle(parts, started, mid, sent, far, y_sems, 0)
-
-    def to_core(block):
-        theirs = pl.ds(pl.multiple_of((2 * block + 1 - c) * rows, rows), rows)
-        return remote(held.at[theirs], sib.at[block], core_sems, block, sibling())
-
-    def weights_back(k, _):
-        rng = pl.ds(pl.multiple_of(k * wide, wide), wide)
-        held[rng, pl.ds(0, 2 * columns)] = dot(normed_t[rng], pair[...], 1, 0).astype(bf16)
-        held[rng, pl.ds(2 * columns, columns)] = dot(cot_t[rng], hidden[...], 1, 0).astype(bf16)
-        for block in range(wide // (2 * rows)):
-            to_core(k * (wide // (2 * rows)) + block).start()
-        return 0
-
-    lax.fori_loop(0, width // wide, weights_back, 0)
-    finish = ring_sum_finish(parts, started, middle, far, near)
-    half = cotangent.shape[0] // 2
-    halves = []
-    for top in range(2):
-        here = pl.ds(top * half, half)
-        total = finish(top)
+    def settle_rows(part):
+        finish = ring_sum_finish(
+            part_subs[part], started[part], middle[part], far.at[part], near.at[part]
+        )
+        here = pl.ds(part * sub, sub)
+        total = jnp.concatenate([finish(0), finish(1)], 0)
         unit_rows = unit[here]
-        incoming = total * gains[0:1]
+        incoming = total * norm_table[2:3]
         result = cotangent[here].astype(f32) + scale[here] * (
             incoming
             - jnp.mean(incoming, -1, keepdims=True)
             - unit_rows * jnp.mean(incoming * unit_rows, -1, keepdims=True)
         )
         resid[here] = result
-        spread[here] = result.astype(bf16)
-        halves.append(ring_gather_half(spread, top, y_sems, 6))
+        spread[pl.ds(4 * part * sub, sub)] = result.astype(bf16)
+        out = spread.at[pl.ds(4 * part * sub, 4 * sub)]
+        halves.append([ring_gather_half(out, top, y_sems, 12 + 6 * part) for top in range(2)])
         both = jnp.concatenate(
             [
                 jnp.sum(total * unit_rows, 0, keepdims=True),
@@ -351,42 +459,108 @@
             ],
             0,
         )
-        sums[...] = both if top == 0 else sums[...] + both
-
-    blocks = sib.shape[0]
+        sums[...] = both if part == 0 else sums[...] + both
+
+    def gather_pass(part):
+        out = spread.at[pl.ds(4 * part * sub, 4 * sub)]
+        passed.append(ring_gather_pass(out, halves[part], y_sems, 12 + 6 * part))
+
+    lax.fori_loop(0, 3, early_weights, 0)
+    ring_middle(1)
+    lax.fori_loop(3, 4, early_weights, 0)
+    for block in range(12, 16):
+        core_sum(block, 0)
+
+    def view(stage, half, d, part):
+        start = c * rows + half * (rows // 2) + part * (rows // 4)
+        rng = pl.ds(pl.multiple_of(start, rows // 4), rows // 4)
+        if half == 0:
+            return held.at[(z + d) % 4, :, rng, groups[0]]
+        return held.at[:, (x + d) % 4, rng, groups[0]]
+
+    reduce = Reduce(view, rows // 2, {0: (rmid, rfar, rnear, (r_send, r_recv))})
+    reduce.begin(0)
+    settle_rows(0)
+
+    def mix(k, _):
+        rng = pl.ds(pl.multiple_of(k * tall, tall), tall)
+        weight = held[tile(k, all_hidden)].reshape(tall, columns)
+        value = dot(hidden[...], weight, 1, 1).astype(bf16)
+        for part in range(2):
+            for block in range(4):
+                start = (part * 4 + block) * sub
+                mixed_parts[pl.ds((2 * block + part) * sub, sub), rng] = value[start : start + sub]
+        return 0
+
+    lax.fori_loop(0, 4, mix, 0)
+    settle_rows(1)
+    gather_pass(0)
+    reduce.combine(0)
+
+    def late_weights(k, _):
+        rng = pl.ds(pl.multiple_of(k * tall, tall), tall)
+        if EARLY < 2 * columns:
+            left = pl.ds(EARLY, 2 * columns - EARLY)
+            grad = dot(normed_t[rng], pair[:, left], 1, 0).astype(bf16)
+            held[tile(k, left)] = grad.reshape(4, 2 * rows, 2 * columns - EARLY)
+        grad = dot(cot_t[rng], hidden[...], 1, 0).astype(bf16)
+        held[tile(k, all_hidden)] = grad.reshape(4, 2 * rows, columns)
+        for block in range(4):
+            to_core(4 * k + block, 1).start()
+
+        @pl.when(k > 0)
+        def _():
+            for block in range(4):
+                add_core(4 * k - 4 + block)
+
+        return 0
 
     def store(block):
-        ours = pl.ds(pl.multiple_of((2 * block + c) * rows, rows), rows)
-        return pltpu.make_async_copy(held.at[ours], chip.at[block], store_sem.at[block])
-
-    def add_core(block, _):
-        to_core(block).wait_recv()
-        ours = pl.ds(pl.multiple_of((2 * block + c) * rows, rows), rows)
-        held[ours] = (held[ours].astype(f32) + sib[block].astype(f32)).astype(bf16)
+        return pltpu.make_async_copy(
+            held.at[block // 4, block % 4, ours, groups[1]], chip.at[block], store_sem.at[block]
+        )
+
+    def add_core(block):
+        core_sum(block, 1)
         store(block).start()
-        return 0
-
-    lax.fori_loop(0, blocks // 2, add_core, 0)
-    passed = ring_gather_pass(spread, halves, y_sems, 6)
-    lax.fori_loop(blocks // 2, blocks, add_core, 0)
+
+    lax.fori_loop(0, 2, late_weights, 0)
+    gather_pass(1)
+    lax.fori_loop(2, 4, late_weights, 0)
+    for block in range(12, 16):
+        add_core(block)
+    reduce.settle(0)
+    top_rows = pl.ds(pl.multiple_of(c * rows, rows // 2), rows // 2)
+    low_rows = pl.ds(pl.multiple_of(c * rows + rows // 2, rows // 2), rows // 2)
+    keep = [
+        pltpu.make_async_copy(held.at[z, :, top_rows, groups[0]], settled.at[0], store_sem.at[16]),
+        pltpu.make_async_copy(held.at[:, x, low_rows, groups[0]], settled.at[1], store_sem.at[17]),
+    ]
+    for copy in keep:
+        copy.start()
 
     def drain(block, _):
-        to_core(block).wait_send()
+        to_core(block, 0).wait_send()
+        to_core(block, 1).wait_send()
         store(block).wait()
         return 0
 
-    lax.fori_loop(0, blocks, drain, 0)
-    for copy in passed + [halves[1][0], halves[0][1]]:
-        copy.wait_recv()
-    for copy in started + middle + halves[0] + halves[1] + passed:
-        copy.wait_send()
-
-
-def feed_forward(normed, cot_rows, cotangent, unit, scale, gains, weights):
+    lax.fori_loop(0, 16, drain, 0)
+    for k in range(2):
+        for copy in passed[k] + [halves[k][1][0], halves[k][0][1]]:
+            copy.wait_recv()
+        for copy in started[k] + middle[k] + halves[k][0] + halves[k][1] + passed[k]:
+            copy.wait_send()
+    reduce.close()
+    for copy in keep:
+        copy.wait()
+
+
+def feed_forward(normed, cot_rows, cotangent, unit, scale, norm_table, weights):
     tokens, width = normed.shape
     here = cotangent.shape[0]
     columns = weights.shape[1] // 3
-    blocks, rows = 16, width // 32
+    rows = width // 32
     full = pl.BlockSpec(memory_space=VMEM)
     anywhere = pl.BlockSpec(memory_space=pl.ANY)
     tiles = -(-columns // 256)
@@ -397,25 +571,30 @@
             jax.ShapeDtypeStruct((2, width), f32),
             jax.ShapeDtypeStruct((tokens, width), bf16),
             jax.ShapeDtypeStruct((tokens, width), bf16),
-            jax.ShapeDtypeStruct((blocks, rows, 3 * columns), bf16),
+            jax.ShapeDtypeStruct((16, rows, 3 * columns - EARLY), bf16),
+            jax.ShapeDtypeStruct((2, 4, rows // 2, EARLY), bf16),
         ),
         in_specs=[full] * 6 + [anywhere],
-        out_specs=(full,) * 4 + (anywhere,),
+        out_specs=(full,) * 4 + (anywhere,) * 2,
         scratch_shapes=[
-            VMEM((width, 3 * columns), bf16),
+            VMEM((4, 4, 2 * rows, 3 * columns), bf16),
             VMEM((tokens, 2 * columns), bf16),
             VMEM((tokens, columns), bf16),
             VMEM((width, tokens), bf16),
             VMEM((width, tokens), bf16),
             VMEM((tokens, width), bf16),
-            VMEM((blocks, rows, 3 * columns), bf16),
+            VMEM((16, rows, 3 * columns), bf16),
         ]
-        + [VMEM((2, here // 2, width), bf16)] * 4
-        + [DMA((tiles, 3)), DMA((blocks,)), DMA((blocks,)), DMA((blocks,)), DMA((12,)), DMA((12,))],
+        + [VMEM((2, 2, here // 4, width), bf16)] * 4
+        + ring_buffers(0, rows // 4, EARLY)
+        + [DMA((tiles, 3)), DMA((18,)), DMA((32,)), DMA((32,)), DMA((24,)), DMA((24,))],
         compiler_params=pltpu.CompilerParams(
             collective_id=2, has_side_effects=True, vmem_limit_bytes=VMEM_LIMIT
         ),
-    )(normed, cot_rows, cotangent, unit, scale, gains, weights)
+    )(
+        normed, cot_rows, cotangent, unit, scale, norm_table,
+        weights.reshape(4, 4, 2 * rows, 3 * columns),
+    )
 
 
 def cube():
@@ -544,8 +723,8 @@
     for q in range(2):
         for t in range(3):
             one_q[q, :, t * hq : (t + 1) * hq] = qkv_weight[t, :, q * hq : (q + 1) * hq]
-        one_q[q, :, 3 * hq : 4 * hq] = out_weight[:, q * hq : (q + 1) * hq]
-        one_q[q, :, 4 * hq :] = extra[q]
+        one_q[q, :, 3 * hq : 3 * hq + EXTRA] = extra[q]
+        one_q[q, :, 3 * hq + EXTRA :] = out_weight[:, q * hq : (q + 1) * hq]
     token_rows[pl.ds(0, here)] = tokens[...]
     greet([at_z(1), at_z(3), at_x(1), at_x(3)] + cube())
 
@@ -576,7 +755,7 @@
 
     norm_moves = [
         remote(
-            one_q.at[0, :, pl.ds(4 * hq, EXTRA)],
+            one_q.at[0, :, pl.ds(3 * hq, EXTRA)],
             norm_in.at[c],
             pair_sems,
             4 + which,
@@ -593,7 +772,9 @@
         for t in range(2):
             two_q[q, :, t * fq : (t + 1) * fq] = gate_up_weight[t, :, q * fq : (q + 1) * fq]
         two_q[q, :, 2 * fq :] = down_weight[:, q * fq : (q + 1) * fq]
-    cot_rows[pl.ds(0, here)] = cotangent[...]
+    sub = here // 2
+    for k in range(2):
+        cot_rows[pl.ds(4 * k * sub, sub)] = cotangent[pl.ds(k * sub, sub)]
     land(0)
     land(1)
     for move in norm_moves:
@@ -603,8 +784,8 @@
         block = pl.ds(pl.multiple_of((own + core) * rows, rows), rows)
         came = norm_in[core].astype(f32)
         place = lax.broadcasted_iota(jnp.int32, came.shape, 0)
-        held = one[block, pl.ds(4 * hq, EXTRA)].astype(f32)
-        one[block, pl.ds(4 * hq, EXTRA)] = (
+        held = one[block, pl.ds(3 * hq, EXTRA)].astype(f32)
+        one[block, pl.ds(3 * hq, EXTRA)] = (
             held + jnp.where((place >= 12) & (place < 20), came, 0.0)
         ).astype(bf16)
     first = Spread(one, rows, (send_one, recv_one), (core_send_one, core_recv_one))
@@ -627,12 +808,16 @@
         first.second_far(df)
     for copy in token_passed + [token_halves[1][0], token_halves[0][1]]:
         copy.wait_recv()
-    cot_halves = [ring_gather_half(cot_rows, top, y_sems, 6) for top in range(2)]
+    cot_subs = [cot_rows.at[pl.ds(4 * k * sub, 4 * sub)] for k in range(2)]
+    cot_halves = [
+        [ring_gather_half(cot_subs[k], top, y_sems, 6 + 6 * k) for top in range(2)]
+        for k in range(2)
+    ]
     first.land()
     keep = pltpu.make_async_copy(one, one_out, local_sem.at[2])
     keep.start()
 
-    read_extras(one, 4 * hq, norm_table, bias)
+    read_extras(one, 3 * hq, norm_table, bias)
 
     def norm_rows(k, _):
         rng = pl.ds(pl.multiple_of(k * here, here), here)
@@ -674,7 +859,9 @@
 
     lax.fori_loop(0, 3 * hq // wide, project, 0)
     second.first_rest()
-    cot_passed = ring_gather_pass(cot_rows, cot_halves, y_sems, 6)
+    cot_passed = [
+        ring_gather_pass(cot_subs[k], cot_halves[k], y_sems, 6 + 6 * k) for k in range(2)
+    ]
     for sequence in range(2):
         mask = causal_mask(sequence, here)
         rng = pl.ds(sequence * 2 * here, 2 * here)
@@ -699,46 +886,72 @@
             second.second_pass(0)
     second.first_far()
 
-    def out_project(k, _):
-        rng = pl.ds(pl.multiple_of(k * wide, wide), wide)
-        parts[:, rng] = dot(head_mix[...], one[rng, pl.ds(3 * hq, hq)], 1, 1).astype(bf16)
-        return 0
-
-    lax.fori_loop(0, one.shape[0] // wide, out_project, 0)
-    for copy in cot_passed + [cot_halves[1][0], cot_halves[0][1]]:
-        copy.wait_recv()
-
-    started = ring_sum_start(parts, mid, near, y_sems, 12)
+    part_subs = [parts.at[pl.ds(4 * k * sub, 4 * sub)] for k in range(2)]
+    started, middle = [], []
+    for part in range(2):
+        mix = jnp.concatenate(
+            [head_mix[pl.ds(k * here + part * sub, sub)] for k in range(4)], 0
+        )
+
+        def out_project(k, _):
+            rng = pl.ds(pl.multiple_of(k * wide, wide), wide)
+            parts[pl.ds(4 * part * sub, 4 * sub), rng] = dot(
+                mix, one[rng, pl.ds(3 * hq + EXTRA, hq)], 1, 1
+            ).astype(bf16)
+            return 0
+
+        lax.fori_loop(0, one.shape[0] // wide, out_project, 0)
+        started.append(
+            ring_sum_start(part_subs[part], mid.at[part], near.at[part], y_sems, 18 + 6 * part)
+        )
     second.second_pass(3)
-    middle = ring_sum_middle(parts, started, mid, sent, far, y_sems, 12)
+    for part in range(2):
+        middle.append(
+            ring_sum_middle(
+                part_subs[part], started[part], mid.at[part], sent.at[part], far.at[part],
+                y_sems, 18 + 6 * part,
+            )
+        )
     second.second_pass(1)
-    finish = ring_sum_finish(parts, started, middle, far, near)
-    half = here // 2
     halves = []
-    for top in range(2):
-        rng = pl.ds(top * half, half)
-        total = tokens[rng].astype(f32) + finish(top)
+    for part in range(2):
+        finish = ring_sum_finish(
+            part_subs[part], started[part], middle[part], far.at[part], near.at[part]
+        )
+        total = jnp.concatenate([finish(0), finish(1)], 0)
+        rng = pl.ds(part * sub, sub)
+        total = total + tokens[rng].astype(f32)
         summed[rng] = total
         centered = total - jnp.mean(total, -1, keepdims=True)
         inverse = lax.rsqrt(jnp.mean(centered * centered, -1, keepdims=True) + EPSILON)
         unit_rows = centered * inverse
         unit[rng] = unit_rows
         scale[rng] = inverse
-        normed_two[rng] = (unit_rows * norm_table[2:3] + norm_table[3:4]).astype(bf16)
-        halves.append(ring_gather_half(normed_two, top, y_sems, 18))
+        normed_two[pl.ds(4 * part * sub, sub)] = (
+            unit_rows * norm_table[2:3] + norm_table[3:4]
+        ).astype(bf16)
+        out = normed_two.at[pl.ds(4 * part * sub, 4 * sub)]
+        halves.append([ring_gather_half(out, top, y_sems, 30 + 6 * part) for top in range(2)])
     second.second_pass(2)
-    passed = ring_gather_pass(normed_two, halves, y_sems, 18)
+    passed = [
+        ring_gather_pass(
+            normed_two.at[pl.ds(4 * k * sub, 4 * sub)], halves[k], y_sems, 30 + 6 * k
+        )
+        for k in range(2)
+    ]
     for df in (0, 3, 1, 2):
         second.second_far(df)
-    for copy in passed + [halves[1][0], halves[0][1]]:
-        copy.wait_recv()
+    for k in range(2):
+        for copy in passed[k] + [halves[k][1][0], halves[k][0][1]]:
+            copy.wait_recv()
+        for copy in cot_passed[k] + [cot_halves[k][1][0], cot_halves[k][0][1]]:
+            copy.wait_recv()
     second.land()
     keep.wait()
     for move in norm_moves:
         move.wait_send()
-    for copies in token_halves + cot_halves + halves + [
-        token_passed, cot_passed, started, middle, passed
-    ]:
+    gathers = token_halves + cot_halves[0] + cot_halves[1] + halves[0] + halves[1]
+    for copies in gathers + [token_passed] + cot_passed + started + middle + passed:
         for copy in copies:
             copy.wait_send()
     first.close()
@@ -783,9 +996,9 @@
             VMEM((4 * here, width), bf16),
             VMEM((4 * here, width), bf16),
         ]
-        + [VMEM((2, here // 2, width), bf16)] * 4
+        + [VMEM((2, 2, here // 4, width), bf16)] * 4
         + [
-            DMA((6,)), DMA((6,)), DMA((3,)), DMA((24,)), DMA((24,)),
+            DMA((6,)), DMA((6,)), DMA((3,)), DMA((42,)), DMA((42,)),
             DMA((64,)), DMA((64,)), DMA((32,)), DMA((32,)),
             DMA((64,)), DMA((64,)), DMA((32,)), DMA((32,)),
         ],
@@ -795,86 +1008,31 @@
     )(qkv_weight, out_weight, gate_up_weight, down_weight, extra, tokens, cotangent, table)
 
 
-class Reduce:
-    def __init__(self, src, mid, far, near, sems, mid2, far2, near2, sems2):
-        self.src, self.rows = src, src.shape[2] // 2
-        self.rings = ((mid, far, near, sems), (mid2, far2, near2, sems2))
-        self.done, self.got = [], {}
-
-    def view(self, stage, half, d, part):
-        piece = self.rows // 2
-        rng = pl.ds(half * self.rows + part * piece, piece)
-        if stage == 0:
-            return self.src.at[d, :, rng] if half == 0 else self.src.at[:, d, rng]
-        return self.src.at[0, d, rng] if half == 0 else self.src.at[d, 0, rng]
-
-    def send(self, name, stage, half, way, src, dst, index):
-        step = (1, -1)[way]
-        device = at_z(step) if (half == 0) == (stage == 0) else at_x(step)
-        copy = remote(src, dst, self.rings[stage][3], half * 6 + index * 2 + way, device)
-        copy.start()
-        self.done.append(copy)
-        self.got[name, stage, half, way] = copy
-
-    def far_rows(self, stage, half):
-        mid = self.rings[stage][0]
-        for way in range(2):
-            self.send("mid", stage, half, way, self.view(stage, half, 2, way), mid.at[half, way], 0)
-
-    def near_rows(self, stage, half):
-        near = self.rings[stage][2]
-        for way in range(2):
-            src = self.view(stage, half, (1, 3)[way], 1 - way)
-            self.send("near", stage, half, way, src, near.at[half, way], 1)
-
-    def combine(self, stage, half):
-        mid, far = self.rings[stage][:2]
-        for way in range(2):
-            self.got["mid", stage, half, way].wait_recv()
-            ref = self.view(stage, half, (1, 3)[way], way)
-            ref[...] = (ref[...].astype(f32) + mid[half, way].astype(f32)).astype(bf16)
-            self.send("far", stage, half, way, ref, far.at[half, way], 2)
-
-    def settle(self, stage, half, out=None):
-        far, near = self.rings[stage][1:3]
-        piece = self.rows // 2
-        for part in range(2):
-            self.got["far", stage, half, part].wait_recv()
-            self.got["near", stage, half, 1 - part].wait_recv()
-            ref = self.view(stage, half, 0, part)
-            total = (
-                ref[...].astype(f32)
-                + far[half, part].astype(f32)
-                + near[half, 1 - part].astype(f32)
-            ).astype(bf16)
-            if out is None:
-                ref[...] = total
-            else:
-                out[half, pl.ds(part * piece, piece)] = total
-
-    def close(self):
-        for copy in self.done:
-            copy.wait_send()
-
-
 def backward_kernel(
-    one, resid_rows, chip, qkv, head_mix, token_rows, stats, table, second_terms, norm_table,
-    mixed_parts, resid, first_sum,
-    result_one, result_two, norm_back, grad_tokens, mixed,
-    held, spare, grad_mix, grad_proj, sib, mid_a, far_a, near_a, mid_b, far_b, near_b,
-    blocks, mid_c, far_c, near_c, mid_d, far_d, near_d, packed_one, packed_two,
-    ymid, ysent, yfar, ynear,
-    load_sem, block_sem, core_send, core_recv, send_a, recv_a, send_b, recv_b,
-    send_c, recv_c, send_d, recv_d, pair_send, pair_recv, local_sem, y_send, y_recv,
+    one, resid_rows, chip, settled, qkv, head_mix, token_rows, stats, table, second_terms,
+    norm_table, mixed_parts, resid, first_sum,
+    out_qkv, out_out, out_gu, out_down, out_extra, grad_tokens, mixed,
+    result_one, result_two, norm_back, held, spare, grad_mix, grad_proj, sib, blocks, pair_sums,
+    *rest,
 ):
+    rings = [rest[5 * k : 5 * k + 5] for k in range(7)]
+    rings = [(mid, far, near, (send, recv)) for mid, far, near, send, recv in rings]
+    (
+        packed_one, packed_two, ymid, ysent, yfar, ynear,
+        load_sem, block_sem, core_send, core_recv, pair_send, pair_recv, local_sem, y_send, y_recv,
+    ) = rest[35:]
     z, x = lax.axis_index("z"), lax.axis_index("x")
     yl, c, yh = lax.axis_index("yl"), lax.axis_index("c"), lax.axis_index("yh")
     here = resid.shape[0]
     rows = result_one.shape[1]
-    hq = head_mix.shape[1]
+    hq, fq = head_mix.shape[1], result_two.shape[2] // 3
+    early, late = pair_sums.shape[3], blocks.shape[3]
+    sub = here // 2
     width = held.shape[0]
     core_sems, pair_sems, y_sems = (core_send, core_recv), (pair_send, pair_recv), (y_send, y_recv)
     wide = 256
+    out_start = 3 * hq + EXTRA
+    columns = (pl.ds(0, out_start), pl.ds(out_start, hq))
 
     def place_of(dz, dx):
         return ((z + dz) % 4) * 4 + (x + dx) % 4
@@ -883,58 +1041,116 @@
         pltpu.make_async_copy(
             one.at[:, pl.ds(start, size)], held.at[:, pl.ds(start, size)], load_sem.at[k]
         )
-        for k, (start, size) in enumerate(((3 * hq, hq), (0, 3 * hq)))
+        for k, (start, size) in enumerate(((out_start, hq), (0, 3 * hq)))
     ]
     loads.append(pltpu.make_async_copy(resid_rows, spare, load_sem.at[2]))
-    order = []
-    for d in (2, 1, 3, 0):
-        for e in (2, 1, 3, 0):
-            for pair in ((d, e), (e, d)):
-                if pair not in order:
-                    order.append(pair)
-    block_loads = {
-        (dz, dx): pltpu.make_async_copy(
+    loads.append(pltpu.make_async_copy(settled, pair_sums, load_sem.at[3]))
+    block_loads = [
+        pltpu.make_async_copy(
             chip.at[place_of(dz, dx)], blocks.at[dz, dx], block_sem.at[dz * 4 + dx]
         )
-        for dz, dx in order
-    }
+        for dz in range(4)
+        for dx in range(4)
+    ]
+    loads[3].start()
     loads[2].start()
     loads[0].start()
-    for pair in order:
-        block_loads[pair].start()
+    for load in block_loads:
+        load.start()
     loads[1].start()
     greet([at_z(1), at_z(3), at_x(1), at_x(3)] + cube())
     mixed_started = ring_sum_start(mixed_parts, ymid.at[0], ynear.at[0], y_sems, 0)
-    second = Reduce(blocks, mid_c, far_c, near_c, (send_c, recv_c), mid_d, far_d, near_d, (send_d, recv_d))
-    first = Reduce(sib, mid_a, far_a, near_a, (send_a, recv_a), mid_b, far_b, near_b, (send_b, recv_b))
-    for pair in order:
-        block_loads[pair].wait()
-    for half in range(2):
-        second.far_rows(0, half)
-    for half in range(2):
-        second.near_rows(0, half)
+
+    def cut(half, part):
+        return pl.ds(half * rows + part * (rows // 2), rows // 2)
+
+    def pair_view(stage, half, d, part):
+        along = x if half == 0 else z
+        return pair_sums.at[half, (along + d) % 4, pl.ds(part * (rows // 2), rows // 2)]
+
+    def view_of(ref, cols):
+        def view(stage, half, d, part):
+            if stage == 0:
+                there = (d, slice(None)) if half == 0 else (slice(None), d)
+            else:
+                there = (0, d) if half == 0 else (d, 0)
+            return ref.at[(*there, cut(half, part), cols)]
+
+        return view
+
+    gate_up = Reduce(pair_view, rows, {1: rings[0]})
+    down = Reduce(view_of(blocks, pl.ds(0, late)), rows, {0: rings[1], 1: rings[2]})
+    out_proj = Reduce(view_of(sib, columns[1]), rows, {0: rings[3], 1: rings[4]})
+    attention = Reduce(view_of(sib, columns[0]), rows, {0: rings[5], 1: rings[6]})
+    loads[3].wait()
+    gate_up.begin(1)
+    for load in block_loads:
+        load.wait()
+    down.begin(0)
+
+    def to_core(block, which):
+        theirs = pl.ds(pl.multiple_of((2 * block + 1 - c) * 2 * rows, 2 * rows), 2 * rows)
+        dz, dx = (block // 4 - z + 4) % 4, (block % 4 - x + 4) % 4
+        return remote(
+            held.at[theirs, columns[which]],
+            sib.at[dz, dx, :, columns[which]],
+            core_sems,
+            block + 16 * which,
+            sibling(),
+        )
+
+    def core_sum(block, which):
+        to_core(block, which).wait_recv()
+        ours = pl.ds(pl.multiple_of((2 * block + c) * 2 * rows, 2 * rows), 2 * rows)
+        there = ((block // 4 - z + 4) % 4, (block % 4 - x + 4) % 4, slice(None), columns[which])
+        sib[there] = (sib[there].astype(f32) + held[ours, columns[which]].astype(f32)).astype(
+            bf16
+        )
 
     loads[2].wait()
     loads[0].wait()
 
+    mix_order = jnp.concatenate(
+        [
+            head_mix[pl.ds(block * here + part * sub, sub)]
+            for part in range(2)
+            for block in range(4)
+        ],
+        0,
+    )
+
     def mix_back(k, _):
         cols = pl.ds(pl.multiple_of(k * wide, wide), wide)
-        grad_mix[:, cols] = dot(
-            spare[...], held[:, pl.ds(pl.multiple_of(3 * hq + k * wide, wide), wide)], 1, 0
+        value = dot(
+            spare[...], held[:, pl.ds(pl.multiple_of(out_start + k * wide, 128), wide)], 1, 0
         ).astype(bf16)
+        for part in range(2):
+            for block in range(4):
+                start = (part * 4 + block) * sub
+                grad_mix[pl.ds(block * here + part * sub, sub), cols] = value[start : start + sub]
         return 0
 
     lax.fori_loop(0, hq // wide, mix_back, 0)
 
     def out_back(k, _):
         rng = pl.ds(pl.multiple_of(k * 2 * wide, 2 * wide), 2 * wide)
-        held[rng, pl.ds(3 * hq, hq)] = dot(spare[:, rng], head_mix[...], 0, 0).astype(bf16)
+        held[rng, columns[1]] = dot(spare[:, rng], mix_order, 0, 0).astype(bf16)
+        for block in range(4):
+            to_core(4 * k + block, 1).start()
         return 0
 
     lax.fori_loop(0, width // (2 * wide), out_back, 0)
+    gate_up.combine(1)
     mixed_middle = ring_sum_middle(
         mixed_parts, mixed_started, ymid.at[0], ysent.at[0], yfar.at[0], y_sems, 0
     )
+
+    def out_sum(block, _):
+        core_sum(block, 1)
+        return 0
+
+    lax.fori_loop(0, 16, out_sum, 0)
+    out_proj.begin(0)
     for sequence in range(2):
         mask = causal_mask(sequence, here)
         rng = pl.ds(sequence * 2 * here, 2 * here)
@@ -954,14 +1170,14 @@
             mix = grad_mix[rng, pair(0)]
             results = ([], [], [])
             for head in range(2):
-                cut = slice(head * HEAD_DIM, (head + 1) * HEAD_DIM)
-                soft = soft_of(q[:, cut], key[:, cut], mask)
-                grad_soft = dot(mix[:, cut], value[:, cut], 1, 1)
+                lanes = slice(head * HEAD_DIM, (head + 1) * HEAD_DIM)
+                soft = soft_of(q[:, lanes], key[:, lanes], mask)
+                grad_soft = dot(mix[:, lanes], value[:, lanes], 1, 1)
                 row_dot = jnp.sum(grad_soft * soft, -1, keepdims=True)
                 grad_score = (soft * (grad_soft - row_dot)).astype(bf16)
-                results[0].append(dot(grad_score, key[:, cut], 1, 0) * SCALE)
-                results[1].append(dot(grad_score, q[:, cut], 0, 0) * SCALE)
-                results[2].append(dot(soft.astype(bf16), mix[:, cut], 0, 0))
+                results[0].append(dot(grad_score, key[:, lanes], 1, 0) * SCALE)
+                results[1].append(dot(grad_score, q[:, lanes], 0, 0) * SCALE)
+                results[2].append(dot(soft.astype(bf16), mix[:, lanes], 0, 0))
             for t in range(3):
                 both = jnp.concatenate(results[t], 1)
                 if t < 2:
@@ -970,7 +1186,9 @@
             return 0
 
         lax.fori_loop(0, hq // 128, heads, 0, unroll=2)
-        second.combine(0, sequence)
+        if sequence == 0:
+            down.combine(0)
+    gate_up.settle(1, packed_two.at[:, :, pl.ds(0, early)])
 
     bias_rows = [
         jnp.sum(grad_proj[:, pl.ds(k * 128, 128)].astype(f32), 0, keepdims=True)
@@ -978,11 +1196,6 @@
     ]
     mean, inverse = stats[0], stats[1]
     loads[1].wait()
-
-    def to_core(block):
-        theirs = pl.ds(pl.multiple_of((2 * block + 1 - c) * 2 * rows, 2 * rows), 2 * rows)
-        dz, dx = (block // 4 - z + 4) % 4, (block % 4 - x + 4) % 4
-        return remote(held.at[theirs], sib.at[dz, dx], core_sems, block, sibling())
 
     def weights_back(k, _):
         rng = pl.ds(pl.multiple_of(k * wide, wide), wide)
@@ -994,13 +1207,13 @@
         gain = jnp.sum(part * unit, 0, keepdims=True)
         shift = jnp.sum(part, 0, keepdims=True)
         for tile in range(wide // 128):
-            cut = slice(tile * 128, (tile + 1) * 128)
+            inner = slice(tile * 128, (tile + 1) * 128)
             lanes = pl.ds(pl.multiple_of(k * wide + tile * 128, 128), 128)
             extra = jnp.concatenate(
                 bias_rows
                 + [
-                    gain[:, cut],
-                    shift[:, cut],
+                    gain[:, inner],
+                    shift[:, inner],
                     second_terms[:, lanes],
                     jnp.zeros((rows - 16, 128), f32),
                 ],
@@ -1008,46 +1221,39 @@
             ).astype(bf16)
             for copy in range(128 // rows):
                 start = pl.multiple_of(k * wide + tile * 128 + copy * rows, rows)
-                held[pl.ds(start, rows), pl.ds(4 * hq, EXTRA)] = extra
-        for block in range(wide // (4 * rows)):
-            to_core(k * (wide // (4 * rows)) + block).start()
+                held[pl.ds(start, rows), pl.ds(3 * hq, EXTRA)] = extra
+        for block in range(2):
+            to_core(2 * k + block, 0).start()
+
+        @pl.when(k > 0)
+        def _():
+            for block in range(2):
+                core_sum(2 * k - 2 + block, 0)
+
         return 0
 
-    lax.fori_loop(0, width // wide, weights_back, 0)
+    lax.fori_loop(0, 5, weights_back, 0)
+    out_proj.combine(0)
+    down.settle(0)
+    down.begin(1)
+    lax.fori_loop(5, width // wide, weights_back, 0)
     first_started = ring_sum_start(spare, ymid.at[1], ynear.at[1], y_sems, 6)
-
-    summed = set()
-
-    def core_sum(dz, dx):
-        if (dz, dx) in summed:
-            return
-        summed.add((dz, dx))
-        block = place_of(dz, dx)
-        to_core(block).wait_recv()
-        ours = pl.ds(pl.multiple_of((2 * block + c) * 2 * rows, 2 * rows), 2 * rows)
-        sib[dz, dx] = (sib[dz, dx].astype(f32) + held[ours].astype(f32)).astype(bf16)
-
-    for half in range(2):
-        for d in (2, 1, 3, 0):
-            core_sum(*((2, d) if half == 0 else (d, 2)))
-        first.far_rows(0, half)
-    for half in range(2):
-        for step in (1, 3):
-            for d in (2, 1, 3, 0):
-                core_sum(*((step, d) if half == 0 else (d, step)))
-        first.near_rows(0, half)
-    core_sum(0, 0)
-    for half in range(2):
-        second.settle(0, half)
-        second.far_rows(1, half)
-        second.near_rows(1, half)
+    for block in range(14, 16):
+        core_sum(block, 0)
+    attention.begin(0)
+    down.combine(1)
+    out_proj.settle(0)
+    out_proj.begin(1)
+    down.settle(1, packed_two.at[:, :, pl.ds(early, late)])
+    home, away = {"yl": c, "c": yl}, {"yl": c, "c": 1 - yl}
+    stay_or_go(packed_two.at[yl], result_two.at[yl], pair_sems, 0, home, local_sem.at[0])
+    cross_two = remote(packed_two.at[1 - yl], result_two.at[yl], pair_sems, 1, away)
+    cross_two.start()
     first_middle = ring_sum_middle(
         spare, first_started, ymid.at[1], ysent.at[1], yfar.at[1], y_sems, 6
     )
-    for half in range(2):
-        first.combine(0, half)
-    for half in range(2):
-        second.combine(1, half)
+    attention.combine(0)
+    out_proj.combine(1)
     half_here = here // 2
     finish = ring_sum_finish(mixed_parts, mixed_started, mixed_middle, yfar.at[0], ynear.at[0])
     for top in range(2):
@@ -1063,25 +1269,16 @@
             - jnp.mean(incoming, -1, keepdims=True)
             - unit_rows * jnp.mean(incoming * unit_rows, -1, keepdims=True)
         )
-
-    home, away = {"yl": c, "c": yl}, {"yl": c, "c": 1 - yl}
-    for half in range(2):
-        second.settle(1, half, packed_two)
-    stay_or_go(packed_two.at[yl], result_two.at[yl], pair_sems, 0, home, local_sem.at[0])
-    cross_two = remote(packed_two.at[1 - yl], result_two.at[yl], pair_sems, 1, away)
-    cross_two.start()
-    for half in range(2):
-        first.settle(0, half)
-        first.far_rows(1, half)
-        first.near_rows(1, half)
-    for half in range(2):
-        first.combine(1, half)
-    for half in range(2):
-        first.settle(1, half, packed_one)
+    out_proj.settle(1, packed_one.at[:, :, columns[1]])
+    attention.settle(0)
+    attention.begin(1)
+    attention.combine(1)
+    attention.settle(1, packed_one.at[:, :, columns[0]])
+
     stay_or_go(packed_one.at[yl], result_one.at[yl], pair_sems, 2, home, local_sem.at[1])
     cross_one = remote(packed_one.at[1 - yl], result_one.at[yl], pair_sems, 3, away)
     cross_one.start()
-    extras = pl.ds(4 * hq, EXTRA)
+    extras = pl.ds(3 * hq, EXTRA)
     norm_moves = [
         remote(
             packed_one.at[core, :, extras],
@@ -1094,70 +1291,89 @@
     ]
     for move in norm_moves:
         move.start()
+    cross_two.wait_recv()
+    stay_or_go_wait(packed_two.at[yl], result_two.at[yl], pair_sems, 0, home, local_sem.at[0])
+    for q in range(2):
+        for t in range(2):
+            out_gu[t, :, q * fq : (q + 1) * fq] = result_two[q, :, t * fq : (t + 1) * fq]
+        out_down[:, q * fq : (q + 1) * fq] = result_two[q, :, 2 * fq :]
+    for copy in [cross_one] + norm_moves:
+        copy.wait_recv()
+    stay_or_go_wait(packed_one.at[yl], result_one.at[yl], pair_sems, 2, home, local_sem.at[1])
+    for q in range(2):
+        for t in range(3):
+            out_qkv[t, :, q * hq : (q + 1) * hq] = result_one[q, :, t * hq : (t + 1) * hq]
+        out_out[:, q * hq : (q + 1) * hq] = result_one[q, :, out_start:]
+        out_extra[q] = result_one[q, :, extras].astype(f32)
+    out_extra[2] = (out_extra[0] + out_extra[1]) + (
+        norm_back[0].astype(f32) + norm_back[1].astype(f32)
+    )
     for copy in [cross_two, cross_one] + norm_moves:
-        copy.wait_recv()
         copy.wait_send()
-    stay_or_go_wait(packed_two.at[yl], result_two.at[yl], pair_sems, 0, home, local_sem.at[0])
-    stay_or_go_wait(packed_one.at[yl], result_one.at[yl], pair_sems, 2, home, local_sem.at[1])
     for copy in mixed_started + mixed_middle + first_started + first_middle:
         copy.wait_send()
 
     def drain(block, _):
-        to_core(block).wait_send()
+        to_core(block, 0).wait_send()
+        to_core(block, 1).wait_send()
         return 0
 
     lax.fori_loop(0, 16, drain, 0)
-    first.close()
-    second.close()
+    for sums in (gate_up, down, out_proj, attention):
+        sums.close()
 
 
 def backward(
-    one, resid_rows, chip, qkv, head_mix, token_rows, stats, table, second_terms, norm_table,
-    mixed_parts, resid, first_sum,
+    one, resid_rows, chip, settled, qkv, head_mix, token_rows, stats, table, second_terms,
+    norm_table, mixed_parts, resid, first_sum,
 ):
     here, width = resid.shape
-    hq = head_mix.shape[1]
+    hq, early, late = head_mix.shape[1], settled.shape[3], chip.shape[2]
+    fq = (early + late) // 3
     rows = width // 64
     piece = rows // 2
-    one_wide, two_wide = one.shape[1], chip.shape[2]
+    one_wide = one.shape[1]
     full = pl.BlockSpec(memory_space=VMEM)
     anywhere = pl.BlockSpec(memory_space=pl.ANY)
-
-    def rings(wide):
-        return [VMEM((2, 2, 4, piece, wide), bf16)] * 3 + [VMEM((2, 2, piece, wide), bf16)] * 3
-
+    rings = ring_buffers(1, piece, early)
+    for wide in (late, hq, 3 * hq + EXTRA):
+        rings += ring_buffers(0, piece, wide) + ring_buffers(1, piece, wide)
     return pl.pallas_call(
         backward_kernel,
         out_shape=(
-            jax.ShapeDtypeStruct((2, rows, one_wide), bf16),
-            jax.ShapeDtypeStruct((2, rows, two_wide), bf16),
-            jax.ShapeDtypeStruct((2, rows, EXTRA), bf16),
+            jax.ShapeDtypeStruct((3, rows, 2 * hq), bf16),
+            jax.ShapeDtypeStruct((rows, 2 * hq), bf16),
+            jax.ShapeDtypeStruct((2, rows, 2 * fq), bf16),
+            jax.ShapeDtypeStruct((rows, 2 * fq), bf16),
+            jax.ShapeDtypeStruct((3, rows, EXTRA), f32),
             jax.ShapeDtypeStruct((here, width), f32),
             jax.ShapeDtypeStruct((here, width), bf16),
         ),
-        in_specs=[anywhere] * 3 + [full] * 10,
-        out_specs=(full,) * 5,
+        in_specs=[anywhere] * 4 + [full] * 10,
+        out_specs=(full,) * 7,
         scratch_shapes=[
+            VMEM((2, rows, one_wide), bf16),
+            VMEM((2, rows, 3 * fq), bf16),
+            VMEM((2, rows, EXTRA), bf16),
             VMEM((width, one_wide), bf16),
             VMEM((4 * here, width), bf16),
             VMEM((4 * here, hq), bf16),
             VMEM((4 * here, 3 * hq), bf16),
             VMEM((4, 4, 2 * rows, one_wide), bf16),
+            VMEM((4, 4, 2 * rows, late), bf16),
+            VMEM((2, 4, rows, early), bf16),
         ]
-        + rings(one_wide)
-        + [VMEM((4, 4, 2 * rows, two_wide), bf16)]
-        + rings(two_wide)
-        + [VMEM((2, rows, one_wide), bf16), VMEM((2, rows, two_wide), bf16)]
+        + rings
+        + [VMEM((2, rows, one_wide), bf16), VMEM((2, rows, 3 * fq), bf16)]
         + [VMEM((2, 2, here // 2, width), bf16)] * 4
-        + [DMA((3,)), DMA((16,)), DMA((16,)), DMA((16,))]
-        + [DMA((12,))] * 8
+        + [DMA((4,)), DMA((16,)), DMA((32,)), DMA((32,))]
         + [DMA((6,)), DMA((6,)), DMA((2,)), DMA((12,)), DMA((12,))],
         compiler_params=pltpu.CompilerParams(
             collective_id=3, has_side_effects=True, vmem_limit_bytes=VMEM_LIMIT
         ),
     )(
-        one, resid_rows, chip, qkv, head_mix, token_rows, stats, table, second_terms, norm_table,
-        mixed_parts, resid, first_sum,
+        one, resid_rows, chip, settled, qkv, head_mix, token_rows, stats, table, second_terms,
+        norm_table, mixed_parts, resid, first_sum,
     )
 
 
@@ -1167,9 +1383,7 @@
     yl, yh, c = lax.axis_index("yl"), lax.axis_index("yh"), lax.axis_index("c")
     mine = ((lax.axis_index("z") * 4 + lax.axis_index("x")) * 2 + yl) * 2 + c
     rows = qkv_weight.shape[1]
-    hq = qkv_weight.shape[2] // 2
-    fq = gate_up_weight.shape[2] // 2
-    heads = hq // HEAD_DIM
+    heads = qkv_weight.shape[2] // 2 // HEAD_DIM
     pairs = 3 * heads // 2
 
     norm_high = lax.optimization_barrier(norm_params.astype(bf16))
@@ -1197,42 +1411,22 @@
     ) = forward(
         qkv_weight, out_weight.T, gate_up_weight, down_weight.T, extra, tokens, cotangent, table
     )
-    grad_resid, second_terms, resid_rows, mixed_parts, chip = feed_forward(
-        normed_two, cot_rows, cotangent, unit_two, scale_two, norm_table[2:], second
-    )
-    first_back, second_back, norm_other, grad_input, mixed = backward(
-        one, resid_rows, chip, qkv, head_mix, token_rows, stats, table, second_terms, norm_table,
-        mixed_parts, grad_resid, first_sum,
-    )
-
-    gu_back, down_back = second_back[:, :, : 2 * fq], second_back[:, :, 2 * fq :]
-    out_down = down_back.transpose(0, 2, 1).reshape(2 * fq, rows).astype(f32)
-    out_gu = (
-        gu_back.reshape(2, rows, 2, fq).transpose(2, 1, 0, 3).reshape(2, rows, 2 * fq).astype(f32)
-    )
-    out_qkv = (
-        first_back[:, :, : 3 * hq]
-        .reshape(2, rows, 3, hq)
-        .transpose(2, 1, 0, 3)
-        .reshape(3, rows, 2 * hq)
-        .astype(f32)
-    )
-    out_out = (
-        first_back[:, :, 3 * hq : 4 * hq].transpose(0, 2, 1).reshape(2 * hq, rows).astype(f32)
-    )
-    extra_back = first_back[:, :, 4 * hq :].astype(f32)
-    out_bias = (
-        lax.dynamic_index_in_dim(
-            extra_back[:, :pairs].reshape(2, pairs, 2, HEAD_DIM), mine, 3, False
-        )
-        .reshape(2, 3, heads)
-        .transpose(1, 0, 2)
-        .reshape(3, 2 * heads, 1)
-    )
-    norm_sums = (extra_back + norm_other.astype(f32)).sum(0)[pairs : pairs + 4]
-    out_norm = lax.dynamic_index_in_dim(
-        norm_sums.reshape(4, EXTRA // share, share), mine % 4 * 2 + yh, 1, False
-    )
+    grad_resid, second_terms, resid_rows, mixed_parts, chip, settled = feed_forward(
+        normed_two, cot_rows, cotangent, unit_two, scale_two, norm_table, second
+    )
+    out_qkv, out_out, out_gu, out_down, out_extra, grad_input, mixed = backward(
+        one, resid_rows, chip, settled, qkv, head_mix, token_rows, stats, table, second_terms,
+        norm_table, mixed_parts, grad_resid, first_sum,
+    )
+
+    bias_sums = out_extra[:2, :pairs].reshape(2, 3, heads // 2, 2, HEAD_DIM)
+    out_bias = jnp.sum(jnp.where(jnp.arange(HEAD_DIM) == mine, bias_sums, 0.0), -1)
+    out_bias = out_bias.transpose(1, 0, 2, 3).reshape(3, 2 * heads, 1)
+    out_norm = lax.dynamic_slice(
+        out_extra[2, pairs : pairs + 4], (0, (mine % 4 * 2 + yh) * share), (4, share)
+    )
+    out_qkv, out_gu = out_qkv.astype(f32), out_gu.astype(f32)
+    out_out, out_down = out_out.T.astype(f32), out_down.T.astype(f32)
     return (mixed, grad_input, out_norm, out_qkv, out_bias, out_out, out_gu, out_down)
 
 

time: 290 us -> 280 us (0.966)
  Pallas kernels: 271 us -> 263 us
  local copies, waits for them, and re-layouts: 11.8 us -> 5.93 us
  other arithmetic: 5.43 us -> 8.92 us
    convert_element_type x8 -> x0, local copies, waits for them, and re-layouts: 5.5 us -> none  [the longest x3 2.4 us: shards(): gu_back.reshape(2, rows, 2, fq).transpose(2, 1, 0, 3)]
    convert_element_type x3 -> x4, other arithmetic: 1.72 us -> 6.78 us  [the longest x2 3.59 us: shards(): out_qkv, out_gu = (out_qkv.astype(f32), out_gu.astype(f32))]
    pallas_call x1, Pallas kernels: 64.6 us -> 60.8 us  [feed_forward(): pl.pallas_call(feed_forward_kernel, out_shape=(jax.ShapeDtypeStruct((here...]
where the time goes in v6:
time: 280 us; the launch traced here: 279 us
  Pallas kernels  263 us (94%)
  other arithmetic  8.92 us (3%)
  local copies, waits for them, and re-layouts  5.93 us (2%)
    pallas_call x1, Pallas kernels, forward(): pl.pallas_call(forward_kernel, out_shape=(shape(width, one_wide), shape(w...  115 us
    pallas_call x1, Pallas kernels, backward(): pl.pallas_call(backward_kernel, out_shape=(jax.ShapeDtypeStruct((3, rows,...  87.8 us
    pallas_call x1, Pallas kernels, feed_forward(): pl.pallas_call(feed_forward_kernel, out_shape=(jax.ShapeDtypeStruct((here...  60.8 us

profile of v6, /device:TPU:0, one launch (start us, length us, event | category | flops | bytes accessed | tf_op | source)
XLA Modules:
  0.0 279.0 jit_solution(1977978905764968904)
XLA Ops:
  0.7 0.1 broadcast_in_dim.48
  0.8 0.7 convert_element_type.31
  1.5 0.7 subtract_convert_fusion
  2.2 0.8 reshape.58
  2.9 0.1 broadcast_in_dim.50
  3.0 0.1 broadcast_in_dim.51
  3.1 0.1 broadcast_in_dim.52
  3.2 0.1 tile.10
  3.4 0.6 pad_maximum_fusion.extra
  4.0 114.8 %shard_map.152 = (bf16[2048,2176]{1,0:T(8,128)(2,1)}, bf16[2048,4224]{1,0:T(8,128)(2,1)}, bf16[512,2048]{1,0:T(8,128)(2,1)}, bf16[512,2048]{1,0:T(8,128)(2,1)}, ...) custom-call(bf16[3,32,1024]{2,1,0:T(8,128)(2,1)} %qkv_weight.1, ...), custom_call_target="tpu_custom_call" | custom-call | tf_op jit(solution)/shard_map/pallas_call | solution.py:972
  118.8 60.8 %shard_map.153 = (f32[128,2048]{1,0:T(8,128)}, f32[2,2048]{1,0:T(2,128)}, bf16[512,2048]{1,0:T(8,128)(2,1)}, bf16[512,2048]{1,0:T(8,128)(2,1)}, bf16[16,64,2816]...) custom-call(bf16[512,2048]{1,0:T(8,128)(2,1)} %get-tuple-element.34.normed, ...), custom_call_target="tpu_custom_call" | custom-call | tf_op jit(solution)/shard_map/pallas_call | solution.py:567
  179.6 87.8 %shard_map.154 = (bf16[3,32,1024]{2,1,0:T(8,128)(2,1)}, bf16[32,1024]{1,0:T(8,128)(2,1)}, bf16[2,32,2816]{2,1,0:T(8,128)(2,1)}, bf16[32,2816]{1,0:T(8,128)(2,1)}...) custom-call(bf16[2048,2176]{1,0:T(8,128)(2,1)} %get-tuple-element.33.one, ...), custom_call_target="tpu_custom_call" | custom-call | tf_op jit(solution)/shard_map/pallas_call | solution.py:1341
  267.4 0.0 copy-start.1
  267.4 0.0 copy-start
  267.4 0.8 slice.6
  268.2 0.7 slice.7
  268.9 0.7 dynamic-slice_bitcast_fusion
  269.6 0.1 reshape.60
  269.7 0.1 select_reduce_fusion
  269.8 0.7 reshape.62
  270.5 1.5 convert_bitcast_fusion.1
  272.0 1.7 convert_bitcast_fusion
  273.6 1.7 convert_element_type.34
  275.4 1.9 convert_element_type.37
  277.2 0.0 copy-done.1
  277.2 0.8 copy.33
  278.0 0.0 copy-done
  278.0 1.0 copy.34
  (13 shorter events, 0.1 us)
Async XLA Ops:
  267.4 9.9 %copy-start.1 = (bf16[128,2048]{1,0:T(8,128)(2,1)S(1)}, bf16[128,2048]{1,0:T(8,128)(2,1)}, u32[]{:S(2)}) copy-start(bf16[128,2048]{1,0:T(8,128)(2,1)} %get-tuple-element.90) | copy-start | bytes 1572868
  267.4 10.6 %copy-start = (f32[128,2048]{1,0:T(8,128)S(1)}, f32[128,2048]{1,0:T(8,128)}, u32[]{:S(2)}) copy-start(f32[128,2048]{1,0:T(8,128)} %get-tuple-element.91) | copy-start | bytes 3145732
